TPU v7x, 512 devices: a whole 4x4x16 slice. The times are simulated.
512 devices in a mesh: dp: 32 (over x, z_lo), tensor: 16 (over y, z_hi, core).
Axes of the slice: x: 4, y: 4, z: 16 (z_hi: 2, z_lo: 8; z = z_hi * 8 + z_lo), core: 2. Of those that a mesh axis runs over, the one named last changes fastest.
Arguments:
- tokens: bfloat16 [8192, 2048], P(('dp', 'tensor')), may hold values from -24 to 24
- masked: int32 [8192], P(('dp', 'tensor')), may hold values 0 or 1
- mask_vector: bfloat16 [2048], replicated, may hold values from -4 to 4
- gate_weight: bfloat16 [2048, 6144], P(None, 'tensor'), may hold values from -0.125 to 0.125
- up_weight: bfloat16 [2048, 6144], P(None, 'tensor'), may hold values from -0.125 to 0.125
- cotangent: bfloat16 [8192, 6144], P('dp', 'tensor'), may hold values from -6 to 6
Outputs:
- hidden: bfloat16 [8192, 6144], P('dp', 'tensor')
- token_grad: bfloat16 [8192, 2048], P(('dp', 'tensor'))
- gate_grad: float32 [2048, 6144], P('dp', 'tensor')
- up_grad: float32 [2048, 6144], P('dp', 'tensor')
All inputs are finite; a program needn't handle non-finite values. No bound on the sum of `masked` on one device may be relied on, other than what follows from the above.
Results may differ from a plain program's by a relative error of at most 0.029.
Values may be sent and summed in bfloat16 or wider, within the bound.
No kernel may reach another device: no remote copies, remote signals or barrier semaphores. Data moves between devices by JAX's collectives and lax.ppermute only.
A program may use at most 64 MiB of HBM per device.

v0:
```python
import jax
import jax.numpy as jnp
from jax import lax
from jax.sharding import PartitionSpec as P


def shards(tokens, masked, mask_vector, gate_weight, up_weight, cotangent):
    width = gate_weight.shape[1]
    flag = masked[:, None] == 1
    mixed_in = jnp.where(flag, mask_vector[None, :], tokens)
    mixed_f = mixed_in.astype(jnp.float32)
    inverse = lax.rsqrt(jnp.mean(mixed_f * mixed_f, axis=-1, keepdims=True) + 1e-06)
    normed_full = mixed_f * inverse
    normed = normed_full.astype(jnp.bfloat16)
    gathered = lax.all_gather(normed, "tensor", axis=0, tiled=True)
    first = jnp.dot(gathered, gate_weight, preferred_element_type=jnp.float32)
    second = jnp.dot(gathered, up_weight, preferred_element_type=jnp.float32)
    joined = jnp.concatenate([first, second], axis=1)
    gate = joined[:, :width]
    up = joined[:, width:]
    sig = jax.nn.sigmoid(gate)
    hidden = (gate * sig * up).astype(jnp.bfloat16)
    cot = cotangent.astype(jnp.float32)
    up_delta = (cot * gate * sig).astype(jnp.bfloat16)
    gate_delta = (cot * up * sig * (1.0 + gate * (1.0 - sig))).astype(jnp.bfloat16)
    contract_last = (((1,), (1,)), ((), ()))
    contract_first = (((0,), (0,)), ((), ()))
    first = lax.dot_general(
        gate_delta, gate_weight, contract_last, preferred_element_type=jnp.float32
    )
    second = lax.dot_general(up_delta, up_weight, contract_last, preferred_element_type=jnp.float32)
    normed_grad = lax.psum_scatter(
        (first + second).astype(jnp.bfloat16), "tensor", scatter_dimension=0, tiled=True
    ).astype(jnp.float32)
    inner = jnp.mean(normed_grad * normed_full, axis=-1, keepdims=True)
    token_grad = jnp.where(flag, 0.0, inverse * (normed_grad - normed_full * inner)).astype(
        jnp.bfloat16
    )
    first = lax.dot_general(
        gathered, gate_delta, contract_first, preferred_element_type=jnp.float32
    )
    second = lax.dot_general(gathered, up_delta, contract_first, preferred_element_type=jnp.float32)
    share = lax.psum_scatter(
        jnp.concatenate([first, second], axis=1).astype(jnp.bfloat16),
        "dp",
        scatter_dimension=0,
        tiled=True,
    ).astype(jnp.float32)
    gate_grad = share[:, :width]
    up_grad = share[:, width:]
    return (hidden, token_grad, gate_grad, up_grad)


def solution(mesh):
    return jax.shard_map(
        shards,
        mesh=mesh,
        in_specs=(
            P(("dp", "tensor"), None),
            P(("dp", "tensor")),
            P(),
            P(None, "tensor"),
            P(None, "tensor"),
            P("dp", "tensor"),
        ),
        out_specs=(
            P("dp", "tensor"),
            P(("dp", "tensor"), None),
            P("dp", "tensor"),
            P("dp", "tensor"),
        ),
        check_vma=False,
    )
```

profile of v0, /device:TPU:16, one launch (start us, length us, event | category | flops | bytes accessed | tf_op | source)
XLA Modules:
  0.0 451.5 jit_solution(4008724487894232962)
XLA Ops:
  7.2 0.0 copy-start
  7.2 0.0 all-gather.2.cloned.1.call-start
  7.2 0.8 broadcast_compare_fusion
  8.0 1.0 fusion.8
  9.0 1.6 fusion.7
  10.6 0.0 copy-start.4
  10.6 0.0 all-gather.2.cloned.1.call-update
  10.6 0.0 reduce-scatter.5.cloned.1.call-start
  10.7 81.8 %all-gather.2.cloned.1.call-done = bf16[256,2048]{1,0:T(8,128)(2,1)} async-done(((bf16[16,2048]{1,0:T(8,128)(2,1)}), bf16[256,2048]{1,0:T(8,128)(2,1)}) %all-gather.2.cloned.1.call-update) | async-done | bytes 1048592 | tf_op jit(solution)/shard_map/all_gather | solution.py:15
  92.4 0.0 copy-start.2
  92.4 2.5 fusion.16
  95.0 0.0 copy-done
  95.0 0.0 copy-done.4
  95.0 0.0 copy-done.2
  95.0 0.0 copy-start.1
  95.0 1.5 fusion.3
  96.5 0.0 copy-done.1
  96.5 0.8 fusion.17
  97.2 1.8 fusion
  99.0 0.0 reduce-scatter.5.cloned.1.call-update
  99.0 0.0 reduce-scatter.7.cloned.1.call-start
  99.1 0.6 convolution_convert_fusion.1
  99.7 0.6 convolution_convert_fusion
  100.3 2.1 pad_maximum_fusion
  102.4 4.7 %copy.14 = bf16[2048,768]{1,0:T(8,128)(2,1)} copy(bf16[2048,768]{0,1:T(8,128)(2,1)} %pad_maximum_fusion) | data formatting | bytes 6291456
  107.0 0.0 copy-start.3
  107.0 0.0 copy-start.5
  107.0 0.0 reduce-scatter.7.cloned.1.call-update
  107.1 90.4 %reduce-scatter.5.cloned.1.call-done = bf16[16,2048]{1,0:T(8,128)(2,1)} async-done(((bf16[256,2048]{1,0:T(8,128)(2,1)}), bf16[16,2048]{1,0:T(8,128)(2,1)}) %reduce-scatter.5.cloned.1.call-update) | async-done | bytes 65552 | tf_op jit(solution)/shard_map/reduce_scatter | solution.py:32
  197.5 0.0 copy-done.3
  197.5 0.0 copy-done.5
  197.5 1.0 fusion.9
  198.6 1.6 fusion.12
  200.1 242.3 %reduce-scatter.7.cloned.1.call-done = bf16[64,768]{1,0:T(8,128)(2,1)} async-done(((bf16[2048,768]{1,0:T(8,128)(2,1)}), bf16[64,768]{1,0:T(8,128)(2,1)}) %reduce-scatter.7.cloned.1.call-update) | async-done | bytes 98320
  442.4 1.1 copy.15
  443.5 0.8 copy.12
  444.3 0.8 copy.13
  (3 shorter events, 0.0 us)
Async XLA Ops:
  7.2 87.8 %copy-start = (bf16[2048,384]{1,0:T(8,128)(2,1)S(1)}, bf16[2048,384]{1,0:T(8,128)(2,1)}, u32[]{:S(2)}) copy-start(bf16[2048,384]{1,0:T(8,128)(2,1)} %param.10) | copy-start | bytes 4718596
  7.2 85.3 %all-gather.2.cloned.1.call-start = ((), (), s32[]{:S(2)}) async-start(), calls=%async_computation.2 | async-start | bytes 1114112 | tf_op jit(solution)/shard_map/all_gather | solution.py:15
  10.6 84.4 %copy-start.4 = (bf16[256,384]{1,0:T(8,128)(2,1)S(1)}, bf16[256,384]{1,0:T(8,128)(2,1)}, u32[]{:S(2)}) copy-start(bf16[256,384]{1,0:T(8,128)(2,1)} %param.11) | copy-start | bytes 589828
  10.6 186.9 %reduce-scatter.5.cloned.1.call-start = ((), (), s32[]{:S(2)}) async-start(), calls=%async_computation.3 | async-start | bytes 1114112 | tf_op jit(solution)/shard_map/reduce_scatter | solution.py:32
  92.4 2.5 copy-start.2
  95.0 1.5 copy-start.1
  99.0 343.4 %reduce-scatter.7.cloned.1.call-start = ((), (), s32[]{:S(2)}) async-start(), calls=%async_computation.4 | async-start | bytes 3244032
  107.0 90.5 %copy-start.3 = (bf16[16,2048]{1,0:T(8,128)(2,1)S(1)}, bf16[16,2048]{1,0:T(8,128)(2,1)}, u32[]{:S(2)}) copy-start(bf16[16,2048]{1,0:T(8,128)(2,1)} %param.6) | copy-start | bytes 196612
  107.0 90.5 %copy-start.5 = (bf16[2048]{0:T(1024)(128)(2,1)S(1)}, bf16[2048]{0:T(1024)(128)(2,1)}, u32[]{:S(2)}) copy-start(bf16[2048]{0:T(1024)(128)(2,1)} %param.8) | copy-start | bytes 12292
Sparse Core Ops, SparseCore 0:
  11.9 80.5 all-gather.1
  99.1 98.3 reduce-scatter.4
  200.6 241.7 reduce-scatter.6
where the time goes:
time: 452 us
  waiting for transfers between devices  415 us (92%)
  between operations  13.8 us (3%)
  other arithmetic  8.07 us (2%)
  matrix products  7.73 us (2%)
  local copies, waits for them, and re-layouts  7.28 us (2%)
    unnamed x4, waiting for transfers between devices  242 us
    reduce_scatter x1, waiting for transfers between devices, shards(): lax.psum_scatter((first + second).astype(jnp.bfloat16), 'tensor', scatter...  90.4 us
    all_gather x1, waiting for transfers between devices, shards(): gathered = lax.all_gather(normed, 'tensor', axis=0, tiled=True)  81.8 us
  transfers between devices with their start and end apart: 3, of which 3 were waited for; matrix products, arithmetic and copies ran while one was open for 2% of the time, Pallas kernels for 0%

commit v1 on v0

v1 whole, which is shorter than its diff:
```python
import jax
import jax.numpy as jnp
from jax import lax
from jax.sharding import PartitionSpec as P

NX, NZ = 4, 8
NY, NH, NC = 4, 2, 2
F32, BF16 = jnp.float32, jnp.bfloat16


def pick(array, index, axis):
    return lax.dynamic_index_in_dim(array, index, axis, keepdims=False)


def move(array, axis_name, count, target):
    return lax.ppermute(array, axis_name, [(i, target(i)) for i in range(count)])


def to_core(array):
    return move(array, "tensor", 16, lambda t: t ^ 1)


def to_high(array):
    return move(array, "tensor", 16, lambda t: t ^ 2)


def to_y(array, step):
    return move(array, "tensor", 16, lambda t: (t + 4 * step) % 16)


def to_x(array, step):
    return move(array, "dp", 32, lambda d: (d + 8 * step) % 32)


def to_z(array, bit):
    return move(array, "dp", 32, lambda d: d ^ bit)


def gather_rows(normed, y, high, core):
    rows, depth = normed.shape
    other = to_high(normed)
    pair = jnp.where(high == 0, jnp.stack([normed, other]), jnp.stack([other, normed]))
    got = [to_y(pair, step) for step in (1, 2, 3)]
    ring = jnp.stack([pair, got[2], got[1], got[0]])
    quad = lax.dynamic_slice_in_dim(jnp.concatenate([ring, ring]), (NY - y) % NY, NY, 0)
    far = to_core(quad)
    both = jnp.where(core == 0, jnp.stack([quad, far], axis=2), jnp.stack([far, quad], axis=2))
    return both.reshape(16 * rows, depth)


def scatter_rows(share, y, high, core):
    rows = share.shape[0] // 16
    share = share.reshape(NY, NH, NC, rows, -1)
    got = to_core(pick(share, 1 - core, 2))
    total = pick(share, core, 2).astype(F32) + got.astype(F32)
    sent = total.astype(BF16)
    got = [to_y(pick(sent, (y + step) % NY, 0), step) for step in (1, 2, 3)]
    total = pick(total, y, 0)
    for part in got:
        total = total + part.astype(F32)
    got = to_high(pick(total, 1 - high, 0).astype(BF16))
    return pick(total, high, 0) + got.astype(F32)


def scatter_weight(part, x, z):
    rows, width = part.shape
    rows = rows // (NX * NZ)
    part = part.reshape(NX, 2, NZ // 2, rows, width)
    far = pick(part, (x + 2) % NX, 0)
    from_left = to_x(far[0], 1)
    from_right = to_x(far[1], -1)
    right = pick(part, (x + 1) % NX, 0)
    left = pick(part, (x + 3) % NX, 0)
    low = (right[0].astype(F32) + from_left.astype(F32)).astype(BF16)
    high = (left[1].astype(F32) + from_right.astype(F32)).astype(BF16)
    from_left = to_x(jnp.stack([low, right[1]]), 1)
    from_right = to_x(jnp.stack([left[0], high]), -1)
    total = pick(part, x, 0).astype(F32) + from_left.astype(F32) + from_right.astype(F32)
    total = total.reshape(2, 2, 2, rows, width)
    bits = ((z // 4) % 2, (z // 2) % 2, z % 2)
    for axis, bit in ((2, 1), (1, 2), (0, 4)):
        got = to_z(pick(total, 1 - bits[axis], axis).astype(BF16), bit)
        total = pick(total, bits[axis], axis) + got.astype(F32)
    return total


def shards(tokens, masked, mask_vector, gate_weight, up_weight, cotangent):
    dp = lax.axis_index("dp")
    tensor = lax.axis_index("tensor")
    x, z = dp // NZ, dp % NZ
    y, high, core = tensor // 4, (tensor // 2) % 2, tensor % 2
    flag = masked[:, None] == 1
    mixed_in = jnp.where(flag, mask_vector[None, :], tokens)
    mixed_f = mixed_in.astype(F32)
    inverse = lax.rsqrt(jnp.mean(mixed_f * mixed_f, axis=-1, keepdims=True) + 1e-06)
    normed_full = mixed_f * inverse
    gathered = gather_rows(normed_full.astype(BF16), y, high, core)
    gate = jnp.dot(gathered, gate_weight, preferred_element_type=F32)
    up = jnp.dot(gathered, up_weight, preferred_element_type=F32)
    sig = jax.nn.sigmoid(gate)
    hidden = (gate * sig * up).astype(BF16)
    cot = cotangent.astype(F32)
    up_delta = (cot * gate * sig).astype(BF16)
    gate_delta = (cot * up * sig * (1.0 + gate * (1.0 - sig))).astype(BF16)
    contract_last = (((1,), (1,)), ((), ()))
    contract_first = (((0,), (0,)), ((), ()))
    first = lax.dot_general(gathered, gate_delta, contract_first, preferred_element_type=F32)
    second = lax.dot_general(gathered, up_delta, contract_first, preferred_element_type=F32)
    gate_grad = scatter_weight(first.astype(BF16), x, z)
    up_grad = scatter_weight(second.astype(BF16), x, z)
    first = lax.dot_general(gate_delta, gate_weight, contract_last, preferred_element_type=F32)
    second = lax.dot_general(up_delta, up_weight, contract_last, preferred_element_type=F32)
    normed_grad = scatter_rows((first + second).astype(BF16), y, high, core)
    inner = jnp.mean(normed_grad * normed_full, axis=-1, keepdims=True)
    token_grad = jnp.where(flag, 0.0, inverse * (normed_grad - normed_full * inner)).astype(BF16)
    return (hidden, token_grad, gate_grad, up_grad)


def solution(mesh):
    return jax.shard_map(
        shards,
        mesh=mesh,
        in_specs=(
            P(("dp", "tensor"), None),
            P(("dp", "tensor")),
            P(),
            P(None, "tensor"),
            P(None, "tensor"),
            P("dp", "tensor"),
        ),
        out_specs=(
            P("dp", "tensor"),
            P(("dp", "tensor"), None),
            P("dp", "tensor"),
            P("dp", "tensor"),
        ),
        check_vma=False,
    )
```

time: 452 us -> 141 us (0.31)
  the two profiles are of different devices: /device:TPU:16 before, /device:TPU:1 now
where the time goes in v1:
time: 141 us; the launch traced here: 139 us
  starting transfers between devices  97 us (69%)
  waiting for transfers between devices  25.7 us (18%)
  other arithmetic  8.14 us (6%)
  matrix products  5.28 us (4%)
  between operations  1.66 us (1%)
  local copies, waits for them, and re-layouts  1.59 us (1%)
    ppermute x24, starting transfers between devices, move(): lax.ppermute(array, axis_name, [(i, target(i)) for i in range(count)])  97 us
    ppermute x24, waiting for transfers between devices, move(): lax.ppermute(array, axis_name, [(i, target(i)) for i in range(count)])  25.7 us
  transfers between devices with their start and end apart: 24, of which 8 were waited for; matrix products, arithmetic and copies ran while one was open for 4% of the time, Pallas kernels for 0%

profile of v1, /device:TPU:1, one launch (start us, length us, event | category | flops | bytes accessed | tf_op | source)
XLA Modules:
  0.0 139.4 jit_solution(5554511611756511280)
XLA Ops:
  0.6 0.0 copy-start
  0.6 0.8 broadcast_compare_fusion
  1.4 1.0 fusion.28
  2.5 0.9 fusion.22
  3.4 16.3 %collective-permute-start = (bf16[16,2048]{1,0:T(8,128)(2,1)S(1)}, bf16[16,2048]{1,0:T(8,128)(2,1)S(1)}, u32[]{:S(2)}, u32[]{:S(2)}) collective-permute-start(bf16[16,2048]{1,0:T(8,128)(2,1)S(1)} %fusion.22), channel_id=1, source_target_pairs={{0,2},{1,3},{2,0},{3,1},{4,6},{5,7},{6,4},{7,5},{8,10},{9,11},{10,... | collective-permute-start | bytes 196616 | tf_op jit(solution)/shard_map/ppermute | solution.py:16
  19.7 0.9 fusion.53
  20.6 0.9 fusion.52
  21.6 4.6 %collective-permute-start.1 = (bf16[2,16,2048]{2,1,0:T(8,128)(2,1)S(1)}, bf16[2,16,2048]{2,1,0:T(8,128)(2,1)S(1)}, u32[]{:S(2)}, u32[]{:S(2)}) collective-permute-start(bf16[2,16,2048]{2,1,0:T(8,128)(2,1)S(1)} %maximum_select_fusion.2), channel_id=1, source_target_pairs={{0,12},{1,13},{2,14},{3,15},{4,0},{5,1},{6,2},{7,3},{8,4},{9,5},{1... | collective-permute-start | bytes 393224 | tf_op jit(solution)/shard_map/ppermute | solution.py:16
  26.3 2.3 %collective-permute-start.2 = (bf16[2,16,2048]{2,1,0:T(8,128)(2,1)S(1)}, bf16[2,16,2048]{2,1,0:T(8,128)(2,1)S(1)}, u32[]{:S(2)}, u32[]{:S(2)}) collective-permute-start(bf16[2,16,2048]{2,1,0:T(8,128)(2,1)S(1)} %maximum_select_fusion.2), channel_id=1, source_target_pairs={{0,8},{1,9},{2,10},{3,11},{4,12},{5,13},{6,14},{7,15},{8,0},{9,1},... | collective-permute-start | bytes 393224 | tf_op jit(solution)/shard_map/ppermute | solution.py:16
  28.6 2.6 %collective-permute-start.3 = (bf16[2,16,2048]{2,1,0:T(8,128)(2,1)S(1)}, bf16[2,16,2048]{2,1,0:T(8,128)(2,1)S(1)}, u32[]{:S(2)}, u32[]{:S(2)}) collective-permute-start(bf16[2,16,2048]{2,1,0:T(8,128)(2,1)S(1)} %maximum_select_fusion.2), channel_id=1, source_target_pairs={{0,4},{1,5},{2,6},{3,7},{4,8},{5,9},{6,10},{7,11},{8,12},{9,13},{1... | collective-permute-start | bytes 393224 | tf_op jit(solution)/shard_map/ppermute | solution.py:16
  31.2 2.3 %collective-permute-done.2 = bf16[2,16,2048]{2,1,0:T(8,128)(2,1)S(1)} collective-permute-done((bf16[2,16,2048]{2,1,0:T(8,128)(2,1)S(1)}, bf16[2,16,2048]{2,1,0:T(8,128)(2,1)S(1)}, u32[]{:S(2)}, u32[]{:S(2)}) %collective-permute-start.2) | collective-permute-done | bytes 131104 | tf_op jit(solution)/shard_map/ppermute | solution.py:16
  33.5 2.0 %collective-permute-done.3 = bf16[2,16,2048]{2,1,0:T(8,128)(2,1)S(1)} collective-permute-done((bf16[2,16,2048]{2,1,0:T(8,128)(2,1)S(1)}, bf16[2,16,2048]{2,1,0:T(8,128)(2,1)S(1)}, u32[]{:S(2)}, u32[]{:S(2)}) %collective-permute-start.3) | collective-permute-done | bytes 131104 | tf_op jit(solution)/shard_map/ppermute | solution.py:16
  35.6 0.9 constant_dynamic-slice_fusion
  36.4 6.8 %collective-permute-start.4 = (bf16[4,2,16,2048]{3,2,1,0:T(8,128)(2,1)}, bf16[4,2,16,2048]{3,2,1,0:T(8,128)(2,1)S(1)}, u32[]{:S(2)}, u32[]{:S(2)}) collective-permute-start(bf16[4,2,16,2048]{3,2,1,0:T(8,128)(2,1)} %constant_dynamic-slice_fusion), channel_id=1, source_target_pairs={{0,1},{1,0},{2,3},{3,2},{4,5},{5,4},{6,7},{7,6},{8,9},{9,8},{10,11... | collective-permute-start | bytes 1572872 | tf_op jit(solution)/shard_map/ppermute | solution.py:16
  43.6 0.0 copy-start.1
  43.6 1.4 collective-permute-done.4
  45.0 0.1 maximum_select_fusion
  45.1 0.0 copy-start.3
  45.1 0.7 fusion.39
  45.9 0.2 copy-done.3
  46.0 0.8 convolution_convert_fusion
  46.9 1.5 %fusion.5 = (bf16[256,384]{1,0:T(8,128)(2,1)S(1)}, bf16[256,384]{1,0:T(8,128)(2,1)}) fusion(bf16[256,384]{1,0:T(8,128)(2,1)S(1)} %copy-done.3, f32[256,384]{1,0:T(8,128)S(1)} %fusion.39, bf16[256,2048]{1,0:T(8,128)(2,1)S(1)} %bitcast.136, bf16[2048,384]{1,0:T(8,128)(2,1)S(1)} %copy-done), kind=kOutput, calls=%fused_computation.15 | convolution fusion | flops 404029440 | bytes 3604480 | tf_op jit(solution)/shard_map/dot_general | solution.py:99
  48.4 0.7 fusion.40
  49.1 0.7 convolution_convert_fusion.1
  49.9 0.8 fusion
  50.6 0.1 dynamic-slice_bitcast_fusion.5
  50.7 3.1 %collective-permute-start.17 = (bf16[4,64,384]{2,1,0:T(8,128)(2,1)S(1)}, bf16[4,64,384]{2,1,0:T(8,128)(2,1)S(1)}, u32[]{:S(2)}, u32[]{:S(2)}) collective-permute-start(bf16[4,64,384]{2,1,0:T(8,128)(2,1)S(1)} %get-tuple-element.8), channel_id=1, source_target_pairs={{0,128},{16,144},{32,160},{48,176},{64,192},{80,208},{96,224},{112... | collective-permute-start | bytes 589832 | tf_op jit(solution)/shard_map/ppermute | solution.py:16
  53.9 3.4 %collective-permute-start.19 = (bf16[4,64,384]{2,1,0:T(8,128)(2,1)S(1)}, bf16[4,64,384]{2,1,0:T(8,128)(2,1)S(1)}, u32[]{:S(2)}, u32[]{:S(2)}) collective-permute-start(bf16[4,64,384]{2,1,0:T(8,128)(2,1)S(1)} %get-tuple-element.10), channel_id=1, source_target_pairs={{0,384},{16,400},{32,416},{48,432},{64,448},{80,464},{96,480},{112... | collective-permute-start | bytes 589832 | tf_op jit(solution)/shard_map/ppermute | solution.py:16
  57.3 2.8 %collective-permute-start.5 = (bf16[4,2,16,2048]{3,2,1,0:T(8,128)(2,1)S(1)}, bf16[4,2,16,2048]{3,2,1,0:T(8,128)(2,1)S(1)}, u32[]{:S(2)}, u32[]{:S(2)}) collective-permute-start(bf16[4,2,16,2048]{3,2,1,0:T(8,128)(2,1)S(1)} %dynamic-slice_bitcast_fusion), channel_id=1, source_target_pairs={{0,1},{1,0},{2,3},{3,2},{4,5},{5,4},{6,7},{7,6},{8,9},{9,8},{10,11... | collective-permute-start | bytes 1572872 | tf_op jit(solution)/shard_map/ppermute | solution.py:16
  60.1 0.1 dynamic-slice_bitcast_fusion.11
  60.2 1.9 %collective-permute-start.10 = (bf16[4,64,384]{2,1,0:T(8,128)(2,1)S(1)}, bf16[4,64,384]{2,1,0:T(8,128)(2,1)S(1)}, u32[]{:S(2)}, u32[]{:S(2)}) collective-permute-start(bf16[4,64,384]{2,1,0:T(8,128)(2,1)S(1)} %get-tuple-element.14), channel_id=1, source_target_pairs={{0,128},{16,144},{32,160},{48,176},{64,192},{80,208},{96,224},{112... | collective-permute-start | bytes 589832 | tf_op jit(solution)/shard_map/ppermute | solution.py:16
  62.2 4.6 %collective-permute-start.12 = (bf16[4,64,384]{2,1,0:T(8,128)(2,1)S(1)}, bf16[4,64,384]{2,1,0:T(8,128)(2,1)S(1)}, u32[]{:S(2)}, u32[]{:S(2)}) collective-permute-start(bf16[4,64,384]{2,1,0:T(8,128)(2,1)S(1)} %get-tuple-element.16), channel_id=1, source_target_pairs={{0,384},{16,400},{32,416},{48,432},{64,448},{80,464},{96,480},{112... | collective-permute-start | bytes 589832 | tf_op jit(solution)/shard_map/ppermute | solution.py:16
  66.8 0.0 collective-permute-done.17
  66.8 0.0 collective-permute-done.19
  66.8 0.1 fusion.18
  66.9 2.0 %collective-permute-start.20 = (bf16[2,4,64,384]{3,2,1,0:T(8,128)(2,1)S(1)}, bf16[2,4,64,384]{3,2,1,0:T(8,128)(2,1)S(1)}, u32[]{:S(2)}, u32[]{:S(2)}) collective-permute-start(bf16[2,4,64,384]{3,2,1,0:T(8,128)(2,1)S(1)} %pad_maximum_fusion.3), channel_id=1, source_target_pairs={{0,384},{16,400},{32,416},{48,432},{64,448},{80,464},{96,480},{112... | collective-permute-start | bytes 1179656 | tf_op jit(solution)/shard_map/ppermute | solution.py:16
  69.0 3.3 %collective-permute-start.18 = (bf16[2,4,64,384]{3,2,1,0:T(8,128)(2,1)S(1)}, bf16[2,4,64,384]{3,2,1,0:T(8,128)(2,1)S(1)}, u32[]{:S(2)}, u32[]{:S(2)}) collective-permute-start(bf16[2,4,64,384]{3,2,1,0:T(8,128)(2,1)S(1)} %pad_maximum_fusion.2), channel_id=1, source_target_pairs={{0,128},{16,144},{32,160},{48,176},{64,192},{80,208},{96,224},{112... | collective-permute-start | bytes 1179656 | tf_op jit(solution)/shard_map/ppermute | solution.py:16
  72.3 0.1 fusion.16
  72.5 3.7 %collective-permute-start.13 = (bf16[2,4,64,384]{3,2,1,0:T(8,128)(2,1)S(1)}, bf16[2,4,64,384]{3,2,1,0:T(8,128)(2,1)S(1)}, u32[]{:S(2)}, u32[]{:S(2)}) collective-permute-start(bf16[2,4,64,384]{3,2,1,0:T(8,128)(2,1)S(1)} %pad_maximum_fusion.1), channel_id=1, source_target_pairs={{0,384},{16,400},{32,416},{48,432},{64,448},{80,464},{96,480},{112... | collective-permute-start | bytes 1179656 | tf_op jit(solution)/shard_map/ppermute | solution.py:16
  76.3 1.9 %collective-permute-start.11 = (bf16[2,4,64,384]{3,2,1,0:T(8,128)(2,1)S(1)}, bf16[2,4,64,384]{3,2,1,0:T(8,128)(2,1)S(1)}, u32[]{:S(2)}, u32[]{:S(2)}) collective-permute-start(bf16[2,4,64,384]{3,2,1,0:T(8,128)(2,1)S(1)} %pad_maximum_fusion), channel_id=1, source_target_pairs={{0,128},{16,144},{32,160},{48,176},{64,192},{80,208},{96,224},{112... | collective-permute-start | bytes 1179656 | tf_op jit(solution)/shard_map/ppermute | solution.py:16
  78.2 0.2 fusion.38
  78.4 1.9 %collective-permute-start.8 = (bf16[2,16,2048]{2,1,0:T(8,128)(2,1)S(1)}, bf16[2,16,2048]{2,1,0:T(8,128)(2,1)S(1)}, u32[]{:S(2)}, u32[]{:S(2)}) collective-permute-start(bf16[2,16,2048]{2,1,0:T(8,128)(2,1)S(1)} %get-tuple-element.21), channel_id=1, source_target_pairs={{0,12},{1,13},{2,14},{3,15},{4,0},{5,1},{6,2},{7,3},{8,4},{9,5},{1... | collective-permute-start | bytes 393224 | tf_op jit(solution)/shard_map/ppermute | solution.py:16
  80.4 3.3 %collective-permute-start.7 = (bf16[2,16,2048]{2,1,0:T(8,128)(2,1)S(1)}, bf16[2,16,2048]{2,1,0:T(8,128)(2,1)S(1)}, u32[]{:S(2)}, u32[]{:S(2)}) collective-permute-start(bf16[2,16,2048]{2,1,0:T(8,128)(2,1)S(1)} %get-tuple-element.22), channel_id=1, source_target_pairs={{0,8},{1,9},{2,10},{3,11},{4,12},{5,13},{6,14},{7,15},{8,0},{9,1},... | collective-permute-start | bytes 393224 | tf_op jit(solution)/shard_map/ppermute | solution.py:16
  83.7 2.8 %collective-permute-start.6 = (bf16[2,16,2048]{2,1,0:T(8,128)(2,1)S(1)}, bf16[2,16,2048]{2,1,0:T(8,128)(2,1)S(1)}, u32[]{:S(2)}, u32[]{:S(2)}) collective-permute-start(bf16[2,16,2048]{2,1,0:T(8,128)(2,1)S(1)} %get-tuple-element.20), channel_id=1, source_target_pairs={{0,4},{1,5},{2,6},{3,7},{4,8},{5,9},{6,10},{7,11},{8,12},{9,13},{1... | collective-permute-start | bytes 393224 | tf_op jit(solution)/shard_map/ppermute | solution.py:16
  86.5 1.1 collective-permute-done.13
  87.6 2.5 %collective-permute-done.11 = bf16[2,4,64,384]{3,2,1,0:T(8,128)(2,1)S(1)} collective-permute-done((bf16[2,4,64,384]{3,2,1,0:T(8,128)(2,1)S(1)}, bf16[2,4,64,384]{3,2,1,0:T(8,128)(2,1)S(1)}, u32[]{:S(2)}, u32[]{:S(2)}) %collective-permute-start.11) | collective-permute-done | bytes 393248 | tf_op jit(solution)/shard_map/ppermute | solution.py:16
  90.1 0.3 fusion.1
  90.4 0.0 copy-start.2
  90.5 0.0 copy-start.4
  90.5 2.2 %collective-permute-start.14 = (bf16[2,2,64,384]{3,2,1,0:T(8,128)(2,1)S(1)}, bf16[2,2,64,384]{3,2,1,0:T(8,128)(2,1)S(1)}, u32[]{:S(2)}, u32[]{:S(2)}) collective-permute-start(bf16[2,2,64,384]{3,2,1,0:T(8,128)(2,1)S(1)} %fusion.14), channel_id=1, source_target_pairs={{0,16},{16,0},{32,48},{48,32},{64,80},{80,64},{96,112},{112,96},{1... | collective-permute-start | bytes 589832 | tf_op jit(solution)/shard_map/ppermute | solution.py:16
  92.7 0.1 fusion.13
  92.8 12.6 %collective-permute-start.9 = (bf16[16,2048]{1,0:T(8,128)(2,1)S(1)}, bf16[16,2048]{1,0:T(8,128)(2,1)S(1)}, u32[]{:S(2)}, u32[]{:S(2)}) collective-permute-start(bf16[16,2048]{1,0:T(8,128)(2,1)S(1)} %fusion.31), channel_id=1, source_target_pairs={{0,2},{1,3},{2,0},{3,1},{4,6},{5,7},{6,4},{7,5},{8,10},{9,11},{10,... | collective-permute-start | bytes 196616 | tf_op jit(solution)/shard_map/ppermute | solution.py:16
  105.4 3.4 %collective-permute-start.21 = (bf16[2,2,64,384]{3,2,1,0:T(8,128)(2,1)S(1)}, bf16[2,2,64,384]{3,2,1,0:T(8,128)(2,1)S(1)}, u32[]{:S(2)}, u32[]{:S(2)}) collective-permute-start(bf16[2,2,64,384]{3,2,1,0:T(8,128)(2,1)S(1)} %fusion.15), channel_id=1, source_target_pairs={{0,16},{16,0},{32,48},{48,32},{64,80},{80,64},{96,112},{112,96},{1... | collective-permute-start | bytes 589832 | tf_op jit(solution)/shard_map/ppermute | solution.py:16
  108.8 0.2 fusion.23
  109.1 0.7 fusion.27
  109.9 4.1 %collective-permute-start.15 = (bf16[2,64,384]{2,1,0:T(8,128)(2,1)S(1)}, bf16[2,64,384]{2,1,0:T(8,128)(2,1)S(1)}, u32[]{:S(2)}, u32[]{:S(2)}) collective-permute-start(bf16[2,64,384]{2,1,0:T(8,128)(2,1)S(1)} %fusion.29), channel_id=1, source_target_pairs={{0,32},{16,48},{32,0},{48,16},{64,96},{80,112},{96,64},{112,80},{1... | collective-permute-start | bytes 294920 | tf_op jit(solution)/shard_map/ppermute | solution.py:16
  114.0 4.4 %collective-permute-done.21 = bf16[2,2,64,384]{3,2,1,0:T(8,128)(2,1)S(1)} collective-permute-done((bf16[2,2,64,384]{3,2,1,0:T(8,128)(2,1)S(1)}, bf16[2,2,64,384]{3,2,1,0:T(8,128)(2,1)S(1)}, u32[]{:S(2)}, u32[]{:S(2)}) %collective-permute-start.21) | collective-permute-done | bytes 196640 | tf_op jit(solution)/shard_map/ppermute | solution.py:16
  118.4 1.9 %collective-permute-start.22 = (bf16[2,64,384]{2,1,0:T(8,128)(2,1)S(1)}, bf16[2,64,384]{2,1,0:T(8,128)(2,1)S(1)}, u32[]{:S(2)}, u32[]{:S(2)}) collective-permute-start(bf16[2,64,384]{2,1,0:T(8,128)(2,1)S(1)} %fusion.30), channel_id=1, source_target_pairs={{0,32},{16,48},{32,0},{48,16},{64,96},{80,112},{96,64},{112,80},{1... | collective-permute-start | bytes 294920 | tf_op jit(solution)/shard_map/ppermute | solution.py:16
  120.4 3.6 %collective-permute-start.16 = (bf16[64,384]{1,0:T(8,128)(2,1)S(1)}, bf16[64,384]{1,0:T(8,128)(2,1)S(1)}, u32[]{:S(2)}, u32[]{:S(2)}) collective-permute-start(bf16[64,384]{1,0:T(8,128)(2,1)S(1)} %fusion.32), channel_id=1, source_target_pairs={{0,64},{16,80},{32,96},{48,112},{64,0},{80,16},{96,32},{112,48},{1... | collective-permute-start | bytes 147464 | tf_op jit(solution)/shard_map/ppermute | solution.py:16
  124.1 4.2 %collective-permute-done.22 = bf16[2,64,384]{2,1,0:T(8,128)(2,1)S(1)} collective-permute-done((bf16[2,64,384]{2,1,0:T(8,128)(2,1)S(1)}, bf16[2,64,384]{2,1,0:T(8,128)(2,1)S(1)}, u32[]{:S(2)}, u32[]{:S(2)}) %collective-permute-start.22) | collective-permute-done | bytes 98336 | tf_op jit(solution)/shard_map/ppermute | solution.py:16
  128.3 1.9 %collective-permute-start.23 = (bf16[64,384]{1,0:T(8,128)(2,1)S(1)}, bf16[64,384]{1,0:T(8,128)(2,1)S(1)}, u32[]{:S(2)}, u32[]{:S(2)}) collective-permute-start(bf16[64,384]{1,0:T(8,128)(2,1)S(1)} %fusion.33), channel_id=1, source_target_pairs={{0,64},{16,80},{32,96},{48,112},{64,0},{80,16},{96,32},{112,48},{1... | collective-permute-start | bytes 147464 | tf_op jit(solution)/shard_map/ppermute | solution.py:16
  130.3 0.7 bitcast_add_fusion.7
  130.9 7.8 %collective-permute-done.23 = bf16[64,384]{1,0:T(8,128)(2,1)S(1)} collective-permute-done((bf16[64,384]{1,0:T(8,128)(2,1)S(1)}, bf16[64,384]{1,0:T(8,128)(2,1)S(1)}, u32[]{:S(2)}, u32[]{:S(2)}) %collective-permute-start.23) | collective-permute-done | bytes 49184 | tf_op jit(solution)/shard_map/ppermute | solution.py:16
  138.8 0.7 bitcast_add_fusion.6
  (47 shorter events, 0.8 us)
Async XLA Ops:
  0.6 46.2 %copy-start = (bf16[2048,384]{1,0:T(8,128)(2,1)S(1)}, bf16[2048,384]{1,0:T(8,128)(2,1)}, u32[]{:S(2)}) copy-start(bf16[2048,384]{1,0:T(8,128)(2,1)} %param.10) | copy-start | bytes 4718596
  3.4 18.2 %collective-permute-start = (bf16[16,2048]{1,0:T(8,128)(2,1)S(1)}, bf16[16,2048]{1,0:T(8,128)(2,1)S(1)}, u32[]{:S(2)}, u32[]{:S(2)}) collective-permute-start(bf16[16,2048]{1,0:T(8,128)(2,1)S(1)} %fusion.22), channel_id=1, source_target_pairs={{0,2},{1,3},{2,0},{3,1},{4,6},{5,7},{6,4},{7,5},{8,10},{9,11},{10,... | collective-permute-start | bytes 196616 | tf_op jit(solution)/shard_map/ppermute | solution.py:16
  21.6 9.6 %collective-permute-start.1 = (bf16[2,16,2048]{2,1,0:T(8,128)(2,1)S(1)}, bf16[2,16,2048]{2,1,0:T(8,128)(2,1)S(1)}, u32[]{:S(2)}, u32[]{:S(2)}) collective-permute-start(bf16[2,16,2048]{2,1,0:T(8,128)(2,1)S(1)} %maximum_select_fusion.2), channel_id=1, source_target_pairs={{0,12},{1,13},{2,14},{3,15},{4,0},{5,1},{6,2},{7,3},{8,4},{9,5},{1... | collective-permute-start | bytes 393224 | tf_op jit(solution)/shard_map/ppermute | solution.py:16
  26.3 7.2 %collective-permute-start.2 = (bf16[2,16,2048]{2,1,0:T(8,128)(2,1)S(1)}, bf16[2,16,2048]{2,1,0:T(8,128)(2,1)S(1)}, u32[]{:S(2)}, u32[]{:S(2)}) collective-permute-start(bf16[2,16,2048]{2,1,0:T(8,128)(2,1)S(1)} %maximum_select_fusion.2), channel_id=1, source_target_pairs={{0,8},{1,9},{2,10},{3,11},{4,12},{5,13},{6,14},{7,15},{8,0},{9,1},... | collective-permute-start | bytes 393224 | tf_op jit(solution)/shard_map/ppermute | solution.py:16
  28.6 6.9 %collective-permute-start.3 = (bf16[2,16,2048]{2,1,0:T(8,128)(2,1)S(1)}, bf16[2,16,2048]{2,1,0:T(8,128)(2,1)S(1)}, u32[]{:S(2)}, u32[]{:S(2)}) collective-permute-start(bf16[2,16,2048]{2,1,0:T(8,128)(2,1)S(1)} %maximum_select_fusion.2), channel_id=1, source_target_pairs={{0,4},{1,5},{2,6},{3,7},{4,8},{5,9},{6,10},{7,11},{8,12},{9,13},{1... | collective-permute-start | bytes 393224 | tf_op jit(solution)/shard_map/ppermute | solution.py:16
  36.4 8.6 %collective-permute-start.4 = (bf16[4,2,16,2048]{3,2,1,0:T(8,128)(2,1)}, bf16[4,2,16,2048]{3,2,1,0:T(8,128)(2,1)S(1)}, u32[]{:S(2)}, u32[]{:S(2)}) collective-permute-start(bf16[4,2,16,2048]{3,2,1,0:T(8,128)(2,1)} %constant_dynamic-slice_fusion), channel_id=1, source_target_pairs={{0,1},{1,0},{2,3},{3,2},{4,5},{5,4},{6,7},{7,6},{8,9},{9,8},{10,11... | collective-permute-start | bytes 1572872 | tf_op jit(solution)/shard_map/ppermute | solution.py:16
  43.6 1.6 %copy-start.1 = (bf16[2048,384]{1,0:T(8,128)(2,1)S(1)}, bf16[2048,384]{1,0:T(8,128)(2,1)}, u32[]{:S(2)}) copy-start(bf16[2048,384]{1,0:T(8,128)(2,1)} %param.9) | copy-start | bytes 4718596
  45.1 0.9 copy-start.3
  50.7 16.0 %collective-permute-start.17 = (bf16[4,64,384]{2,1,0:T(8,128)(2,1)S(1)}, bf16[4,64,384]{2,1,0:T(8,128)(2,1)S(1)}, u32[]{:S(2)}, u32[]{:S(2)}) collective-permute-start(bf16[4,64,384]{2,1,0:T(8,128)(2,1)S(1)} %get-tuple-element.8), channel_id=1, source_target_pairs={{0,128},{16,144},{32,160},{48,176},{64,192},{80,208},{96,224},{112... | collective-permute-start | bytes 589832 | tf_op jit(solution)/shard_map/ppermute | solution.py:16
  53.9 12.9 %collective-permute-start.19 = (bf16[4,64,384]{2,1,0:T(8,128)(2,1)S(1)}, bf16[4,64,384]{2,1,0:T(8,128)(2,1)S(1)}, u32[]{:S(2)}, u32[]{:S(2)}) collective-permute-start(bf16[4,64,384]{2,1,0:T(8,128)(2,1)S(1)} %get-tuple-element.10), channel_id=1, source_target_pairs={{0,384},{16,400},{32,416},{48,432},{64,448},{80,464},{96,480},{112... | collective-permute-start | bytes 589832 | tf_op jit(solution)/shard_map/ppermute | solution.py:16
  57.3 20.9 %collective-permute-start.5 = (bf16[4,2,16,2048]{3,2,1,0:T(8,128)(2,1)S(1)}, bf16[4,2,16,2048]{3,2,1,0:T(8,128)(2,1)S(1)}, u32[]{:S(2)}, u32[]{:S(2)}) collective-permute-start(bf16[4,2,16,2048]{3,2,1,0:T(8,128)(2,1)S(1)} %dynamic-slice_bitcast_fusion), channel_id=1, source_target_pairs={{0,1},{1,0},{2,3},{3,2},{4,5},{5,4},{6,7},{7,6},{8,9},{9,8},{10,11... | collective-permute-start | bytes 1572872 | tf_op jit(solution)/shard_map/ppermute | solution.py:16
  60.2 12.1 %collective-permute-start.10 = (bf16[4,64,384]{2,1,0:T(8,128)(2,1)S(1)}, bf16[4,64,384]{2,1,0:T(8,128)(2,1)S(1)}, u32[]{:S(2)}, u32[]{:S(2)}) collective-permute-start(bf16[4,64,384]{2,1,0:T(8,128)(2,1)S(1)} %get-tuple-element.14), channel_id=1, source_target_pairs={{0,128},{16,144},{32,160},{48,176},{64,192},{80,208},{96,224},{112... | collective-permute-start | bytes 589832 | tf_op jit(solution)/shard_map/ppermute | solution.py:16
  62.2 10.1 %collective-permute-start.12 = (bf16[4,64,384]{2,1,0:T(8,128)(2,1)S(1)}, bf16[4,64,384]{2,1,0:T(8,128)(2,1)S(1)}, u32[]{:S(2)}, u32[]{:S(2)}) collective-permute-start(bf16[4,64,384]{2,1,0:T(8,128)(2,1)S(1)} %get-tuple-element.16), channel_id=1, source_target_pairs={{0,384},{16,400},{32,416},{48,432},{64,448},{80,464},{96,480},{112... | collective-permute-start | bytes 589832 | tf_op jit(solution)/shard_map/ppermute | solution.py:16
  66.9 13.4 %collective-permute-start.20 = (bf16[2,4,64,384]{3,2,1,0:T(8,128)(2,1)S(1)}, bf16[2,4,64,384]{3,2,1,0:T(8,128)(2,1)S(1)}, u32[]{:S(2)}, u32[]{:S(2)}) collective-permute-start(bf16[2,4,64,384]{3,2,1,0:T(8,128)(2,1)S(1)} %pad_maximum_fusion.3), channel_id=1, source_target_pairs={{0,384},{16,400},{32,416},{48,432},{64,448},{80,464},{96,480},{112... | collective-permute-start | bytes 1179656 | tf_op jit(solution)/shard_map/ppermute | solution.py:16
  69.0 14.7 %collective-permute-start.18 = (bf16[2,4,64,384]{3,2,1,0:T(8,128)(2,1)S(1)}, bf16[2,4,64,384]{3,2,1,0:T(8,128)(2,1)S(1)}, u32[]{:S(2)}, u32[]{:S(2)}) collective-permute-start(bf16[2,4,64,384]{3,2,1,0:T(8,128)(2,1)S(1)} %pad_maximum_fusion.2), channel_id=1, source_target_pairs={{0,128},{16,144},{32,160},{48,176},{64,192},{80,208},{96,224},{112... | collective-permute-start | bytes 1179656 | tf_op jit(solution)/shard_map/ppermute | solution.py:16
  72.5 15.1 %collective-permute-start.13 = (bf16[2,4,64,384]{3,2,1,0:T(8,128)(2,1)S(1)}, bf16[2,4,64,384]{3,2,1,0:T(8,128)(2,1)S(1)}, u32[]{:S(2)}, u32[]{:S(2)}) collective-permute-start(bf16[2,4,64,384]{3,2,1,0:T(8,128)(2,1)S(1)} %pad_maximum_fusion.1), channel_id=1, source_target_pairs={{0,384},{16,400},{32,416},{48,432},{64,448},{80,464},{96,480},{112... | collective-permute-start | bytes 1179656 | tf_op jit(solution)/shard_map/ppermute | solution.py:16
  76.3 13.8 %collective-permute-start.11 = (bf16[2,4,64,384]{3,2,1,0:T(8,128)(2,1)S(1)}, bf16[2,4,64,384]{3,2,1,0:T(8,128)(2,1)S(1)}, u32[]{:S(2)}, u32[]{:S(2)}) collective-permute-start(bf16[2,4,64,384]{3,2,1,0:T(8,128)(2,1)S(1)} %pad_maximum_fusion), channel_id=1, source_target_pairs={{0,128},{16,144},{32,160},{48,176},{64,192},{80,208},{96,224},{112... | collective-permute-start | bytes 1179656 | tf_op jit(solution)/shard_map/ppermute | solution.py:16
  78.4 14.2 %collective-permute-start.8 = (bf16[2,16,2048]{2,1,0:T(8,128)(2,1)S(1)}, bf16[2,16,2048]{2,1,0:T(8,128)(2,1)S(1)}, u32[]{:S(2)}, u32[]{:S(2)}) collective-permute-start(bf16[2,16,2048]{2,1,0:T(8,128)(2,1)S(1)} %get-tuple-element.21), channel_id=1, source_target_pairs={{0,12},{1,13},{2,14},{3,15},{4,0},{5,1},{6,2},{7,3},{8,4},{9,5},{1... | collective-permute-start | bytes 393224 | tf_op jit(solution)/shard_map/ppermute | solution.py:16
  80.4 12.3 %collective-permute-start.7 = (bf16[2,16,2048]{2,1,0:T(8,128)(2,1)S(1)}, bf16[2,16,2048]{2,1,0:T(8,128)(2,1)S(1)}, u32[]{:S(2)}, u32[]{:S(2)}) collective-permute-start(bf16[2,16,2048]{2,1,0:T(8,128)(2,1)S(1)} %get-tuple-element.22), channel_id=1, source_target_pairs={{0,8},{1,9},{2,10},{3,11},{4,12},{5,13},{6,14},{7,15},{8,0},{9,1},... | collective-permute-start | bytes 393224 | tf_op jit(solution)/shard_map/ppermute | solution.py:16
  83.7 9.0 %collective-permute-start.6 = (bf16[2,16,2048]{2,1,0:T(8,128)(2,1)S(1)}, bf16[2,16,2048]{2,1,0:T(8,128)(2,1)S(1)}, u32[]{:S(2)}, u32[]{:S(2)}) collective-permute-start(bf16[2,16,2048]{2,1,0:T(8,128)(2,1)S(1)} %get-tuple-element.20), channel_id=1, source_target_pairs={{0,4},{1,5},{2,6},{3,7},{4,8},{5,9},{6,10},{7,11},{8,12},{9,13},{1... | collective-permute-start | bytes 393224 | tf_op jit(solution)/shard_map/ppermute | solution.py:16
  90.4 18.4 %copy-start.2 = (bf16[16,2048]{1,0:T(8,128)(2,1)S(1)}, bf16[16,2048]{1,0:T(8,128)(2,1)}, u32[]{:S(2)}) copy-start(bf16[16,2048]{1,0:T(8,128)(2,1)} %param.6) | copy-start | bytes 196612
  90.5 18.4 %copy-start.4 = (bf16[2048]{0:T(1024)(128)(2,1)S(1)}, bf16[2048]{0:T(1024)(128)(2,1)}, u32[]{:S(2)}) copy-start(bf16[2048]{0:T(1024)(128)(2,1)} %param.8) | copy-start | bytes 12292
  90.5 19.3 %collective-permute-start.14 = (bf16[2,2,64,384]{3,2,1,0:T(8,128)(2,1)S(1)}, bf16[2,2,64,384]{3,2,1,0:T(8,128)(2,1)S(1)}, u32[]{:S(2)}, u32[]{:S(2)}) collective-permute-start(bf16[2,2,64,384]{3,2,1,0:T(8,128)(2,1)S(1)} %fusion.14), channel_id=1, source_target_pairs={{0,16},{16,0},{32,48},{48,32},{64,80},{80,64},{96,112},{112,96},{1... | collective-permute-start | bytes 589832 | tf_op jit(solution)/shard_map/ppermute | solution.py:16
  92.8 16.0 %collective-permute-start.9 = (bf16[16,2048]{1,0:T(8,128)(2,1)S(1)}, bf16[16,2048]{1,0:T(8,128)(2,1)S(1)}, u32[]{:S(2)}, u32[]{:S(2)}) collective-permute-start(bf16[16,2048]{1,0:T(8,128)(2,1)S(1)} %fusion.31), channel_id=1, source_target_pairs={{0,2},{1,3},{2,0},{3,1},{4,6},{5,7},{6,4},{7,5},{8,10},{9,11},{10,... | collective-permute-start | bytes 196616 | tf_op jit(solution)/shard_map/ppermute | solution.py:16
  105.4 12.9 %collective-permute-start.21 = (bf16[2,2,64,384]{3,2,1,0:T(8,128)(2,1)S(1)}, bf16[2,2,64,384]{3,2,1,0:T(8,128)(2,1)S(1)}, u32[]{:S(2)}, u32[]{:S(2)}) collective-permute-start(bf16[2,2,64,384]{3,2,1,0:T(8,128)(2,1)S(1)} %fusion.15), channel_id=1, source_target_pairs={{0,16},{16,0},{32,48},{48,32},{64,80},{80,64},{96,112},{112,96},{1... | collective-permute-start | bytes 589832 | tf_op jit(solution)/shard_map/ppermute | solution.py:16
  109.9 10.5 %collective-permute-start.15 = (bf16[2,64,384]{2,1,0:T(8,128)(2,1)S(1)}, bf16[2,64,384]{2,1,0:T(8,128)(2,1)S(1)}, u32[]{:S(2)}, u32[]{:S(2)}) collective-permute-start(bf16[2,64,384]{2,1,0:T(8,128)(2,1)S(1)} %fusion.29), channel_id=1, source_target_pairs={{0,32},{16,48},{32,0},{48,16},{64,96},{80,112},{96,64},{112,80},{1... | collective-permute-start | bytes 294920 | tf_op jit(solution)/shard_map/ppermute | solution.py:16
  118.4 9.8 %collective-permute-start.22 = (bf16[2,64,384]{2,1,0:T(8,128)(2,1)S(1)}, bf16[2,64,384]{2,1,0:T(8,128)(2,1)S(1)}, u32[]{:S(2)}, u32[]{:S(2)}) collective-permute-start(bf16[2,64,384]{2,1,0:T(8,128)(2,1)S(1)} %fusion.30), channel_id=1, source_target_pairs={{0,32},{16,48},{32,0},{48,16},{64,96},{80,112},{96,64},{112,80},{1... | collective-permute-start | bytes 294920 | tf_op jit(solution)/shard_map/ppermute | solution.py:16
  120.4 9.8 %collective-permute-start.16 = (bf16[64,384]{1,0:T(8,128)(2,1)S(1)}, bf16[64,384]{1,0:T(8,128)(2,1)S(1)}, u32[]{:S(2)}, u32[]{:S(2)}) collective-permute-start(bf16[64,384]{1,0:T(8,128)(2,1)S(1)} %fusion.32), channel_id=1, source_target_pairs={{0,64},{16,80},{32,96},{48,112},{64,0},{80,16},{96,32},{112,48},{1... | collective-permute-start | bytes 147464 | tf_op jit(solution)/shard_map/ppermute | solution.py:16
  128.3 10.4 %collective-permute-start.23 = (bf16[64,384]{1,0:T(8,128)(2,1)S(1)}, bf16[64,384]{1,0:T(8,128)(2,1)S(1)}, u32[]{:S(2)}, u32[]{:S(2)}) collective-permute-start(bf16[64,384]{1,0:T(8,128)(2,1)S(1)} %fusion.33), channel_id=1, source_target_pairs={{0,64},{16,80},{32,96},{48,112},{64,0},{80,16},{96,32},{112,48},{1... | collective-permute-start | bytes 147464 | tf_op jit(solution)/shard_map/ppermute | solution.py:16

commit v2 on v1

v2 whole, which is shorter than its diff:
```python
import jax
import jax.numpy as jnp
from jax import lax
from jax.experimental import pallas as pl
from jax.experimental.pallas import tpu as pltpu
from jax.sharding import PartitionSpec as P

NX, NZ = 4, 8
NY, NH, NC = 4, 2, 2
F32, BF16 = jnp.float32, jnp.bfloat16


def pick(array, index, axis):
    return lax.dynamic_index_in_dim(array, index, axis, keepdims=False)


def move(array, axis_name, count, target):
    return lax.ppermute(array, axis_name, [(i, target(i)) for i in range(count)])


def to_core(array):
    return move(array, "tensor", 16, lambda t: t ^ 1)


def to_y(array, target):
    return move(array, "tensor", 16, lambda t: 4 * target(t // 4) + t % 4)


def to_x(array, step):
    return move(array, "dp", 32, lambda d: (d + 8 * step) % 32)


def to_z(array, bit):
    return move(array, "dp", 32, lambda d: d ^ bit)


def to_high(array):
    return move(array, "tensor", 16, lambda t: t ^ 2)


def copy_kernel(array_ref, other_ref, out_ref):
    out_ref[...] = array_ref[...]


def after(array, other):
    return pl.pallas_call(
        copy_kernel,
        out_shape=jax.ShapeDtypeStruct(array.shape, array.dtype),
        in_specs=[pl.BlockSpec(memory_space=pltpu.VMEM), pl.BlockSpec(memory_space=pl.ANY)],
        out_specs=pl.BlockSpec(memory_space=pltpu.VMEM),
    )(array, other)


def gather_rows(normed, y, high, core):
    rows, depth = normed.shape
    across = to_high(normed)
    other = to_y(normed, lambda i: 3 - i)
    two = jnp.where(y < 2, jnp.stack([normed, other]), jnp.stack([other, normed]))
    got = to_y(jnp.concatenate([two, across[None]]), lambda i: i ^ 1)
    outer, even = (y == 0) | (y == 3), y % 2 == 0
    ends, middle = jnp.where(outer, two, got[:2]), jnp.where(outer, got[:2], two)
    near = jnp.stack([ends[0], middle[0], middle[1], ends[1]])
    two = jnp.where(even, jnp.stack([across, got[2]]), jnp.stack([got[2], across]))
    other = to_y(two, lambda i: 3 - i)
    away = jnp.where(y < 2, jnp.concatenate([two, other]), jnp.concatenate([other, two]))
    quad = jnp.where(high == 0, jnp.stack([near, away], axis=1), jnp.stack([away, near], axis=1))
    far = to_core(quad)
    both = jnp.where(core == 0, jnp.stack([quad, far], axis=2), jnp.stack([far, quad], axis=2))
    return both.reshape(16 * rows, depth)


def scatter_rows(share, early, late, y, high, core):
    rows = share.shape[0] // 16
    share = share.reshape(NY, NH, NC, rows, -1)
    got = to_core(pick(share, 1 - core, 2))
    total = pick(share, core, 2).astype(F32) + got.astype(F32)
    outer = (y == 0) | (y == 3)
    ends, middle = jnp.stack([total[0], total[3]]), total[1:3]
    got = to_y(jnp.where(outer, middle, ends).astype(BF16), lambda i: i ^ 1)
    total = jnp.where(outer, ends, middle) + got.astype(F32)
    sent = after(jnp.where(y < 2, total[1], total[0]).astype(BF16), early)
    got = to_y(sent, lambda i: 3 - i)
    total = jnp.where(y < 2, total[0], total[1]) + got.astype(F32)
    got = to_high(pick(total, 1 - high, 0).astype(BF16))
    return pick(total, high, 0) + after(got, late).astype(F32)


LANES = 128


def call(kernel, outs, scratch, place, flops, *arrays):
    moved = sum(a.size * a.dtype.itemsize for a in (*arrays, *outs))
    return pl.pallas_call(
        kernel,
        out_shape=outs,
        in_specs=[pl.BlockSpec(memory_space=pltpu.SMEM)]
        + [pl.BlockSpec(memory_space=pltpu.VMEM)] * len(arrays),
        out_specs=[pl.BlockSpec(memory_space=pltpu.VMEM)] * len(outs),
        scratch_shapes=scratch,
        compiler_params=pltpu.CompilerParams(vmem_limit_bytes=32 * 2**20),
        cost_estimate=pl.CostEstimate(flops=flops, bytes_accessed=moved, transcendentals=0),
    )(place, *arrays)


def columns(ref, index, rows=slice(None)):
    width = ref.shape[1] // NX
    return ref[rows, pl.ds(pl.multiple_of(index * width, LANES), width)]


def put(ref, row, block):
    for start in range(0, block.shape[1], LANES):
        ref[row : row + block.shape[0], :] = block[:, start : start + LANES]
        row += block.shape[0]
    return row


def lanes(ref, row, rows, width):
    return jnp.concatenate([ref[row + i * rows : row + (i + 1) * rows, :] for i in range(width // LANES)], axis=1)


def pack_kernel(place, rows_ref, gate_ref, up_ref, right_ref, left_ref, gate_out, up_out):
    x, core = place[0], place[1]
    half = rows_ref.shape[0] // 2
    mine = pl.ds(pl.multiple_of(core * half, half), half)
    row = put(right_ref, 0, up_ref[...])
    row = put(right_ref, row, columns(rows_ref, lax.rem(x + 1, NX), mine))
    row = put(right_ref, row, gate_ref[...])
    put(right_ref, row, columns(rows_ref, lax.rem(x + 2, NX), slice(0, half)))
    row = put(left_ref, 0, gate_ref[...])
    row = put(left_ref, row, columns(rows_ref, lax.rem(x + 3, NX), mine))
    row = put(left_ref, row, up_ref[...])
    put(left_ref, row, columns(rows_ref, lax.rem(x + 2, NX), slice(half, 2 * half)))
    gate_out[...] = gate_ref[...]
    up_out[...] = up_ref[...]


def times(rows, deltas, out, total=None):
    depth = rows.shape[1]
    for start in range(0, depth, LANES):
        part = lax.dot_general(
            rows[:, start : start + LANES],
            deltas[...],
            (((0,), (0,)), ((), ())),
            preferred_element_type=F32,
        )
        if total is not None:
            part = part + total[start : start + LANES, :]
        out[start : start + LANES, :] = part


def near_kernel(place, rows_ref, gate_ref, up_ref, left_ref, right_ref, other_ref, out_ref, rows, deltas):
    x, core = place[0], place[1]
    count, width = gate_ref.shape
    half, quarter = count // 2, rows_ref.shape[1] // NX
    mine = pl.multiple_of(core * half, half)
    others = pl.multiple_of((1 - core) * half, half)
    chunk, piece = count * width // LANES, half * quarter // LANES
    rows[0:count, :] = columns(rows_ref, x)
    deltas[0:count, 0:width] = gate_ref[...]
    deltas[0:count, width : 2 * width] = up_ref[...]
    for step, ref in ((1, left_ref), (2, right_ref)):
        rows[pl.ds(step * count + mine, half), :] = lanes(ref, chunk, half, quarter)
        rows[pl.ds(step * count + others, half), :] = lanes(other_ref, (step - 1) * piece, half, quarter)
        low, high = lanes(ref, 0, count, width), lanes(ref, chunk + piece, count, width)
        gate, up = (high, low) if step == 1 else (low, high)
        deltas[step * count : (step + 1) * count, 0:width] = gate
        deltas[step * count : (step + 1) * count, width : 2 * width] = up
    times(rows, deltas, out_ref)


def far_kernel(
    place, near_ref, left_ref, right_ref, gate_out, up_out, gate_keep, up_keep, rows, deltas, total
):
    bit = place[2]
    count, width = rows.shape[0], gate_out.shape[1]
    half, quarter = count // 2, rows.shape[1]
    chunk = count * width // LANES
    rows[0:half, :] = lanes(left_ref, chunk, half, quarter)
    rows[half:count, :] = lanes(right_ref, chunk, half, quarter)
    deltas[:, 0:width] = lanes(left_ref, 0, count, width)
    deltas[:, width : 2 * width] = lanes(right_ref, 0, count, width)
    times(rows, deltas, total, near_ref)
    small = quarter // NZ
    for k in range(NZ // 2):
        to = slice(k * small, (k + 1) * small)
        keep = pl.ds(pl.multiple_of((2 * k + bit) * small, small), small)
        send = pl.ds(pl.multiple_of((2 * k + 1 - bit) * small, small), small)
        gate_keep[to, :] = total[keep, 0:width]
        up_keep[to, :] = total[keep, width : 2 * width]
        gate_out[to, :] = total[send, 0:width].astype(BF16)
        up_out[to, :] = total[send, width : 2 * width].astype(BF16)


def weight_parts(gathered, gate_delta, up_delta, x, z, core):
    count, width = gate_delta.shape
    half, quarter = count // 2, gathered.shape[1] // NX
    chunk, piece = count * width // LANES, half * quarter // LANES
    place = jnp.stack([x, core, z % 2]).astype(jnp.int32)
    shape = jax.ShapeDtypeStruct
    message = shape((2 * (chunk + piece), LANES), BF16)
    outs = [message] * 2 + [shape(gate_delta.shape, BF16)] * 2
    right, left, gate_delta, up_delta = call(
        pack_kernel, outs, [], place, 0, gathered, gate_delta, up_delta
    )
    left, right = to_x(right, 1), to_x(left, -1)
    far_left = to_x(left[chunk + piece :], 1)
    far_right = to_x(right[chunk + piece :], -1)
    near = slice(chunk, chunk + piece)
    other = to_core(jnp.concatenate([left[near], right[near]]))
    both = pltpu.VMEM((3 * count, quarter), BF16), pltpu.VMEM((3 * count, 2 * width), BF16)
    outs = [shape((quarter, 2 * width), F32)]
    flops = 2 * 3 * count * quarter * 2 * width
    (total,) = call(
        near_kernel, outs, both, place, flops, gathered, gate_delta, up_delta, left, right, other
    )
    both = pltpu.VMEM((count, quarter), BF16), pltpu.VMEM((count, 2 * width), BF16)
    outs = [shape((quarter // 2, width), BF16)] * 2 + [shape((quarter // 2, width), F32)] * 2
    scratch = [*both, pltpu.VMEM((quarter, 2 * width), F32)]
    parts = call(far_kernel, outs, scratch, place, flops // 3, total, far_left, far_right)
    return parts, gate_delta, up_delta, other


def scatter_z(sent, kept, z):
    total = kept + to_z(sent, 1).astype(F32)
    total = total.reshape(2, 2, total.shape[0] * 2 // NZ, -1)
    bits = ((z // 4) % 2, (z // 2) % 2)
    for axis, bit in ((1, 2), (0, 4)):
        sent = pick(total, 1 - bits[axis], axis).astype(BF16)
        got = to_z(sent, bit)
        total = pick(total, bits[axis], axis) + got.astype(F32)
    return total, sent


def shards(tokens, masked, mask_vector, gate_weight, up_weight, cotangent):
    dp = lax.axis_index("dp")
    tensor = lax.axis_index("tensor")
    x, z = dp // NZ, dp % NZ
    y, high, core = tensor // 4, (tensor // 2) % 2, tensor % 2
    flag = masked[:, None] == 1
    mixed_in = jnp.where(flag, mask_vector[None, :], tokens)
    mixed_f = mixed_in.astype(F32)
    inverse = lax.rsqrt(jnp.mean(mixed_f * mixed_f, axis=-1, keepdims=True) + 1e-06)
    normed_full = mixed_f * inverse
    gathered = gather_rows(normed_full.astype(BF16), y, high, core)
    gate = jnp.dot(gathered, gate_weight, preferred_element_type=F32)
    up = jnp.dot(gathered, up_weight, preferred_element_type=F32)
    sig = jax.nn.sigmoid(gate)
    hidden = (gate * sig * up).astype(BF16)
    cot = cotangent.astype(F32)
    up_delta = (cot * gate * sig).astype(BF16)
    gate_delta = (cot * up * sig * (1.0 + gate * (1.0 - sig))).astype(BF16)
    sent, gate_delta, up_delta, other = weight_parts(gathered, gate_delta, up_delta, x, z, core)
    gate_grad, late = scatter_z(sent[0], sent[2], z)
    up_grad, _ = scatter_z(sent[1], sent[3], z)
    contract_last = (((1,), (1,)), ((), ()))
    first = lax.dot_general(gate_delta, gate_weight, contract_last, preferred_element_type=F32)
    second = lax.dot_general(up_delta, up_weight, contract_last, preferred_element_type=F32)
    normed_grad = scatter_rows((first + second).astype(BF16), other, late, y, high, core)
    inner = jnp.mean(normed_grad * normed_full, axis=-1, keepdims=True)
    token_grad = jnp.where(flag, 0.0, inverse * (normed_grad - normed_full * inner)).astype(BF16)
    return (hidden, token_grad, gate_grad, up_grad)


def solution(mesh):
    return jax.shard_map(
        shards,
        mesh=mesh,
        in_specs=(
            P(("dp", "tensor"), None),
            P(("dp", "tensor")),
            P(),
            P(None, "tensor"),
            P(None, "tensor"),
            P("dp", "tensor"),
        ),
        out_specs=(
            P("dp", "tensor"),
            P(("dp", "tensor"), None),
            P("dp", "tensor"),
            P("dp", "tensor"),
        ),
        check_vma=False,
    )
```

time: 141 us -> 154 us (1.092)
  local copies, waits for them, and re-layouts: 1.59 us -> 10.6 us
  starting transfers between devices: 97 us -> 88.4 us
  Pallas kernels: 0 us -> 6.96 us
  waiting for transfers between devices: 25.7 us -> 31 us
  other arithmetic: 8.14 us -> 10.6 us
  matrix products: 5.28 us -> 3.73 us
    ppermute x24 -> x20, starting transfers between devices: 97 us -> 88.4 us  [move(): lax.ppermute(array, axis_name, [(i, target(i)) for i in range(count)])]
    unnamed x15 -> x40, local copies, waits for them, and re-layouts: 0.26 us -> 8.05 us
    pallas_call x0 -> x5, Pallas kernels: none -> 6.96 us  [the longest x3 3.91 us: call(): pl.pallas_call(kernel, out_shape=outs, in_specs=[pl.BlockSpec(memory_spac...]
    ppermute x24 -> x20, waiting for transfers between devices: 25.7 us -> 31 us  [move(): lax.ppermute(array, axis_name, [(i, target(i)) for i in range(count)])]
    slice x0 -> x7, local copies, waits for them, and re-layouts: none -> 1.58 us  [the longest x1 0.77 us: weight_parts(): far_right = to_x(right[chunk + piece:], -1)]
    dot_general x2 -> x0, matrix products: 1.55 us -> none  [the longest x1 0.81 us: shards(): lax.dot_general(gathered, up_delta, contract_first, preferred_element_typ...]
  transfers between devices with their start and end apart: 24 -> 20, of which waited for: 8 -> 7; matrix products, arithmetic and copies ran while one was open for 4% -> 6% of each run, Pallas kernels for 0% -> 4%
where the time goes in v2:
time: 154 us; the launch traced here: 153 us
  starting transfers between devices  88.4 us (57%)
  waiting for transfers between devices  31 us (20%)
  local copies, waits for them, and re-layouts  10.6 us (7%)
  other arithmetic  10.6 us (7%)
  Pallas kernels  6.96 us (5%)
  matrix products  3.73 us (2%)
  between operations  1.54 us (1%)
    ppermute x20, starting transfers between devices, move(): lax.ppermute(array, axis_name, [(i, target(i)) for i in range(count)])  88.4 us
    ppermute x20, waiting for transfers between devices, move(): lax.ppermute(array, axis_name, [(i, target(i)) for i in range(count)])  31 us
    unnamed x40, local copies, waits for them, and re-layouts  8.05 us
    pallas_call x3, Pallas kernels, call(): pl.pallas_call(kernel, out_shape=outs, in_specs=[pl.BlockSpec(memory_spac...  3.91 us
  transfers between devices with their start and end apart: 20, of which 7 were waited for; matrix products, arithmetic and copies ran while one was open for 6% of the time, Pallas kernels for 4%

profile of v2, /device:TPU:1, one launch (start us, length us, event | category | flops | bytes accessed | tf_op | source)
XLA Modules:
  0.0 152.8 jit_solution(1517054518895879886)
XLA Ops:
  0.6 0.8 broadcast_compare_fusion
  1.4 1.0 fusion.14
  2.5 0.9 fusion.8
  3.4 5.5 %collective-permute-start = (bf16[16,2048]{1,0:T(8,128)(2,1)S(1)}, bf16[16,2048]{1,0:T(8,128)(2,1)S(1)}, u32[]{:S(2)}, u32[]{:S(2)}) collective-permute-start(bf16[16,2048]{1,0:T(8,128)(2,1)S(1)} %fusion.8), channel_id=1, source_target_pairs={{0,12},{1,13},{2,14},{3,15},{4,8},{5,9},{6,10},{7,11},{8,4},{9,5},... | collective-permute-start | bytes 196616 | tf_op jit(solution)/shard_map/ppermute | solution.py:18
  8.9 15.4 %collective-permute-start.1 = (bf16[16,2048]{1,0:T(8,128)(2,1)S(1)}, bf16[16,2048]{1,0:T(8,128)(2,1)S(1)}, u32[]{:S(2)}, u32[]{:S(2)}) collective-permute-start(bf16[16,2048]{1,0:T(8,128)(2,1)S(1)} %fusion.8), channel_id=1, source_target_pairs={{0,2},{1,3},{2,0},{3,1},{4,6},{5,7},{6,4},{7,5},{8,10},{9,11},{10,... | collective-permute-start | bytes 196616 | tf_op jit(solution)/shard_map/ppermute | solution.py:18
  24.3 0.9 fusion.36
  25.3 0.8 collective-permute-done.1
  26.1 1.9 %collective-permute-start.2 = (bf16[3,16,2048]{2,1,0:T(8,128)(2,1)S(1)}, bf16[3,16,2048]{2,1,0:T(8,128)(2,1)S(1)}, u32[]{:S(2)}, u32[]{:S(2)}) collective-permute-start(bf16[3,16,2048]{2,1,0:T(8,128)(2,1)S(1)} %pad_maximum_fusion.3), channel_id=1, source_target_pairs={{0,4},{1,5},{2,6},{3,7},{4,0},{5,1},{6,2},{7,3},{8,12},{9,13},{10,... | collective-permute-start | bytes 589832 | tf_op jit(solution)/shard_map/ppermute | solution.py:18
  28.1 4.4 %collective-permute-done.2 = bf16[3,16,2048]{2,1,0:T(8,128)(2,1)S(1)} collective-permute-done((bf16[3,16,2048]{2,1,0:T(8,128)(2,1)S(1)}, bf16[3,16,2048]{2,1,0:T(8,128)(2,1)S(1)}, u32[]{:S(2)}, u32[]{:S(2)}) %collective-permute-start.2) | collective-permute-done | bytes 196640 | tf_op jit(solution)/shard_map/ppermute | solution.py:18
  32.6 1.9 %collective-permute-start.3 = (bf16[2,16,2048]{2,1,0:T(8,128)(2,1)S(1)}, bf16[2,16,2048]{2,1,0:T(8,128)(2,1)S(1)}, u32[]{:S(2)}, u32[]{:S(2)}) collective-permute-start(bf16[2,16,2048]{2,1,0:T(8,128)(2,1)S(1)} %maximum_select_fusion.5), channel_id=1, source_target_pairs={{0,12},{1,13},{2,14},{3,15},{4,8},{5,9},{6,10},{7,11},{8,4},{9,5},... | collective-permute-start | bytes 393224 | tf_op jit(solution)/shard_map/ppermute | solution.py:18
  34.7 4.9 %collective-permute-done.3 = bf16[2,16,2048]{2,1,0:T(8,128)(2,1)S(1)} collective-permute-done((bf16[2,16,2048]{2,1,0:T(8,128)(2,1)S(1)}, bf16[2,16,2048]{2,1,0:T(8,128)(2,1)S(1)}, u32[]{:S(2)}, u32[]{:S(2)}) %collective-permute-start.3) | collective-permute-done | bytes 131104 | tf_op jit(solution)/shard_map/ppermute | solution.py:18
  39.6 0.1 maximum_select_fusion.2
  39.7 7.6 %collective-permute-start.4 = (bf16[4,2,16,2048]{3,2,0,1:T(8,128)(2,1)S(1)}, bf16[4,2,16,2048]{3,2,0,1:T(8,128)(2,1)S(1)}, u32[]{:S(2)}, u32[]{:S(2)}) collective-permute-start(bf16[4,2,16,2048]{3,2,0,1:T(8,128)(2,1)S(1)} %maximum_select_fusion.2), channel_id=1, source_target_pairs={{0,1},{1,0},{2,3},{3,2},{4,5},{5,4},{6,7},{7,6},{8,9},{9,8},{10,11... | collective-permute-start | bytes 1572872 | tf_op jit(solution)/shard_map/ppermute | solution.py:18
  47.3 0.1 pad_add_fusion.place
  47.4 0.1 maximum_select_fusion.1
  47.5 1.3 collective-permute-done.4
  48.8 0.2 maximum_select_fusion
  49.1 1.3 copy-done.11
  50.4 0.7 fusion.25
  51.1 1.5 fusion.3
  52.7 0.7 shard_map.93
  53.5 0.7 fusion.26
  54.2 0.1 copy-done.9
  54.3 0.2 copy-done.10
  54.6 0.7 fusion
  55.4 1.0 copy-done.12
  56.3 0.8 dynamic-slice_bitcast_fusion
  57.2 2.3 %collective-permute-start.5 = (bf16[4,2,16,2048]{3,2,1,0:T(8,128)(2,1)}, bf16[4,2,16,2048]{3,2,1,0:T(8,128)(2,1)}, u32[]{:S(2)}, u32[]{:S(2)}) collective-permute-start(bf16[4,2,16,2048]{3,2,1,0:T(8,128)(2,1)} %dynamic-slice_bitcast_fusion), channel_id=1, source_target_pairs={{0,1},{1,0},{2,3},{3,2},{4,5},{5,4},{6,7},{7,6},{8,9},{9,8},{10,11... | collective-permute-start | bytes 1572872 | tf_op jit(solution)/shard_map/ppermute | solution.py:18
  59.5 3.1 %collective-permute-start.7 = (bf16[2560,128]{1,0:T(8,128)(2,1)}, bf16[2560,128]{1,0:T(8,128)(2,1)S(1)}, u32[]{:S(2)}, u32[]{:S(2)}) collective-permute-start(bf16[2560,128]{1,0:T(8,128)(2,1)} %copy-done.10), channel_id=1, source_target_pairs={{0,128},{16,144},{32,160},{48,176},{64,192},{80,208},{96,224},{112... | collective-permute-start | bytes 1966088 | tf_op jit(solution)/shard_map/ppermute | solution.py:18
  62.6 3.4 %collective-permute-start.8 = (bf16[2560,128]{1,0:T(8,128)(2,1)}, bf16[2560,128]{1,0:T(8,128)(2,1)S(1)}, u32[]{:S(2)}, u32[]{:S(2)}) collective-permute-start(bf16[2560,128]{1,0:T(8,128)(2,1)} %copy-done.9), channel_id=1, source_target_pairs={{0,384},{16,400},{32,416},{48,432},{64,448},{80,464},{96,480},{112... | collective-permute-start | bytes 1966088 | tf_op jit(solution)/shard_map/ppermute | solution.py:18
  66.0 1.3 convert_add_fusion
  67.4 1.9 %collective-permute-start.6 = (bf16[2,2,16,2048]{3,2,1,0:T(8,128)(2,1)S(1)}, bf16[2,2,16,2048]{3,2,1,0:T(8,128)(2,1)S(1)}, u32[]{:S(2)}, u32[]{:S(2)}) collective-permute-start(bf16[2,2,16,2048]{3,2,1,0:T(8,128)(2,1)S(1)} %select_convert_fusion), channel_id=1, source_target_pairs={{0,4},{1,5},{2,6},{3,7},{4,0},{5,1},{6,2},{7,3},{8,12},{9,13},{10,... | collective-permute-start | bytes 786440 | tf_op jit(solution)/shard_map/ppermute | solution.py:18
  69.4 9.6 %collective-permute-done.7.left_ref = bf16[2560,128]{1,0:T(8,128)(2,1)S(1)} collective-permute-done((bf16[2560,128]{1,0:T(8,128)(2,1)}, bf16[2560,128]{1,0:T(8,128)(2,1)S(1)}, u32[]{:S(2)}, u32[]{:S(2)}) %collective-permute-start.7) | collective-permute-done | bytes 655392 | tf_op jit(solution)/shard_map/ppermute | solution.py:18
  79.0 1.6 %collective-permute-done.8.right_ref = bf16[2560,128]{1,0:T(8,128)(2,1)S(1)} collective-permute-done((bf16[2560,128]{1,0:T(8,128)(2,1)}, bf16[2560,128]{1,0:T(8,128)(2,1)S(1)}, u32[]{:S(2)}, u32[]{:S(2)}) %collective-permute-start.8) | collective-permute-done | bytes 655392 | tf_op jit(solution)/shard_map/ppermute | solution.py:18
  80.6 3.2 %collective-permute-start.9 = (bf16[1024,128]{1,0:T(8,128)(2,1)S(1)}, bf16[1024,128]{1,0:T(8,128)(2,1)S(1)}, u32[]{:S(2)}, u32[]{:S(2)}) collective-permute-start(bf16[1024,128]{1,0:T(8,128)(2,1)S(1)} %pad_maximum_fusion.2), channel_id=1, source_target_pairs={{0,1},{1,0},{2,3},{3,2},{4,5},{5,4},{6,7},{7,6},{8,9},{9,8},{10,11... | collective-permute-start | bytes 786440 | tf_op jit(solution)/shard_map/ppermute | solution.py:18
  83.8 0.7 slice.70
  84.5 3.1 %collective-permute-start.12 = (bf16[1280,128]{1,0:T(8,128)(2,1)}, bf16[1280,128]{1,0:T(8,128)(2,1)}, u32[]{:S(2)}, u32[]{:S(2)}) collective-permute-start(bf16[1280,128]{1,0:T(8,128)(2,1)} %slice.70), channel_id=1, source_target_pairs={{0,128},{16,144},{32,160},{48,176},{64,192},{80,208},{96,224},{112... | collective-permute-start | bytes 983048 | tf_op jit(solution)/shard_map/ppermute | solution.py:18
  87.7 0.8 slice.71
  88.4 3.4 %collective-permute-start.13 = (bf16[1280,128]{1,0:T(8,128)(2,1)}, bf16[1280,128]{1,0:T(8,128)(2,1)}, u32[]{:S(2)}, u32[]{:S(2)}) collective-permute-start(bf16[1280,128]{1,0:T(8,128)(2,1)} %slice.71), channel_id=1, source_target_pairs={{0,384},{16,400},{32,416},{48,432},{64,448},{80,464},{96,480},{112... | collective-permute-start | bytes 983048 | tf_op jit(solution)/shard_map/ppermute | solution.py:18
  91.9 0.8 fusion.15.array_ref
  92.7 0.1 copy-done.13
  92.8 0.7 copy-done.3
  93.5 1.6 %shard_map.94 = bf16[2,16,2048]{2,1,0:T(8,128)(2,1)} custom-call(bf16[2,16,2048]{2,1,0:T(8,128)(2,1)} %fusion.15.array_ref, bf16[1024,128]{1,0:T(8,128)(2,1)} %copy-done.3), custom_call_target="tpu_custom_call" | custom-call | tf_op jit(solution)/shard_map/pallas_call | solution.py:46
  95.1 2.5 %collective-permute-start.10 = (bf16[2,16,2048]{2,1,0:T(8,128)(2,1)}, bf16[2,16,2048]{2,1,0:T(8,128)(2,1)S(1)}, u32[]{:S(2)}, u32[]{:S(2)}) collective-permute-start(bf16[2,16,2048]{2,1,0:T(8,128)(2,1)} %shard_map.94), channel_id=1, source_target_pairs={{0,12},{1,13},{2,14},{3,15},{4,8},{5,9},{6,10},{7,11},{8,4},{9,5},... | collective-permute-start | bytes 393224 | tf_op jit(solution)/shard_map/ppermute | solution.py:18
  97.6 1.1 copy-done.2
  98.7 0.9 copy-done.4
  99.7 0.9 copy-done.6
  100.6 0.9 copy-done.8
  101.5 1.5 shard_map.95.near_ref
  103.1 1.7 %shard_map.96 = (bf16[256,384]{1,0:T(8,128)(2,1)S(1)}, bf16[256,384]{1,0:T(8,128)(2,1)S(1)}, f32[256,384]{1,0:T(8,128)S(1)}, f32[256,384]{1,0:T(8,128)S(1)}) custom-call(s32[3]{0:T(128)S(1)} %pad_add_fusion.place, f32[512,768]{1,0:T(8,128)S(1)} %shard_map.95.near_ref, bf16[1280,128]{1,0:T(8,128)(2,1)} %collective-permute-done.12.left_ref, ...), custom_call_target="tpu_custom_call" | custom-call | flops 201326592 | bytes 3407872 | tf_op jit(solution)/shard_map/pallas_call | solution.py:93
  104.7 1.9 %collective-permute-start.17 = (bf16[256,384]{1,0:T(8,128)(2,1)S(1)}, bf16[256,384]{1,0:T(8,128)(2,1)S(1)}, u32[]{:S(2)}, u32[]{:S(2)}) collective-permute-start(bf16[256,384]{1,0:T(8,128)(2,1)S(1)} %get-tuple-element.19), channel_id=1, source_target_pairs={{0,16},{16,0},{32,48},{48,32},{64,80},{80,64},{96,112},{112,96},{1... | collective-permute-start | bytes 589832 | tf_op jit(solution)/shard_map/ppermute | solution.py:18
  106.7 3.4 %collective-permute-start.14 = (bf16[256,384]{1,0:T(8,128)(2,1)S(1)}, bf16[256,384]{1,0:T(8,128)(2,1)S(1)}, u32[]{:S(2)}, u32[]{:S(2)}) collective-permute-start(bf16[256,384]{1,0:T(8,128)(2,1)S(1)} %get-tuple-element.17), channel_id=1, source_target_pairs={{0,16},{16,0},{32,48},{48,32},{64,80},{80,64},{96,112},{112,96},{1... | collective-permute-start | bytes 589832 | tf_op jit(solution)/shard_map/ppermute | solution.py:18
  110.1 12.5 %collective-permute-start.11 = (bf16[16,2048]{1,0:T(8,128)(2,1)S(1)}, bf16[16,2048]{1,0:T(8,128)(2,1)S(1)}, u32[]{:S(2)}, u32[]{:S(2)}) collective-permute-start(bf16[16,2048]{1,0:T(8,128)(2,1)S(1)} %fusion.20), channel_id=1, source_target_pairs={{0,2},{1,3},{2,0},{3,1},{4,6},{5,7},{6,4},{7,5},{8,10},{9,11},{10,... | collective-permute-start | bytes 196616 | tf_op jit(solution)/shard_map/ppermute | solution.py:18
  122.8 3.0 %collective-permute-start.18 = (bf16[2,64,384]{2,1,0:T(8,128)(2,1)S(1)}, bf16[2,64,384]{2,1,0:T(8,128)(2,1)S(1)}, u32[]{:S(2)}, u32[]{:S(2)}) collective-permute-start(bf16[2,64,384]{2,1,0:T(8,128)(2,1)S(1)} %fusion.19), channel_id=1, source_target_pairs={{0,32},{16,48},{32,0},{48,16},{64,96},{80,112},{96,64},{112,80},{1... | collective-permute-start | bytes 294920 | tf_op jit(solution)/shard_map/ppermute | solution.py:18
  125.9 3.2 %collective-permute-start.15 = (bf16[2,64,384]{2,1,0:T(8,128)(2,1)S(1)}, bf16[2,64,384]{2,1,0:T(8,128)(2,1)S(1)}, u32[]{:S(2)}, u32[]{:S(2)}) collective-permute-start(bf16[2,64,384]{2,1,0:T(8,128)(2,1)S(1)} %fusion.18), channel_id=1, source_target_pairs={{0,32},{16,48},{32,0},{48,16},{64,96},{80,112},{96,64},{112,80},{1... | collective-permute-start | bytes 294920 | tf_op jit(solution)/shard_map/ppermute | solution.py:18
  129.1 8.3 %collective-permute-done.18 = bf16[2,64,384]{2,1,0:T(8,128)(2,1)S(1)} collective-permute-done((bf16[2,64,384]{2,1,0:T(8,128)(2,1)S(1)}, bf16[2,64,384]{2,1,0:T(8,128)(2,1)S(1)}, u32[]{:S(2)}, u32[]{:S(2)}) %collective-permute-start.18) | collective-permute-done | bytes 98336 | tf_op jit(solution)/shard_map/ppermute | solution.py:18
  137.4 3.2 %collective-permute-start.19 = (bf16[64,384]{1,0:T(8,128)(2,1)S(1)}, bf16[64,384]{1,0:T(8,128)(2,1)S(1)}, u32[]{:S(2)}, u32[]{:S(2)}) collective-permute-start(bf16[64,384]{1,0:T(8,128)(2,1)S(1)} %fusion.22), channel_id=1, source_target_pairs={{0,64},{16,80},{32,96},{48,112},{64,0},{80,16},{96,32},{112,48},{1... | collective-permute-start | bytes 147464 | tf_op jit(solution)/shard_map/ppermute | solution.py:18
  140.7 6.0 %collective-permute-start.16 = (bf16[64,384]{1,0:T(8,128)(2,1)S(1)}, bf16[64,384]{1,0:T(8,128)(2,1)S(1)}, u32[]{:S(2)}, u32[]{:S(2)}) collective-permute-start(bf16[64,384]{1,0:T(8,128)(2,1)S(1)} %fusion.21.other_ref), channel_id=1, source_target_pairs={{0,64},{16,80},{32,96},{48,112},{64,0},{80,16},{96,32},{112,48},{1... | collective-permute-start | bytes 147464 | tf_op jit(solution)/shard_map/ppermute | solution.py:18
  146.7 0.6 copy-done.18
  147.4 1.5 shard_map.97
  148.8 1.0 fusion.9
  149.9 1.6 %fusion.13 = bf16[16,2048]{1,0:T(8,128)(2,1)} fusion(bf16[16,2048]{1,0:T(8,128)(2,1)} %shard_map.97, f32[2,16,2048]{2,1,0:T(8,128)S(1)} %bitcast_add_fusion, s32[]{:T(128)S(6)} %select_n.243, f32[16]{0:T(128)S(1)} %broadcast_multiply_fusion, f32[16]{0:T(128)S(1)} %add_rsqrt_fusion, pred[16]{0:T(512)(128)(4,1)S(1)} %broadcast_compare_fusion, ...), kind=kLoop, calls=%fused_computation.40 | loop fusion | flops 327680 | bytes 331924 | tf_op jit(solution)/shard_map/convert_element_type | solution.py:260
  151.5 0.7 bitcast_add_fusion.4
  152.1 0.7 bitcast_add_fusion.5
  (70 shorter events, 0.9 us)
Async XLA Ops:
  0.6 50.5 %copy-start = (bf16[2048,384]{1,0:T(8,128)(2,1)S(1)}, bf16[2048,384]{1,0:T(8,128)(2,1)}, u32[]{:S(2)}) copy-start(bf16[2048,384]{1,0:T(8,128)(2,1)} %param.10) | copy-start | bytes 4718596
  3.4 21.9 %collective-permute-start = (bf16[16,2048]{1,0:T(8,128)(2,1)S(1)}, bf16[16,2048]{1,0:T(8,128)(2,1)S(1)}, u32[]{:S(2)}, u32[]{:S(2)}) collective-permute-start(bf16[16,2048]{1,0:T(8,128)(2,1)S(1)} %fusion.8), channel_id=1, source_target_pairs={{0,12},{1,13},{2,14},{3,15},{4,8},{5,9},{6,10},{7,11},{8,4},{9,5},... | collective-permute-start | bytes 196616 | tf_op jit(solution)/shard_map/ppermute | solution.py:18
  8.9 17.2 %collective-permute-start.1 = (bf16[16,2048]{1,0:T(8,128)(2,1)S(1)}, bf16[16,2048]{1,0:T(8,128)(2,1)S(1)}, u32[]{:S(2)}, u32[]{:S(2)}) collective-permute-start(bf16[16,2048]{1,0:T(8,128)(2,1)S(1)} %fusion.8), channel_id=1, source_target_pairs={{0,2},{1,3},{2,0},{3,1},{4,6},{5,7},{6,4},{7,5},{8,10},{9,11},{10,... | collective-permute-start | bytes 196616 | tf_op jit(solution)/shard_map/ppermute | solution.py:18
  26.1 6.4 %collective-permute-start.2 = (bf16[3,16,2048]{2,1,0:T(8,128)(2,1)S(1)}, bf16[3,16,2048]{2,1,0:T(8,128)(2,1)S(1)}, u32[]{:S(2)}, u32[]{:S(2)}) collective-permute-start(bf16[3,16,2048]{2,1,0:T(8,128)(2,1)S(1)} %pad_maximum_fusion.3), channel_id=1, source_target_pairs={{0,4},{1,5},{2,6},{3,7},{4,0},{5,1},{6,2},{7,3},{8,12},{9,13},{10,... | collective-permute-start | bytes 589832 | tf_op jit(solution)/shard_map/ppermute | solution.py:18
  32.6 6.9 %collective-permute-start.3 = (bf16[2,16,2048]{2,1,0:T(8,128)(2,1)S(1)}, bf16[2,16,2048]{2,1,0:T(8,128)(2,1)S(1)}, u32[]{:S(2)}, u32[]{:S(2)}) collective-permute-start(bf16[2,16,2048]{2,1,0:T(8,128)(2,1)S(1)} %maximum_select_fusion.5), channel_id=1, source_target_pairs={{0,12},{1,13},{2,14},{3,15},{4,8},{5,9},{6,10},{7,11},{8,4},{9,5},... | collective-permute-start | bytes 393224 | tf_op jit(solution)/shard_map/ppermute | solution.py:18
  39.7 9.1 %collective-permute-start.4 = (bf16[4,2,16,2048]{3,2,0,1:T(8,128)(2,1)S(1)}, bf16[4,2,16,2048]{3,2,0,1:T(8,128)(2,1)S(1)}, u32[]{:S(2)}, u32[]{:S(2)}) collective-permute-start(bf16[4,2,16,2048]{3,2,0,1:T(8,128)(2,1)S(1)} %maximum_select_fusion.2), channel_id=1, source_target_pairs={{0,1},{1,0},{2,3},{3,2},{4,5},{5,4},{6,7},{7,6},{8,9},{9,8},{10,11... | collective-permute-start | bytes 1572872 | tf_op jit(solution)/shard_map/ppermute | solution.py:18
  49.0 1.4 copy-start.11
  49.1 2.1 %copy-start.19 = (bf16[256,384]{1,0:T(8,128)(2,1)S(1)}, bf16[256,384]{1,0:T(8,128)(2,1)}, u32[]{:S(2)}) copy-start(bf16[256,384]{1,0:T(8,128)(2,1)} %param.11) | copy-start | bytes 589828
  53.4 0.8 copy-start.7
  53.4 0.9 copy-start.9
  53.4 1.1 copy-start.10
  53.4 1.2 copy-start.5
  55.4 1.0 copy-start.12
  57.2 8.8 %collective-permute-start.5 = (bf16[4,2,16,2048]{3,2,1,0:T(8,128)(2,1)}, bf16[4,2,16,2048]{3,2,1,0:T(8,128)(2,1)}, u32[]{:S(2)}, u32[]{:S(2)}) collective-permute-start(bf16[4,2,16,2048]{3,2,1,0:T(8,128)(2,1)} %dynamic-slice_bitcast_fusion), channel_id=1, source_target_pairs={{0,1},{1,0},{2,3},{3,2},{4,5},{5,4},{6,7},{7,6},{8,9},{9,8},{10,11... | collective-permute-start | bytes 1572872 | tf_op jit(solution)/shard_map/ppermute | solution.py:18
  59.5 19.5 %collective-permute-start.7 = (bf16[2560,128]{1,0:T(8,128)(2,1)}, bf16[2560,128]{1,0:T(8,128)(2,1)S(1)}, u32[]{:S(2)}, u32[]{:S(2)}) collective-permute-start(bf16[2560,128]{1,0:T(8,128)(2,1)} %copy-done.10), channel_id=1, source_target_pairs={{0,128},{16,144},{32,160},{48,176},{64,192},{80,208},{96,224},{112... | collective-permute-start | bytes 1966088 | tf_op jit(solution)/shard_map/ppermute | solution.py:18
  62.6 18.0 %collective-permute-start.8 = (bf16[2560,128]{1,0:T(8,128)(2,1)}, bf16[2560,128]{1,0:T(8,128)(2,1)S(1)}, u32[]{:S(2)}, u32[]{:S(2)}) collective-permute-start(bf16[2560,128]{1,0:T(8,128)(2,1)} %copy-done.9), channel_id=1, source_target_pairs={{0,384},{16,400},{32,416},{48,432},{64,448},{80,464},{96,480},{112... | collective-permute-start | bytes 1966088 | tf_op jit(solution)/shard_map/ppermute | solution.py:18
  67.4 24.4 %collective-permute-start.6 = (bf16[2,2,16,2048]{3,2,1,0:T(8,128)(2,1)S(1)}, bf16[2,2,16,2048]{3,2,1,0:T(8,128)(2,1)S(1)}, u32[]{:S(2)}, u32[]{:S(2)}) collective-permute-start(bf16[2,2,16,2048]{3,2,1,0:T(8,128)(2,1)S(1)} %select_convert_fusion), channel_id=1, source_target_pairs={{0,4},{1,5},{2,6},{3,7},{4,0},{5,1},{6,2},{7,3},{8,12},{9,13},{10,... | collective-permute-start | bytes 786440 | tf_op jit(solution)/shard_map/ppermute | solution.py:18
  80.6 11.3 %copy-start.1 = (bf16[2560,128]{1,0:T(8,128)(2,1)}, bf16[2560,128]{1,0:T(8,128)(2,1)S(1)}, u32[]{:S(2)}) copy-start(bf16[2560,128]{1,0:T(8,128)(2,1)S(1)} %collective-permute-done.8.right_ref) | copy-start | bytes 1966084
  80.6 12.2 %collective-permute-start.9 = (bf16[1024,128]{1,0:T(8,128)(2,1)S(1)}, bf16[1024,128]{1,0:T(8,128)(2,1)S(1)}, u32[]{:S(2)}, u32[]{:S(2)}) collective-permute-start(bf16[1024,128]{1,0:T(8,128)(2,1)S(1)} %pad_maximum_fusion.2), channel_id=1, source_target_pairs={{0,1},{1,0},{2,3},{3,2},{4,5},{5,4},{6,7},{7,6},{8,9},{9,8},{10,11... | collective-permute-start | bytes 786440 | tf_op jit(solution)/shard_map/ppermute | solution.py:18
  84.5 18.5 %collective-permute-start.12 = (bf16[1280,128]{1,0:T(8,128)(2,1)}, bf16[1280,128]{1,0:T(8,128)(2,1)}, u32[]{:S(2)}, u32[]{:S(2)}) collective-permute-start(bf16[1280,128]{1,0:T(8,128)(2,1)} %slice.70), channel_id=1, source_target_pairs={{0,128},{16,144},{32,160},{48,176},{64,192},{80,208},{96,224},{112... | collective-permute-start | bytes 983048 | tf_op jit(solution)/shard_map/ppermute | solution.py:18
  88.4 14.7 %collective-permute-start.13 = (bf16[1280,128]{1,0:T(8,128)(2,1)}, bf16[1280,128]{1,0:T(8,128)(2,1)}, u32[]{:S(2)}, u32[]{:S(2)}) collective-permute-start(bf16[1280,128]{1,0:T(8,128)(2,1)} %slice.71), channel_id=1, source_target_pairs={{0,384},{16,400},{32,416},{48,432},{64,448},{80,464},{96,480},{112... | collective-permute-start | bytes 983048 | tf_op jit(solution)/shard_map/ppermute | solution.py:18
  91.9 0.9 copy-start.13
  92.8 0.7 copy-start.3
  95.1 15.0 %collective-permute-start.10 = (bf16[2,16,2048]{2,1,0:T(8,128)(2,1)}, bf16[2,16,2048]{2,1,0:T(8,128)(2,1)S(1)}, u32[]{:S(2)}, u32[]{:S(2)}) collective-permute-start(bf16[2,16,2048]{2,1,0:T(8,128)(2,1)} %shard_map.94), channel_id=1, source_target_pairs={{0,12},{1,13},{2,14},{3,15},{4,8},{5,9},{6,10},{7,11},{8,4},{9,5},... | collective-permute-start | bytes 393224 | tf_op jit(solution)/shard_map/ppermute | solution.py:18
  97.6 1.1 copy-start.2
  98.7 0.9 copy-start.4
  99.7 0.9 copy-start.6
  100.6 0.9 copy-start.8
  103.0 7.0 %copy-start.14 = (f32[2,2,16,2048]{3,2,1,0:T(8,128)S(1)}, f32[2,2,16,2048]{3,2,1,0:T(8,128)}, u32[]{:S(2)}) copy-start(f32[2,2,16,2048]{3,2,1,0:T(8,128)} %copy-done.13) | copy-start | bytes 1572868
  104.7 17.9 %collective-permute-start.17 = (bf16[256,384]{1,0:T(8,128)(2,1)S(1)}, bf16[256,384]{1,0:T(8,128)(2,1)S(1)}, u32[]{:S(2)}, u32[]{:S(2)}) collective-permute-start(bf16[256,384]{1,0:T(8,128)(2,1)S(1)} %get-tuple-element.19), channel_id=1, source_target_pairs={{0,16},{16,0},{32,48},{48,32},{64,80},{80,64},{96,112},{112,96},{1... | collective-permute-start | bytes 589832 | tf_op jit(solution)/shard_map/ppermute | solution.py:18
  106.7 19.1 %collective-permute-start.14 = (bf16[256,384]{1,0:T(8,128)(2,1)S(1)}, bf16[256,384]{1,0:T(8,128)(2,1)S(1)}, u32[]{:S(2)}, u32[]{:S(2)}) collective-permute-start(bf16[256,384]{1,0:T(8,128)(2,1)S(1)} %get-tuple-element.17), channel_id=1, source_target_pairs={{0,16},{16,0},{32,48},{48,32},{64,80},{80,64},{96,112},{112,96},{1... | collective-permute-start | bytes 589832 | tf_op jit(solution)/shard_map/ppermute | solution.py:18
  110.1 36.6 %collective-permute-start.11 = (bf16[16,2048]{1,0:T(8,128)(2,1)S(1)}, bf16[16,2048]{1,0:T(8,128)(2,1)S(1)}, u32[]{:S(2)}, u32[]{:S(2)}) collective-permute-start(bf16[16,2048]{1,0:T(8,128)(2,1)S(1)} %fusion.20), channel_id=1, source_target_pairs={{0,2},{1,3},{2,0},{3,1},{4,6},{5,7},{6,4},{7,5},{8,10},{9,11},{10,... | collective-permute-start | bytes 196616 | tf_op jit(solution)/shard_map/ppermute | solution.py:18
  122.7 26.1 %copy-start.15 = (bf16[16,2048]{1,0:T(8,128)(2,1)S(1)}, bf16[16,2048]{1,0:T(8,128)(2,1)}, u32[]{:S(2)}) copy-start(bf16[16,2048]{1,0:T(8,128)(2,1)} %param.6) | copy-start | bytes 196612
  122.7 26.1 %copy-start.17 = (bf16[2048]{0:T(1024)(128)(2,1)S(1)}, bf16[2048]{0:T(1024)(128)(2,1)}, u32[]{:S(2)}) copy-start(bf16[2048]{0:T(1024)(128)(2,1)} %param.8) | copy-start | bytes 12292
  122.8 14.6 %collective-permute-start.18 = (bf16[2,64,384]{2,1,0:T(8,128)(2,1)S(1)}, bf16[2,64,384]{2,1,0:T(8,128)(2,1)S(1)}, u32[]{:S(2)}, u32[]{:S(2)}) collective-permute-start(bf16[2,64,384]{2,1,0:T(8,128)(2,1)S(1)} %fusion.19), channel_id=1, source_target_pairs={{0,32},{16,48},{32,0},{48,16},{64,96},{80,112},{96,64},{112,80},{1... | collective-permute-start | bytes 294920 | tf_op jit(solution)/shard_map/ppermute | solution.py:18
  125.9 14.8 %collective-permute-start.15 = (bf16[2,64,384]{2,1,0:T(8,128)(2,1)S(1)}, bf16[2,64,384]{2,1,0:T(8,128)(2,1)S(1)}, u32[]{:S(2)}, u32[]{:S(2)}) collective-permute-start(bf16[2,64,384]{2,1,0:T(8,128)(2,1)S(1)} %fusion.18), channel_id=1, source_target_pairs={{0,32},{16,48},{32,0},{48,16},{64,96},{80,112},{96,64},{112,80},{1... | collective-permute-start | bytes 294920 | tf_op jit(solution)/shard_map/ppermute | solution.py:18
  137.4 14.1 %collective-permute-start.19 = (bf16[64,384]{1,0:T(8,128)(2,1)S(1)}, bf16[64,384]{1,0:T(8,128)(2,1)S(1)}, u32[]{:S(2)}, u32[]{:S(2)}) collective-permute-start(bf16[64,384]{1,0:T(8,128)(2,1)S(1)} %fusion.22), channel_id=1, source_target_pairs={{0,64},{16,80},{32,96},{48,112},{64,0},{80,16},{96,32},{112,48},{1... | collective-permute-start | bytes 147464 | tf_op jit(solution)/shard_map/ppermute | solution.py:18
  140.7 6.0 %copy-start.16 = (bf16[64,384]{1,0:T(8,128)(2,1)}, bf16[64,384]{1,0:T(8,128)(2,1)S(1)}, u32[]{:S(2)}) copy-start(bf16[64,384]{1,0:T(8,128)(2,1)S(1)} %fusion.21.other_ref) | copy-start | bytes 147460
  140.7 11.4 %collective-permute-start.16 = (bf16[64,384]{1,0:T(8,128)(2,1)S(1)}, bf16[64,384]{1,0:T(8,128)(2,1)S(1)}, u32[]{:S(2)}, u32[]{:S(2)}) collective-permute-start(bf16[64,384]{1,0:T(8,128)(2,1)S(1)} %fusion.21.other_ref), channel_id=1, source_target_pairs={{0,64},{16,80},{32,96},{48,112},{64,0},{80,16},{96,32},{112,48},{1... | collective-permute-start | bytes 147464 | tf_op jit(solution)/shard_map/ppermute | solution.py:18
  146.7 0.6 copy-start.18

commit v3 on v1

v3 whole, which is shorter than its diff:
```python
import jax
import jax.numpy as jnp
from jax import lax
from jax.experimental import pallas as pl
from jax.experimental.pallas import tpu as pltpu
from jax.sharding import PartitionSpec as P

NX, NZ = 4, 8
NY, NH, NC = 4, 2, 2
F32, BF16 = jnp.float32, jnp.bfloat16


def pick(array, index, axis):
    return lax.dynamic_index_in_dim(array, index, axis, keepdims=False)


def move(array, axis_name, count, target):
    return lax.ppermute(array, axis_name, [(i, target(i)) for i in range(count)])


def to_core(array):
    return move(array, "tensor", 16, lambda t: t ^ 1)


def to_y(array, target):
    return move(array, "tensor", 16, lambda t: 4 * target(t // 4) + t % 4)


def to_x(array, step):
    return move(array, "dp", 32, lambda d: (d + 8 * step) % 32)


def to_z(array, bit):
    return move(array, "dp", 32, lambda d: d ^ bit)


HIGH_PAIRS = [[t, t + 2] for t in range(16) if (t // 2) % 2 == 0]


def copy_kernel(array_ref, other_ref, out_ref):
    out_ref[...] = array_ref[...]


def after(array, other):
    return pl.pallas_call(
        copy_kernel,
        out_shape=jax.ShapeDtypeStruct(array.shape, array.dtype),
        in_specs=[pl.BlockSpec(memory_space=pltpu.VMEM), pl.BlockSpec(memory_space=pl.ANY)],
        out_specs=pl.BlockSpec(memory_space=pltpu.VMEM),
        compiler_params=pltpu.CompilerParams(vmem_limit_bytes=2 * 2**20),
    )(array, other)


def two_of_y(block, y):
    other = to_y(block, lambda i: 3 - i)
    return jnp.where(y < 2, jnp.stack([block, other]), jnp.stack([other, block]))


def all_of_y(two, y):
    other = to_y(two, lambda i: i ^ 1)
    outer = (y == 0) | (y == 3)
    ends, middle = jnp.where(outer, two, other), jnp.where(outer, other, two)
    return jnp.stack([ends[0], middle[0], middle[1], ends[1]])


def gather_rows(normed, y, high, core):
    rows, depth = normed.shape
    pair = lax.all_gather(normed, "tensor", axis=0, axis_index_groups=HIGH_PAIRS)
    two = two_of_y(normed, y)
    near = all_of_y(two, y)
    away = all_of_y(two_of_y(after(pick(pair, 1 - high, 0), near), y), y)
    quad = jnp.where(high == 0, jnp.stack([near, away], axis=1), jnp.stack([away, near], axis=1))
    far = to_core(quad)
    both = jnp.where(core == 0, jnp.stack([quad, far], axis=2), jnp.stack([far, quad], axis=2))
    return both.reshape(16 * rows, depth)


def scatter_rows(share, late, y, core):
    rows = share.shape[0] // 16
    share = share.reshape(NY, NH, NC, rows, -1)
    got = to_core(pick(share, 1 - core, 2))
    total = pick(share, core, 2).astype(F32) + got.astype(F32)
    outer = (y == 0) | (y == 3)
    ends, middle = jnp.stack([total[0], total[3]]), total[1:3]
    got = to_y(jnp.where(outer, middle, ends).astype(BF16), lambda i: i ^ 1)
    total = jnp.where(outer, ends, middle) + got.astype(F32)
    got = to_y(jnp.where(y < 2, total[1], total[0]).astype(BF16), lambda i: 3 - i)
    total = jnp.where(y < 2, total[0], total[1]) + got.astype(F32)
    total = lax.psum_scatter(total.astype(BF16), "tensor", axis_index_groups=HIGH_PAIRS)
    return after(total, late).astype(F32)


def scatter_x(parts, x):
    width = parts.shape[1] // 2
    parts = parts.reshape(NX, -1, 2 * width)
    across, right, left = (pick(parts, (x + step) % NX, 0) for step in (2, 1, 3))
    gate_far = to_x(across[:, :width], 1)
    up_far = to_x(across[:, width:], -1)
    gate_right = to_x((right[:, :width].astype(F32) + gate_far.astype(F32)).astype(BF16), 1)
    up_left = to_x((left[:, width:].astype(F32) + up_far.astype(F32)).astype(BF16), -1)
    up_right = to_x(right[:, width:], 1)
    gate_left = to_x(left[:, :width], -1)
    own = pick(parts, x, 0).astype(F32)
    gate = own[:, :width] + gate_left.astype(F32) + gate_right.astype(F32)
    gate, up_left = lax.optimization_barrier((gate, up_left))
    up = own[:, width:] + up_right.astype(F32) + up_left.astype(F32)
    return gate, up


def scatter_z(total, z):
    total = total.reshape(2, 2, 2, total.shape[0] // NZ, -1)
    bits = ((z // 4) % 2, (z // 2) % 2, z % 2)
    for axis, bit in ((2, 1), (1, 2), (0, 4)):
        sent = pick(total, 1 - bits[axis], axis).astype(BF16)
        total = pick(total, bits[axis], axis) + to_z(sent, bit).astype(F32)
    return total, sent


def shards(tokens, masked, mask_vector, gate_weight, up_weight, cotangent):
    dp = lax.axis_index("dp")
    tensor = lax.axis_index("tensor")
    x, z = dp // NZ, dp % NZ
    y, high, core = tensor // 4, (tensor // 2) % 2, tensor % 2
    flag = masked[:, None] == 1
    mixed_in = jnp.where(flag, mask_vector[None, :], tokens)
    mixed_f = mixed_in.astype(F32)
    inverse = lax.rsqrt(jnp.mean(mixed_f * mixed_f, axis=-1, keepdims=True) + 1e-06)
    normed_full = mixed_f * inverse
    gathered = gather_rows(normed_full.astype(BF16), y, high, core)
    gate = jnp.dot(gathered, gate_weight, preferred_element_type=F32)
    up = jnp.dot(gathered, up_weight, preferred_element_type=F32)
    sig = jax.nn.sigmoid(gate)
    hidden = (gate * sig * up).astype(BF16)
    cot = cotangent.astype(F32)
    up_delta = (cot * gate * sig).astype(BF16)
    gate_delta = (cot * up * sig * (1.0 + gate * (1.0 - sig))).astype(BF16)
    contract_last = (((1,), (1,)), ((), ()))
    contract_first = (((0,), (0,)), ((), ()))
    deltas = jnp.concatenate([gate_delta, up_delta], axis=1)
    parts = lax.dot_general(gathered, deltas, contract_first, preferred_element_type=F32)
    gate_grad, up_grad = scatter_x(parts.astype(BF16), x)
    gate_grad, _ = scatter_z(gate_grad, z)
    up_grad, late = scatter_z(up_grad, z)
    first = lax.dot_general(gate_delta, gate_weight, contract_last, preferred_element_type=F32)
    second = lax.dot_general(up_delta, up_weight, contract_last, preferred_element_type=F32)
    normed_grad = scatter_rows((first + second).astype(BF16), late, y, core)
    inner = jnp.mean(normed_grad * normed_full, axis=-1, keepdims=True)
    token_grad = jnp.where(flag, 0.0, inverse * (normed_grad - normed_full * inner)).astype(BF16)
    return (hidden, token_grad, gate_grad, up_grad)


def solution(mesh):
    return jax.shard_map(
        shards,
        mesh=mesh,
        in_specs=(
            P(("dp", "tensor"), None),
            P(("dp", "tensor")),
            P(),
            P(None, "tensor"),
            P(None, "tensor"),
            P("dp", "tensor"),
        ),
        out_specs=(
            P("dp", "tensor"),
            P(("dp", "tensor"), None),
            P("dp", "tensor"),
            P("dp", "tensor"),
        ),
        check_vma=False,
    )
```

time: 141 us -> 161 us (1.14)
  starting transfers between devices: 97 us -> 71.4 us
  blocking collectives: 0 us -> 16 us
  waiting for transfers between devices: 25.7 us -> 39.8 us
  between operations: 1.66 us -> 14.9 us
  local copies, waits for them, and re-layouts: 1.59 us -> 4.04 us
    ppermute x24 -> x20, starting transfers between devices: 97 us -> 71.4 us  [move(): lax.ppermute(array, axis_name, [(i, target(i)) for i in range(count)])]
    all_gather x0 -> x1, blocking collectives: none -> 16 us  [gather_rows(): lax.all_gather(normed, 'tensor', axis=0, axis_index_groups=HIGH_PAIRS)]
    ppermute x24 -> x20, waiting for transfers between devices: 25.7 us -> 39.8 us  [move(): lax.ppermute(array, axis_name, [(i, target(i)) for i in range(count)])]
    unnamed x15 -> x12, local copies, waits for them, and re-layouts: 0.26 us -> 2.15 us
  transfers between devices with their start and end apart: 24 -> 21, of which waited for: 8 -> 9; matrix products, arithmetic and copies ran while one was open for 4% -> 4% of each run, Pallas kernels for 0% -> 0%
where the time goes in v3:
time: 161 us; the launch traced here: 159 us
  starting transfers between devices  71.4 us (44%)
  waiting for transfers between devices  39.8 us (25%)
  blocking collectives  16 us (10%)
  between operations  14.9 us (9%)
  other arithmetic  8.31 us (5%)
  matrix products  4.81 us (3%)
  local copies, waits for them, and re-layouts  4.04 us (3%)
    ppermute x20, starting transfers between devices, move(): lax.ppermute(array, axis_name, [(i, target(i)) for i in range(count)])  71.4 us
    ppermute x20, waiting for transfers between devices, move(): lax.ppermute(array, axis_name, [(i, target(i)) for i in range(count)])  39.8 us
    all_gather x1, blocking collectives, gather_rows(): lax.all_gather(normed, 'tensor', axis=0, axis_index_groups=HIGH_PAIRS)  16 us
  transfers between devices with their start and end apart: 21, of which 9 were waited for; matrix products, arithmetic and copies ran while one was open for 4% of the time, Pallas kernels for 0%

profile of v3, /device:TPU:1, one launch (start us, length us, event | category | flops | bytes accessed | tf_op | source)
XLA Modules:
  0.0 159.2 jit_solution(5757865474297784785)
XLA Ops:
  7.2 0.0 reduce-scatter.2.cloned.1.call-start
  7.2 0.8 broadcast_compare_fusion
  8.0 1.0 fusion.16
  9.0 0.9 fusion.15
  10.0 5.5 %collective-permute-start = (bf16[16,2048]{1,0:T(8,128)(2,1)S(1)}, bf16[16,2048]{1,0:T(8,128)(2,1)S(1)}, u32[]{:S(2)}, u32[]{:S(2)}) collective-permute-start(bf16[16,2048]{1,0:T(8,128)(2,1)S(1)} %fusion.15), channel_id=1, source_target_pairs={{0,12},{1,13},{2,14},{3,15},{4,8},{5,9},{6,10},{7,11},{8,4},{9,5},... | collective-permute-start | bytes 196616 | tf_op jit(solution)/shard_map/ppermute | solution.py:18
  15.5 0.9 fusion.46
  16.4 16.0 %all-gather = bf16[32,2048]{1,0:T(8,128)(2,1)S(1)} all-gather(bf16[16,2048]{1,0:T(8,128)(2,1)S(1)} %fusion.15), channel_id=2, replica_groups={{0,2},{1,3},{4,6},{5,7},{8,10},{9,11},{12,14},{13,15},{16,18},{17,19},{..., dimensions={0}, use_global_device_ids=true | all-gather | bytes 196608 | tf_op jit(solution)/shard_map/all_gather | solution.py:68
  32.4 1.9 %collective-permute-start.1 = (bf16[2,16,2048]{2,1,0:T(8,128)(2,1)S(1)}, bf16[2,16,2048]{2,1,0:T(8,128)(2,1)S(1)}, u32[]{:S(2)}, u32[]{:S(2)}) collective-permute-start(bf16[2,16,2048]{2,1,0:T(8,128)(2,1)S(1)} %maximum_select_fusion.3), channel_id=1, source_target_pairs={{0,4},{1,5},{2,6},{3,7},{4,0},{5,1},{6,2},{7,3},{8,12},{9,13},{10,... | collective-permute-start | bytes 393224 | tf_op jit(solution)/shard_map/ppermute | solution.py:18
  34.4 3.8 %collective-permute-done.1 = bf16[2,16,2048]{2,1,0:T(8,128)(2,1)S(1)} collective-permute-done((bf16[2,16,2048]{2,1,0:T(8,128)(2,1)S(1)}, bf16[2,16,2048]{2,1,0:T(8,128)(2,1)S(1)}, u32[]{:S(2)}, u32[]{:S(2)}) %collective-permute-start.1) | collective-permute-done | bytes 131104 | tf_op jit(solution)/shard_map/ppermute | solution.py:18
  38.2 0.1 fusion.30
  38.3 4.0 %collective-permute-start.2 = (bf16[16,2048]{1,0:T(8,128)(2,1)S(1)}, bf16[16,2048]{1,0:T(8,128)(2,1)S(1)}, u32[]{:S(2)}, u32[]{:S(2)}) collective-permute-start(bf16[16,2048]{1,0:T(8,128)(2,1)S(1)} %shard_map.93), channel_id=1, source_target_pairs={{0,12},{1,13},{2,14},{3,15},{4,8},{5,9},{6,10},{7,11},{8,4},{9,5},... | collective-permute-start | bytes 196616 | tf_op jit(solution)/shard_map/ppermute | solution.py:18
  42.3 2.2 %collective-permute-done.2 = bf16[16,2048]{1,0:T(8,128)(2,1)S(1)} collective-permute-done((bf16[16,2048]{1,0:T(8,128)(2,1)S(1)}, bf16[16,2048]{1,0:T(8,128)(2,1)S(1)}, u32[]{:S(2)}, u32[]{:S(2)}) %collective-permute-start.2) | collective-permute-done | bytes 65568 | tf_op jit(solution)/shard_map/ppermute | solution.py:18
  44.5 1.9 %collective-permute-start.3 = (bf16[2,16,2048]{2,1,0:T(8,128)(2,1)S(1)}, bf16[2,16,2048]{2,1,0:T(8,128)(2,1)S(1)}, u32[]{:S(2)}, u32[]{:S(2)}) collective-permute-start(bf16[2,16,2048]{2,1,0:T(8,128)(2,1)S(1)} %maximum_select_fusion.4), channel_id=1, source_target_pairs={{0,4},{1,5},{2,6},{3,7},{4,0},{5,1},{6,2},{7,3},{8,12},{9,13},{10,... | collective-permute-start | bytes 393224 | tf_op jit(solution)/shard_map/ppermute | solution.py:18
  46.5 3.8 %collective-permute-done.3 = bf16[2,16,2048]{2,1,0:T(8,128)(2,1)S(1)} collective-permute-done((bf16[2,16,2048]{2,1,0:T(8,128)(2,1)S(1)}, bf16[2,16,2048]{2,1,0:T(8,128)(2,1)S(1)}, u32[]{:S(2)}, u32[]{:S(2)}) %collective-permute-start.3) | collective-permute-done | bytes 131104 | tf_op jit(solution)/shard_map/ppermute | solution.py:18
  50.3 0.1 maximum_select_fusion.2
  50.4 8.8 %collective-permute-start.4 = (bf16[4,2,16,2048]{3,2,0,1:T(8,128)(2,1)S(1)}, bf16[4,2,16,2048]{3,2,0,1:T(8,128)(2,1)S(1)}, u32[]{:S(2)}, u32[]{:S(2)}) collective-permute-start(bf16[4,2,16,2048]{3,2,0,1:T(8,128)(2,1)S(1)} %maximum_select_fusion.2), channel_id=1, source_target_pairs={{0,1},{1,0},{2,3},{3,2},{4,5},{5,4},{6,7},{7,6},{8,9},{9,8},{10,11... | collective-permute-start | bytes 1572872 | tf_op jit(solution)/shard_map/ppermute | solution.py:18
  59.4 0.1 maximum_select_fusion.1
  59.5 1.2 collective-permute-done.4
  60.8 0.2 maximum_select_fusion
  60.9 0.1 copy.10
  61.1 1.3 copy-done.2
  62.3 0.7 fusion.35
  63.1 1.5 fusion.5
  64.6 0.8 fusion.36
  65.4 0.8 fusion
  66.2 2.3 %collective-permute-start.5 = (bf16[4,2,16,2048]{3,2,1,0:T(8,128)(2,1)S(1)}, bf16[4,2,16,2048]{3,2,1,0:T(8,128)(2,1)S(1)}, u32[]{:S(2)}, u32[]{:S(2)}) collective-permute-start(bf16[4,2,16,2048]{3,2,1,0:T(8,128)(2,1)S(1)} %dynamic-slice_bitcast_fusion.3), channel_id=1, source_target_pairs={{0,1},{1,0},{2,3},{3,2},{4,5},{5,4},{6,7},{7,6},{8,9},{9,8},{10,11... | collective-permute-start | bytes 1572872 | tf_op jit(solution)/shard_map/ppermute | solution.py:18
  68.5 1.0 convolution_convert_fusion
  69.5 0.3 dynamic-slice_bitcast_fusion.1
  69.8 0.1 fusion.32
  69.9 3.1 %collective-permute-start.10 = (bf16[512,384]{1,0:T(8,128)(2,1)S(1)}, bf16[512,384]{1,0:T(8,128)(2,1)S(1)}, u32[]{:S(2)}, u32[]{:S(2)}) collective-permute-start(bf16[512,384]{1,0:T(8,128)(2,1)S(1)} %get-tuple-element.15), channel_id=1, source_target_pairs={{0,128},{16,144},{32,160},{48,176},{64,192},{80,208},{96,224},{112... | collective-permute-start | bytes 1179656 | tf_op jit(solution)/shard_map/ppermute | solution.py:18
  73.1 3.4 %collective-permute-start.9 = (bf16[512,384]{1,0:T(8,128)(2,1)S(1)}, bf16[512,384]{1,0:T(8,128)(2,1)S(1)}, u32[]{:S(2)}, u32[]{:S(2)}) collective-permute-start(bf16[512,384]{1,0:T(8,128)(2,1)S(1)} %slice.88), channel_id=1, source_target_pairs={{0,384},{16,400},{32,416},{48,432},{64,448},{80,464},{96,480},{112... | collective-permute-start | bytes 1179656 | tf_op jit(solution)/shard_map/ppermute | solution.py:18
  76.5 3.2 %collective-permute-start.12 = (bf16[512,384]{1,0:T(8,128)(2,1)S(1)}, bf16[512,384]{1,0:T(8,128)(2,1)S(1)}, u32[]{:S(2)}, u32[]{:S(2)}) collective-permute-start(bf16[512,384]{1,0:T(8,128)(2,1)S(1)} %get-tuple-element.14), channel_id=1, source_target_pairs={{0,384},{16,400},{32,416},{48,432},{64,448},{80,464},{96,480},{112... | collective-permute-start | bytes 1179656 | tf_op jit(solution)/shard_map/ppermute | solution.py:18
  79.7 2.1 %collective-permute-start.8 = (bf16[512,384]{1,0:T(8,128)(2,1)S(1)}, bf16[512,384]{1,0:T(8,128)(2,1)S(1)}, u32[]{:S(2)}, u32[]{:S(2)}) collective-permute-start(bf16[512,384]{1,0:T(8,128)(2,1)S(1)} %slice.86), channel_id=1, source_target_pairs={{0,128},{16,144},{32,160},{48,176},{64,192},{80,208},{96,224},{112... | collective-permute-start | bytes 1179656 | tf_op jit(solution)/shard_map/ppermute | solution.py:18
  81.8 0.1 convert_add_fusion
  82.0 0.1 select_convert_fusion
  82.1 1.9 %collective-permute-start.6 = (bf16[2,2,16,2048]{3,2,1,0:T(8,128)(2,1)S(1)}, bf16[2,2,16,2048]{3,2,1,0:T(8,128)(2,1)S(1)}, u32[]{:S(2)}, u32[]{:S(2)}) collective-permute-start(bf16[2,2,16,2048]{3,2,1,0:T(8,128)(2,1)S(1)} %select_convert_fusion), channel_id=1, source_target_pairs={{0,4},{1,5},{2,6},{3,7},{4,0},{5,1},{6,2},{7,3},{8,12},{9,13},{10,... | collective-permute-start | bytes 786440 | tf_op jit(solution)/shard_map/ppermute | solution.py:18
  84.0 0.1 add_convert_fusion.1
  84.1 1.9 %collective-permute-start.11 = (bf16[512,384]{1,0:T(8,128)(2,1)S(1)}, bf16[512,384]{1,0:T(8,128)(2,1)S(1)}, u32[]{:S(2)}, u32[]{:S(2)}) collective-permute-start(bf16[512,384]{1,0:T(8,128)(2,1)S(1)} %add_convert_fusion.1), channel_id=1, source_target_pairs={{0,128},{16,144},{32,160},{48,176},{64,192},{80,208},{96,224},{112... | collective-permute-start | bytes 1179656 | tf_op jit(solution)/shard_map/ppermute | solution.py:18
  86.1 7.6 %collective-permute-done.12 = bf16[512,384]{1,0:T(8,128)(2,1)S(1)} collective-permute-done((bf16[512,384]{1,0:T(8,128)(2,1)S(1)}, bf16[512,384]{1,0:T(8,128)(2,1)S(1)}, u32[]{:S(2)}, u32[]{:S(2)}) %collective-permute-start.12) | collective-permute-done | bytes 393248 | tf_op jit(solution)/shard_map/ppermute | solution.py:18
  93.7 0.1 add_convert_fusion
  93.8 4.6 %collective-permute-start.13 = (bf16[512,384]{1,0:T(8,128)(2,1)S(1)}, bf16[512,384]{1,0:T(8,128)(2,1)S(1)}, u32[]{:S(2)}, u32[]{:S(2)}) collective-permute-start(bf16[512,384]{1,0:T(8,128)(2,1)S(1)} %add_convert_fusion), channel_id=1, source_target_pairs={{0,384},{16,400},{32,416},{48,432},{64,448},{80,464},{96,480},{112... | collective-permute-start | bytes 1179656 | tf_op jit(solution)/shard_map/ppermute | solution.py:18
  98.4 0.1 convert_add_fusion.1
  98.5 2.4 %collective-permute-start.7 = (bf16[2,16,2048]{2,1,0:T(8,128)(2,1)S(1)}, bf16[2,16,2048]{2,1,0:T(8,128)(2,1)S(1)}, u32[]{:S(2)}, u32[]{:S(2)}) collective-permute-start(bf16[2,16,2048]{2,1,0:T(8,128)(2,1)S(1)} %fusion.21), channel_id=1, source_target_pairs={{0,12},{1,13},{2,14},{3,15},{4,8},{5,9},{6,10},{7,11},{8,4},{9,5},... | collective-permute-start | bytes 393224 | tf_op jit(solution)/shard_map/ppermute | solution.py:18
  101.0 0.1 fusion.1
  101.1 4.4 %collective-permute-done.13 = bf16[512,384]{1,0:T(8,128)(2,1)S(1)} collective-permute-done((bf16[512,384]{1,0:T(8,128)(2,1)S(1)}, bf16[512,384]{1,0:T(8,128)(2,1)S(1)}, u32[]{:S(2)}, u32[]{:S(2)}) %collective-permute-start.13) | collective-permute-done | bytes 393248 | tf_op jit(solution)/shard_map/ppermute | solution.py:18
  105.5 0.1 fusion.2
  105.6 0.7 fusion.13
  106.3 2.1 %collective-permute-start.14 = (bf16[2,2,64,384]{3,2,0,1:T(8,128)(2,1)}, bf16[2,2,64,384]{3,2,0,1:T(8,128)(2,1)S(1)}, u32[]{:S(2)}, u32[]{:S(2)}) collective-permute-start(bf16[2,2,64,384]{3,2,0,1:T(8,128)(2,1)} %fusion.13), channel_id=1, source_target_pairs={{0,16},{16,0},{32,48},{48,32},{64,80},{80,64},{96,112},{112,96},{1... | collective-permute-start | bytes 589832 | tf_op jit(solution)/shard_map/ppermute | solution.py:18
  108.5 0.7 fusion.12
  109.2 3.1 %collective-permute-start.16 = (bf16[2,2,64,384]{3,2,1,0:T(8,128)(2,1)}, bf16[2,2,64,384]{3,2,1,0:T(8,128)(2,1)S(1)}, u32[]{:S(2)}, u32[]{:S(2)}) collective-permute-start(bf16[2,2,64,384]{3,2,1,0:T(8,128)(2,1)} %fusion.12), channel_id=1, source_target_pairs={{0,16},{16,0},{32,48},{48,32},{64,80},{80,64},{96,112},{112,96},{1... | collective-permute-start | bytes 589832 | tf_op jit(solution)/shard_map/ppermute | solution.py:18
  112.3 0.7 fusion.11
  113.0 0.0 reduce-scatter.2.cloned.1.call-update
  113.0 5.2 %collective-permute-done.16 = bf16[2,2,64,384]{3,2,1,0:T(8,128)(2,1)S(1)} collective-permute-done((bf16[2,2,64,384]{3,2,1,0:T(8,128)(2,1)}, bf16[2,2,64,384]{3,2,1,0:T(8,128)(2,1)S(1)}, u32[]{:S(2)}, u32[]{:S(2)}) %collective-permute-start.16) | collective-permute-done | bytes 196640 | tf_op jit(solution)/shard_map/ppermute | solution.py:18
  118.3 2.4 %collective-permute-start.17 = (bf16[2,64,384]{2,1,0:T(8,128)(2,1)S(1)}, bf16[2,64,384]{2,1,0:T(8,128)(2,1)S(1)}, u32[]{:S(2)}, u32[]{:S(2)}) collective-permute-start(bf16[2,64,384]{2,1,0:T(8,128)(2,1)S(1)} %fusion.25), channel_id=1, source_target_pairs={{0,32},{16,48},{32,0},{48,16},{64,96},{80,112},{96,64},{112,80},{1... | collective-permute-start | bytes 294920 | tf_op jit(solution)/shard_map/ppermute | solution.py:18
  120.8 3.7 %collective-permute-start.15 = (bf16[2,64,384]{2,1,0:T(8,128)(2,1)S(1)}, bf16[2,64,384]{2,1,0:T(8,128)(2,1)S(1)}, u32[]{:S(2)}, u32[]{:S(2)}) collective-permute-start(bf16[2,64,384]{2,1,0:T(8,128)(2,1)S(1)} %fusion.24), channel_id=1, source_target_pairs={{0,32},{16,48},{32,0},{48,16},{64,96},{80,112},{96,64},{112,80},{1... | collective-permute-start | bytes 294920 | tf_op jit(solution)/shard_map/ppermute | solution.py:18
  124.6 0.9 collective-permute-done.17
  125.5 6.7 %collective-permute-start.18 = (bf16[64,384]{1,0:T(8,128)(2,1)S(1)}, bf16[64,384]{1,0:T(8,128)(2,1)S(1)}, u32[]{:S(2)}, u32[]{:S(2)}) collective-permute-start(bf16[64,384]{1,0:T(8,128)(2,1)S(1)} %fusion.27), channel_id=1, source_target_pairs={{0,64},{16,80},{32,96},{48,112},{64,0},{80,16},{96,32},{112,48},{1... | collective-permute-start | bytes 147464 | tf_op jit(solution)/shard_map/ppermute | solution.py:18
  132.3 6.1 %collective-permute-start.19 = (bf16[64,384]{1,0:T(8,128)(2,1)S(1)}, bf16[64,384]{1,0:T(8,128)(2,1)S(1)}, u32[]{:S(2)}, u32[]{:S(2)}) collective-permute-start(bf16[64,384]{1,0:T(8,128)(2,1)S(1)} %fusion.26.other_ref), channel_id=1, source_target_pairs={{0,64},{16,80},{32,96},{48,112},{64,0},{80,16},{96,32},{112,48},{1... | collective-permute-start | bytes 147464 | tf_op jit(solution)/shard_map/ppermute | solution.py:18
  138.5 0.7 bitcast_add_fusion.6
  139.2 10.7 %collective-permute-done.19 = bf16[64,384]{1,0:T(8,128)(2,1)S(1)} collective-permute-done((bf16[64,384]{1,0:T(8,128)(2,1)S(1)}, bf16[64,384]{1,0:T(8,128)(2,1)S(1)}, u32[]{:S(2)}, u32[]{:S(2)}) %collective-permute-start.19) | collective-permute-done | bytes 49184 | tf_op jit(solution)/shard_map/ppermute | solution.py:18
  149.9 0.7 bitcast_add_fusion.5
  150.6 0.8 copy-done.1
  151.4 0.2 fusion.17
  151.6 0.7 fusion.20
  (47 shorter events, 0.6 us)
Async XLA Ops:
  7.2 55.9 %copy-start = (bf16[2048,384]{1,0:T(8,128)(2,1)S(1)}, bf16[2048,384]{1,0:T(8,128)(2,1)}, u32[]{:S(2)}) copy-start(bf16[2048,384]{1,0:T(8,128)(2,1)} %param.10) | copy-start | bytes 4718596
  7.2 143.4 %reduce-scatter.2.cloned.1.call-start = ((), (), s32[]{:S(2)}) async-start(), calls=%async_computation.1 | async-start | bytes 196608 | tf_op jit(solution)/shard_map/reduce_scatter | solution.py:89
  10.0 22.4 %collective-permute-start = (bf16[16,2048]{1,0:T(8,128)(2,1)S(1)}, bf16[16,2048]{1,0:T(8,128)(2,1)S(1)}, u32[]{:S(2)}, u32[]{:S(2)}) collective-permute-start(bf16[16,2048]{1,0:T(8,128)(2,1)S(1)} %fusion.15), channel_id=1, source_target_pairs={{0,12},{1,13},{2,14},{3,15},{4,8},{5,9},{6,10},{7,11},{8,4},{9,5},... | collective-permute-start | bytes 196616 | tf_op jit(solution)/shard_map/ppermute | solution.py:18
  32.4 5.7 %collective-permute-start.1 = (bf16[2,16,2048]{2,1,0:T(8,128)(2,1)S(1)}, bf16[2,16,2048]{2,1,0:T(8,128)(2,1)S(1)}, u32[]{:S(2)}, u32[]{:S(2)}) collective-permute-start(bf16[2,16,2048]{2,1,0:T(8,128)(2,1)S(1)} %maximum_select_fusion.3), channel_id=1, source_target_pairs={{0,4},{1,5},{2,6},{3,7},{4,0},{5,1},{6,2},{7,3},{8,12},{9,13},{10,... | collective-permute-start | bytes 393224 | tf_op jit(solution)/shard_map/ppermute | solution.py:18
  38.3 6.2 %collective-permute-start.2 = (bf16[16,2048]{1,0:T(8,128)(2,1)S(1)}, bf16[16,2048]{1,0:T(8,128)(2,1)S(1)}, u32[]{:S(2)}, u32[]{:S(2)}) collective-permute-start(bf16[16,2048]{1,0:T(8,128)(2,1)S(1)} %shard_map.93), channel_id=1, source_target_pairs={{0,12},{1,13},{2,14},{3,15},{4,8},{5,9},{6,10},{7,11},{8,4},{9,5},... | collective-permute-start | bytes 196616 | tf_op jit(solution)/shard_map/ppermute | solution.py:18
  44.5 5.7 %collective-permute-start.3 = (bf16[2,16,2048]{2,1,0:T(8,128)(2,1)S(1)}, bf16[2,16,2048]{2,1,0:T(8,128)(2,1)S(1)}, u32[]{:S(2)}, u32[]{:S(2)}) collective-permute-start(bf16[2,16,2048]{2,1,0:T(8,128)(2,1)S(1)} %maximum_select_fusion.4), channel_id=1, source_target_pairs={{0,4},{1,5},{2,6},{3,7},{4,0},{5,1},{6,2},{7,3},{8,12},{9,13},{10,... | collective-permute-start | bytes 393224 | tf_op jit(solution)/shard_map/ppermute | solution.py:18
  50.4 10.3 %collective-permute-start.4 = (bf16[4,2,16,2048]{3,2,0,1:T(8,128)(2,1)S(1)}, bf16[4,2,16,2048]{3,2,0,1:T(8,128)(2,1)S(1)}, u32[]{:S(2)}, u32[]{:S(2)}) collective-permute-start(bf16[4,2,16,2048]{3,2,0,1:T(8,128)(2,1)S(1)} %maximum_select_fusion.2), channel_id=1, source_target_pairs={{0,1},{1,0},{2,3},{3,2},{4,5},{5,4},{6,7},{7,6},{8,9},{9,8},{10,11... | collective-permute-start | bytes 1572872 | tf_op jit(solution)/shard_map/ppermute | solution.py:18
  60.9 1.4 copy-start.2
  61.1 2.0 %copy-start.5 = (bf16[256,384]{1,0:T(8,128)(2,1)S(1)}, bf16[256,384]{1,0:T(8,128)(2,1)}, u32[]{:S(2)}) copy-start(bf16[256,384]{1,0:T(8,128)(2,1)} %param.11) | copy-start | bytes 589828
  66.2 15.6 %collective-permute-start.5 = (bf16[4,2,16,2048]{3,2,1,0:T(8,128)(2,1)S(1)}, bf16[4,2,16,2048]{3,2,1,0:T(8,128)(2,1)S(1)}, u32[]{:S(2)}, u32[]{:S(2)}) collective-permute-start(bf16[4,2,16,2048]{3,2,1,0:T(8,128)(2,1)S(1)} %dynamic-slice_bitcast_fusion.3), channel_id=1, source_target_pairs={{0,1},{1,0},{2,3},{3,2},{4,5},{5,4},{6,7},{7,6},{8,9},{9,8},{10,11... | collective-permute-start | bytes 1572872 | tf_op jit(solution)/shard_map/ppermute | solution.py:18
  69.9 14.1 %collective-permute-start.10 = (bf16[512,384]{1,0:T(8,128)(2,1)S(1)}, bf16[512,384]{1,0:T(8,128)(2,1)S(1)}, u32[]{:S(2)}, u32[]{:S(2)}) collective-permute-start(bf16[512,384]{1,0:T(8,128)(2,1)S(1)} %get-tuple-element.15), channel_id=1, source_target_pairs={{0,128},{16,144},{32,160},{48,176},{64,192},{80,208},{96,224},{112... | collective-permute-start | bytes 1179656 | tf_op jit(solution)/shard_map/ppermute | solution.py:18
  73.1 27.9 %collective-permute-start.9 = (bf16[512,384]{1,0:T(8,128)(2,1)S(1)}, bf16[512,384]{1,0:T(8,128)(2,1)S(1)}, u32[]{:S(2)}, u32[]{:S(2)}) collective-permute-start(bf16[512,384]{1,0:T(8,128)(2,1)S(1)} %slice.88), channel_id=1, source_target_pairs={{0,384},{16,400},{32,416},{48,432},{64,448},{80,464},{96,480},{112... | collective-permute-start | bytes 1179656 | tf_op jit(solution)/shard_map/ppermute | solution.py:18
  76.5 17.2 %collective-permute-start.12 = (bf16[512,384]{1,0:T(8,128)(2,1)S(1)}, bf16[512,384]{1,0:T(8,128)(2,1)S(1)}, u32[]{:S(2)}, u32[]{:S(2)}) collective-permute-start(bf16[512,384]{1,0:T(8,128)(2,1)S(1)} %get-tuple-element.14), channel_id=1, source_target_pairs={{0,384},{16,400},{32,416},{48,432},{64,448},{80,464},{96,480},{112... | collective-permute-start | bytes 1179656 | tf_op jit(solution)/shard_map/ppermute | solution.py:18
  79.7 25.8 %collective-permute-start.8 = (bf16[512,384]{1,0:T(8,128)(2,1)S(1)}, bf16[512,384]{1,0:T(8,128)(2,1)S(1)}, u32[]{:S(2)}, u32[]{:S(2)}) collective-permute-start(bf16[512,384]{1,0:T(8,128)(2,1)S(1)} %slice.86), channel_id=1, source_target_pairs={{0,128},{16,144},{32,160},{48,176},{64,192},{80,208},{96,224},{112... | collective-permute-start | bytes 1179656 | tf_op jit(solution)/shard_map/ppermute | solution.py:18
  82.1 16.3 %collective-permute-start.6 = (bf16[2,2,16,2048]{3,2,1,0:T(8,128)(2,1)S(1)}, bf16[2,2,16,2048]{3,2,1,0:T(8,128)(2,1)S(1)}, u32[]{:S(2)}, u32[]{:S(2)}) collective-permute-start(bf16[2,2,16,2048]{3,2,1,0:T(8,128)(2,1)S(1)} %select_convert_fusion), channel_id=1, source_target_pairs={{0,4},{1,5},{2,6},{3,7},{4,0},{5,1},{6,2},{7,3},{8,12},{9,13},{10,... | collective-permute-start | bytes 786440 | tf_op jit(solution)/shard_map/ppermute | solution.py:18
  84.1 16.8 %collective-permute-start.11 = (bf16[512,384]{1,0:T(8,128)(2,1)S(1)}, bf16[512,384]{1,0:T(8,128)(2,1)S(1)}, u32[]{:S(2)}, u32[]{:S(2)}) collective-permute-start(bf16[512,384]{1,0:T(8,128)(2,1)S(1)} %add_convert_fusion.1), channel_id=1, source_target_pairs={{0,128},{16,144},{32,160},{48,176},{64,192},{80,208},{96,224},{112... | collective-permute-start | bytes 1179656 | tf_op jit(solution)/shard_map/ppermute | solution.py:18
  93.8 11.7 %collective-permute-start.13 = (bf16[512,384]{1,0:T(8,128)(2,1)S(1)}, bf16[512,384]{1,0:T(8,128)(2,1)S(1)}, u32[]{:S(2)}, u32[]{:S(2)}) collective-permute-start(bf16[512,384]{1,0:T(8,128)(2,1)S(1)} %add_convert_fusion), channel_id=1, source_target_pairs={{0,384},{16,400},{32,416},{48,432},{64,448},{80,464},{96,480},{112... | collective-permute-start | bytes 1179656 | tf_op jit(solution)/shard_map/ppermute | solution.py:18
  98.5 13.8 %collective-permute-start.7 = (bf16[2,16,2048]{2,1,0:T(8,128)(2,1)S(1)}, bf16[2,16,2048]{2,1,0:T(8,128)(2,1)S(1)}, u32[]{:S(2)}, u32[]{:S(2)}) collective-permute-start(bf16[2,16,2048]{2,1,0:T(8,128)(2,1)S(1)} %fusion.21), channel_id=1, source_target_pairs={{0,12},{1,13},{2,14},{3,15},{4,8},{5,9},{6,10},{7,11},{8,4},{9,5},... | collective-permute-start | bytes 393224 | tf_op jit(solution)/shard_map/ppermute | solution.py:18
  106.3 14.4 %collective-permute-start.14 = (bf16[2,2,64,384]{3,2,0,1:T(8,128)(2,1)}, bf16[2,2,64,384]{3,2,0,1:T(8,128)(2,1)S(1)}, u32[]{:S(2)}, u32[]{:S(2)}) collective-permute-start(bf16[2,2,64,384]{3,2,0,1:T(8,128)(2,1)} %fusion.13), channel_id=1, source_target_pairs={{0,16},{16,0},{32,48},{48,32},{64,80},{80,64},{96,112},{112,96},{1... | collective-permute-start | bytes 589832 | tf_op jit(solution)/shard_map/ppermute | solution.py:18
  109.2 9.0 %collective-permute-start.16 = (bf16[2,2,64,384]{3,2,1,0:T(8,128)(2,1)}, bf16[2,2,64,384]{3,2,1,0:T(8,128)(2,1)S(1)}, u32[]{:S(2)}, u32[]{:S(2)}) collective-permute-start(bf16[2,2,64,384]{3,2,1,0:T(8,128)(2,1)} %fusion.12), channel_id=1, source_target_pairs={{0,16},{16,0},{32,48},{48,32},{64,80},{80,64},{96,112},{112,96},{1... | collective-permute-start | bytes 589832 | tf_op jit(solution)/shard_map/ppermute | solution.py:18
  118.2 33.2 %copy-start.3 = (bf16[16,2048]{1,0:T(8,128)(2,1)S(1)}, bf16[16,2048]{1,0:T(8,128)(2,1)}, u32[]{:S(2)}) copy-start(bf16[16,2048]{1,0:T(8,128)(2,1)} %param.6) | copy-start | bytes 196612
  118.3 33.2 %copy-start.4 = (bf16[2048]{0:T(1024)(128)(2,1)S(1)}, bf16[2048]{0:T(1024)(128)(2,1)}, u32[]{:S(2)}) copy-start(bf16[2048]{0:T(1024)(128)(2,1)} %param.8) | copy-start | bytes 12292
  118.3 7.2 %collective-permute-start.17 = (bf16[2,64,384]{2,1,0:T(8,128)(2,1)S(1)}, bf16[2,64,384]{2,1,0:T(8,128)(2,1)S(1)}, u32[]{:S(2)}, u32[]{:S(2)}) collective-permute-start(bf16[2,64,384]{2,1,0:T(8,128)(2,1)S(1)} %fusion.25), channel_id=1, source_target_pairs={{0,32},{16,48},{32,0},{48,16},{64,96},{80,112},{96,64},{112,80},{1... | collective-permute-start | bytes 294920 | tf_op jit(solution)/shard_map/ppermute | solution.py:18
  120.8 11.4 %collective-permute-start.15 = (bf16[2,64,384]{2,1,0:T(8,128)(2,1)S(1)}, bf16[2,64,384]{2,1,0:T(8,128)(2,1)S(1)}, u32[]{:S(2)}, u32[]{:S(2)}) collective-permute-start(bf16[2,64,384]{2,1,0:T(8,128)(2,1)S(1)} %fusion.24), channel_id=1, source_target_pairs={{0,32},{16,48},{32,0},{48,16},{64,96},{80,112},{96,64},{112,80},{1... | collective-permute-start | bytes 294920 | tf_op jit(solution)/shard_map/ppermute | solution.py:18
  125.5 13.0 %collective-permute-start.18 = (bf16[64,384]{1,0:T(8,128)(2,1)S(1)}, bf16[64,384]{1,0:T(8,128)(2,1)S(1)}, u32[]{:S(2)}, u32[]{:S(2)}) collective-permute-start(bf16[64,384]{1,0:T(8,128)(2,1)S(1)} %fusion.27), channel_id=1, source_target_pairs={{0,64},{16,80},{32,96},{48,112},{64,0},{80,16},{96,32},{112,48},{1... | collective-permute-start | bytes 147464 | tf_op jit(solution)/shard_map/ppermute | solution.py:18
  132.3 17.6 %collective-permute-start.19 = (bf16[64,384]{1,0:T(8,128)(2,1)S(1)}, bf16[64,384]{1,0:T(8,128)(2,1)S(1)}, u32[]{:S(2)}, u32[]{:S(2)}) collective-permute-start(bf16[64,384]{1,0:T(8,128)(2,1)S(1)} %fusion.26.other_ref), channel_id=1, source_target_pairs={{0,64},{16,80},{32,96},{48,112},{64,0},{80,16},{96,32},{112,48},{1... | collective-permute-start | bytes 147464 | tf_op jit(solution)/shard_map/ppermute | solution.py:18
  150.6 0.8 copy-start.1
Sparse Core Ops, SparseCore 0:
  113.2 35.7 reduce-scatter.1

commit v4 on v1

--- a/solution.py
+++ b/solution.py
@@ -10,6 +10,20 @@
 
 def pick(array, index, axis):
     return lax.dynamic_index_in_dim(array, index, axis, keepdims=False)
+
+
+def choose(index, options):
+    out = options[-1]
+    for i in range(len(options) - 1):
+        out = jnp.where(index == i, options[i], out)
+    return out
+
+
+def wait(array, early):
+    rows, width = early.shape[0], array.shape[-1]
+    early = jnp.tile(early, (1, -(-width // early.shape[1])))[:, :width]
+    held = jnp.where(early == early, array.reshape(-1, rows, width), 0)
+    return held.reshape(array.shape)
 
 
 def move(array, axis_name, count, target):
@@ -29,7 +43,11 @@
 
 
 def to_x(array, step):
-    return move(array, "dp", 32, lambda d: (d + 8 * step) % 32)
+    def target(i):
+        d, t = i // 16, i % 16
+        return (d + 8 * (step if t % 2 == 0 else -step)) % 32 * 16 + t
+
+    return move(array, ("dp", "tensor"), 512, target)
 
 
 def to_z(array, bit):
@@ -41,8 +59,8 @@
     other = to_high(normed)
     pair = jnp.where(high == 0, jnp.stack([normed, other]), jnp.stack([other, normed]))
     got = [to_y(pair, step) for step in (1, 2, 3)]
-    ring = jnp.stack([pair, got[2], got[1], got[0]])
-    quad = lax.dynamic_slice_in_dim(jnp.concatenate([ring, ring]), (NY - y) % NY, NY, 0)
+    ring = [pair, got[2], got[1], got[0]]
+    quad = jnp.stack([choose(y, [ring[(i - j) % NY] for j in range(NY)]) for i in range(NY)])
     far = to_core(quad)
     both = jnp.where(core == 0, jnp.stack([quad, far], axis=2), jnp.stack([far, quad], axis=2))
     return both.reshape(16 * rows, depth)
@@ -58,33 +76,40 @@
     total = pick(total, y, 0)
     for part in got:
         total = total + part.astype(F32)
-    got = to_high(pick(total, 1 - high, 0).astype(BF16))
+    return total
+
+
+def scatter_high(total, late, high):
+    got = wait(to_high(pick(total, 1 - high, 0).astype(BF16)), late)
     return pick(total, high, 0) + got.astype(F32)
 
 
-def scatter_weight(part, x, z):
-    rows, width = part.shape
-    rows = rows // (NX * NZ)
-    part = part.reshape(NX, 2, NZ // 2, rows, width)
-    far = pick(part, (x + 2) % NX, 0)
-    from_left = to_x(far[0], 1)
-    from_right = to_x(far[1], -1)
-    right = pick(part, (x + 1) % NX, 0)
-    left = pick(part, (x + 3) % NX, 0)
-    low = (right[0].astype(F32) + from_left.astype(F32)).astype(BF16)
-    high = (left[1].astype(F32) + from_right.astype(F32)).astype(BF16)
-    from_left = to_x(jnp.stack([low, right[1]]), 1)
-    from_right = to_x(jnp.stack([left[0], high]), -1)
-    total = pick(part, x, 0).astype(F32) + from_left.astype(F32) + from_right.astype(F32)
-    total = total.reshape(2, 2, 2, rows, width)
-    bits = ((z // 4) % 2, (z // 2) % 2, z % 2)
-    for axis, bit in ((2, 1), (1, 2), (0, 4)):
-        got = to_z(pick(total, 1 - bits[axis], axis).astype(BF16), bit)
-        total = pick(total, bits[axis], axis) + got.astype(F32)
-    return total
+def scatter_x(gathered, deltas, x, core):
+    width = gathered.shape[1] // NX
+    quarters = [gathered[:, i * width : (i + 1) * width] for i in range(NX)]
+
+    def part(i):
+        rows = choose(i, quarters)
+        dims = (((0,), (0,)), ((), ()))
+        return lax.dot_general(rows, deltas, dims, preferred_element_type=F32).astype(BF16)
+
+    ahead = jnp.where(core == 0, 1, 3)
+    far = to_x(part((x + 2) % NX), 1)
+    joined = part((x + ahead) % NX).astype(F32) + far.astype(F32)
+    joined = joined.astype(BF16)
+    last = to_x(joined, 1)
+    near = to_x(wait(part((x + 4 - ahead) % NX), joined[:16]), -1)
+    return part(x).astype(F32) + near.astype(F32) + last.astype(F32)
+
+
+def scatter_z(total, z, bit, axis):
+    mine = (z // bit) % 2
+    sent = pick(total, 1 - mine, axis).astype(BF16)
+    return pick(total, mine, axis) + to_z(sent, bit).astype(F32)
 
 
 def shards(tokens, masked, mask_vector, gate_weight, up_weight, cotangent):
+    depth, width = gate_weight.shape
     dp = lax.axis_index("dp")
     tensor = lax.axis_index("tensor")
     x, z = dp // NZ, dp % NZ
@@ -103,14 +128,19 @@
     up_delta = (cot * gate * sig).astype(BF16)
     gate_delta = (cot * up * sig * (1.0 + gate * (1.0 - sig))).astype(BF16)
     contract_last = (((1,), (1,)), ((), ()))
-    contract_first = (((0,), (0,)), ((), ()))
-    first = lax.dot_general(gathered, gate_delta, contract_first, preferred_element_type=F32)
-    second = lax.dot_general(gathered, up_delta, contract_first, preferred_element_type=F32)
-    gate_grad = scatter_weight(first.astype(BF16), x, z)
-    up_grad = scatter_weight(second.astype(BF16), x, z)
+    deltas = jnp.concatenate([gate_delta, up_delta], axis=1)
     first = lax.dot_general(gate_delta, gate_weight, contract_last, preferred_element_type=F32)
     second = lax.dot_general(up_delta, up_weight, contract_last, preferred_element_type=F32)
-    normed_grad = scatter_rows((first + second).astype(BF16), y, high, core)
+    rows = scatter_rows((first + second).astype(BF16), y, high, core)
+    total = scatter_x(gathered, deltas, x, core)
+    normed_grad = scatter_high(rows, total[:16], high)
+    total = total.reshape(2, 2, 2, depth // (NX * NZ), 2 * width)
+    gate_grad = scatter_z(total[..., :width], z, 1, 2)
+    up_grad = scatter_z(total[..., width:], z, 1, 2)
+    gate_grad = scatter_z(gate_grad, z, 2, 1)
+    up_grad = scatter_z(up_grad, z, 2, 1)
+    gate_grad = scatter_z(gate_grad, z, 4, 0)
+    up_grad = scatter_z(up_grad, z, 4, 0)
     inner = jnp.mean(normed_grad * normed_full, axis=-1, keepdims=True)
     token_grad = jnp.where(flag, 0.0, inverse * (normed_grad - normed_full * inner)).astype(BF16)
     return (hidden, token_grad, gate_grad, up_grad)

time: 141 us -> 135 us (0.957)
  starting transfers between devices: 97 us -> 88.3 us
  matrix products: 5.28 us -> 8.99 us
  waiting for transfers between devices: 25.7 us -> 24 us
    ppermute x24 -> x19, starting transfers between devices: 97 us -> 88.3 us  [move(): lax.ppermute(array, axis_name, [(i, target(i)) for i in range(count)])]
    dot_general x2 -> x4, matrix products: 1.55 us -> 3.86 us  [part(): lax.dot_general(rows, deltas, dims, preferred_element_type=F32).astype(BF16)]
    ppermute x24 -> x19, waiting for transfers between devices: 25.7 us -> 24 us  [move(): lax.ppermute(array, axis_name, [(i, target(i)) for i in range(count)])]
    unnamed x15, local copies, waits for them, and re-layouts: 0.26 us -> 1.88 us
    dot_general x1, matrix products: 0.73 us -> 2.15 us  [shards(): gate = jnp.dot(gathered, gate_weight, preferred_element_type=F32)]
  transfers between devices with their start and end apart: 24 -> 19, of which waited for: 8 -> 10; matrix products, arithmetic and copies ran while one was open for 4% -> 6% of each run, Pallas kernels for 0% -> 0%
where the time goes in v4:
time: 135 us
  starting transfers between devices  88.3 us (65%)
  waiting for transfers between devices  24 us (18%)
  other arithmetic  9.29 us (7%)
  matrix products  8.99 us (7%)
  local copies, waits for them, and re-layouts  2.37 us (2%)
  between operations  1.52 us (1%)
    ppermute x19, starting transfers between devices, move(): lax.ppermute(array, axis_name, [(i, target(i)) for i in range(count)])  88.3 us
    ppermute x19, waiting for transfers between devices, move(): lax.ppermute(array, axis_name, [(i, target(i)) for i in range(count)])  24 us
    dot_general x4, matrix products, part(): lax.dot_general(rows, deltas, dims, preferred_element_type=F32).astype(BF16)  3.86 us
  transfers between devices with their start and end apart: 19, of which 10 were waited for; matrix products, arithmetic and copies ran while one was open for 6% of the time, Pallas kernels for 0%

profile of v4, /device:TPU:1, one launch (start us, length us, event | category | flops | bytes accessed | tf_op | source)
XLA Modules:
  0.0 134.5 jit_solution(12665121363149435704)
XLA Ops:
  0.6 0.0 copy-start
  0.6 0.8 broadcast_compare_fusion
  1.4 1.0 fusion.60
  2.5 0.9 fusion.54
  3.4 16.3 %collective-permute-start = (bf16[16,2048]{1,0:T(8,128)(2,1)S(1)}, bf16[16,2048]{1,0:T(8,128)(2,1)S(1)}, u32[]{:S(2)}, u32[]{:S(2)}) collective-permute-start(bf16[16,2048]{1,0:T(8,128)(2,1)S(1)} %fusion.54), channel_id=1, source_target_pairs={{0,2},{1,3},{2,0},{3,1},{4,6},{5,7},{6,4},{7,5},{8,10},{9,11},{10,... | collective-permute-start | bytes 196616 | tf_op jit(solution)/shard_map/ppermute | solution.py:30
  19.7 0.9 fusion.80
  20.7 0.9 collective-permute-done
  21.6 4.6 %collective-permute-start.3 = (bf16[2,16,2048]{2,1,0:T(8,128)(2,1)S(1)}, bf16[2,16,2048]{2,1,0:T(8,128)(2,1)S(1)}, u32[]{:S(2)}, u32[]{:S(2)}) collective-permute-start(bf16[2,16,2048]{2,1,0:T(8,128)(2,1)S(1)} %maximum_select_fusion.1), channel_id=1, source_target_pairs={{0,12},{1,13},{2,14},{3,15},{4,0},{5,1},{6,2},{7,3},{8,4},{9,5},{1... | collective-permute-start | bytes 393224 | tf_op jit(solution)/shard_map/ppermute | solution.py:30
  26.2 1.9 %collective-permute-start.2 = (bf16[2,16,2048]{2,1,0:T(8,128)(2,1)S(1)}, bf16[2,16,2048]{2,1,0:T(8,128)(2,1)S(1)}, u32[]{:S(2)}, u32[]{:S(2)}) collective-permute-start(bf16[2,16,2048]{2,1,0:T(8,128)(2,1)S(1)} %maximum_select_fusion.1), channel_id=1, source_target_pairs={{0,4},{1,5},{2,6},{3,7},{4,8},{5,9},{6,10},{7,11},{8,12},{9,13},{1... | collective-permute-start | bytes 393224 | tf_op jit(solution)/shard_map/ppermute | solution.py:30
  28.1 3.5 %collective-permute-start.1 = (bf16[2,16,2048]{2,1,0:T(8,128)(2,1)S(1)}, bf16[2,16,2048]{2,1,0:T(8,128)(2,1)S(1)}, u32[]{:S(2)}, u32[]{:S(2)}) collective-permute-start(bf16[2,16,2048]{2,1,0:T(8,128)(2,1)S(1)} %maximum_select_fusion.1), channel_id=1, source_target_pairs={{0,8},{1,9},{2,10},{3,11},{4,12},{5,13},{6,14},{7,15},{8,0},{9,1},... | collective-permute-start | bytes 393224 | tf_op jit(solution)/shard_map/ppermute | solution.py:30
  31.7 0.0 collective-permute-done.3
  31.7 1.4 %collective-permute-done.2 = bf16[2,16,2048]{2,1,0:T(8,128)(2,1)S(1)} collective-permute-done((bf16[2,16,2048]{2,1,0:T(8,128)(2,1)S(1)}, bf16[2,16,2048]{2,1,0:T(8,128)(2,1)S(1)}, u32[]{:S(2)}, u32[]{:S(2)}) %collective-permute-start.2) | collective-permute-done | bytes 131104 | tf_op jit(solution)/shard_map/ppermute | solution.py:30
  33.1 2.9 %collective-permute-done.1 = bf16[2,16,2048]{2,1,0:T(8,128)(2,1)S(1)} collective-permute-done((bf16[2,16,2048]{2,1,0:T(8,128)(2,1)S(1)}, bf16[2,16,2048]{2,1,0:T(8,128)(2,1)S(1)}, u32[]{:S(2)}, u32[]{:S(2)}) %collective-permute-start.1) | collective-permute-done | bytes 131104 | tf_op jit(solution)/shard_map/ppermute | solution.py:30
  36.0 0.1 select_bitcast_fusion.3
  36.1 0.1 fusion.67
  36.2 6.0 %collective-permute-start.4 = (bf16[4,2,16,2048]{3,2,1,0:T(8,128)(2,1)S(1)}, bf16[4,2,16,2048]{3,2,1,0:T(8,128)(2,1)S(1)}, u32[]{:S(2)}, u32[]{:S(2)}) collective-permute-start(bf16[4,2,16,2048]{3,2,1,0:T(8,128)(2,1)S(1)} %get-tuple-element.15), channel_id=1, source_target_pairs={{0,1},{1,0},{2,3},{3,2},{4,5},{5,4},{6,7},{7,6},{8,9},{9,8},{10,11... | collective-permute-start | bytes 1572872 | tf_op jit(solution)/shard_map/ppermute | solution.py:30
  42.2 1.5 %collective-permute-done.4 = bf16[4,2,16,2048]{3,2,1,0:T(8,128)(2,1)S(1)} collective-permute-done((bf16[4,2,16,2048]{3,2,1,0:T(8,128)(2,1)S(1)}, bf16[4,2,16,2048]{3,2,1,0:T(8,128)(2,1)S(1)}, u32[]{:S(2)}, u32[]{:S(2)}) %collective-permute-start.4) | collective-permute-done | bytes 524320 | tf_op jit(solution)/shard_map/ppermute | solution.py:30
  43.7 0.8 copy-done.4
  44.5 1.4 %maximum_select_fusion = bf16[4,2,2,16,2048]{4,3,2,1,0:T(8,128)(2,1)S(1)} fusion(bf16[4,2,1,16,2048]{4,3,2,1,0:T(8,128)(2,1)} %bitcast.95, bf16[4,2,1,16,2048]{4,3,2,1,0:T(8,128)(2,1)S(1)} %get-tuple-element.14, pred[]{:T(512)S(6)} %eq.87), kind=kLoop, calls=%fused_computation.9 | loop fusion | flops 1572864 | bytes 2097153 | tf_op jit(solution)/shard_map/jit(_where)/select_n | solution.py:65
  45.9 0.0 copy-start.6
  45.9 2.2 %fusion.70 = f32[256,384]{1,0:T(8,128)S(1)} fusion(bf16[256,2048]{1,0:T(8,128)(2,1)S(1)} %bitcast.83, bf16[2048,384]{1,0:T(8,128)(2,1)} %param.9), kind=kOutput, calls=%fused_computation.122 | convolution fusion | flops 402653184 | bytes 3014656 | tf_op jit(solution)/shard_map/dot_general | solution.py:123
  48.1 0.0 copy-start.1
  48.1 1.5 %fusion.3 = (bf16[256,384]{1,0:T(8,128)(2,1)S(1)}, bf16[256,384]{1,0:T(8,128)(2,1)}, bf16[256,384]{1,0:T(8,128)(2,1)S(1)}) fusion(bf16[256,384]{1,0:T(8,128)(2,1)S(1)} %copy-done.6, f32[256,384]{1,0:T(8,128)S(1)} %fusion.70, bf16[256,2048]{1,0:T(8,128)(2,1)S(1)} %bitcast.84, bf16[2048,384]{1,0:T(8,128)(2,1)S(1)} %copy-done), kind=kOutput, calls=%fused_computation.17 | convolution fusion | flops 404324352 | bytes 3801088 | tf_op jit(solution)/shard_map/dot_general | solution.py:124
  49.6 0.7 fusion.71
  50.3 0.7 fusion
  51.1 1.0 copy-done.2
  52.1 2.3 %collective-permute-start.5 = (bf16[4,2,16,2048]{3,2,1,0:T(8,128)(2,1)S(1)}, bf16[4,2,16,2048]{3,2,1,0:T(8,128)(2,1)}, u32[]{:S(2)}, u32[]{:S(2)}) collective-permute-start(bf16[4,2,16,2048]{3,2,1,0:T(8,128)(2,1)S(1)} %dynamic-slice_bitcast_fusion), channel_id=1, source_target_pairs={{0,1},{1,0},{2,3},{3,2},{4,5},{5,4},{6,7},{7,6},{8,9},{9,8},{10,11... | collective-permute-start | bytes 1572872 | tf_op jit(solution)/shard_map/ppermute | solution.py:30
  54.5 1.3 convolution_convert_fusion.1
  55.8 4.4 %collective-permute-start.9 = (bf16[512,768]{1,0:T(8,128)(2,1)}, bf16[512,768]{1,0:T(8,128)(2,1)}, u32[]{:S(2)}, u32[]{:S(2)}) collective-permute-start(bf16[512,768]{1,0:T(8,128)(2,1)} %convolution_convert_fusion.1), channel_id=1, source_target_pairs={{0,128},{1,385},{2,130},{3,387},{4,132},{5,389},{6,134},{7,391},{8... | collective-permute-start | bytes 2359304 | tf_op jit(solution)/shard_map/ppermute | solution.py:30
  60.5 1.4 %fusion.68 = (bf16[4,2,16,2048]{3,2,1,0:T(8,128)(2,1)S(1)}, f32[4,2,16,2048]{3,2,1,0:T(8,128)S(1)}) fusion(bf16[4,2,16,2048]{3,2,1,0:T(8,128)(2,1)} %collective-permute-done.5, bf16[4,2,2,16,2048]{4,3,2,1,0:T(8,128)(2,1)} %bitcast.91, s32[]{:T(128)S(6)} %select_n.327), kind=kLoop, calls=%fused_computation.120 | loop fusion | flops 1048576 | bytes 2621444 | tf_op jit(solution)/shard_map/convert_element_type | solution.py:74
  61.9 2.2 %collective-permute-start.6 = (bf16[2,16,2048]{2,1,0:T(8,128)(2,1)S(1)}, bf16[2,16,2048]{2,1,0:T(8,128)(2,1)S(1)}, u32[]{:S(2)}, u32[]{:S(2)}) collective-permute-start(bf16[2,16,2048]{2,1,0:T(8,128)(2,1)S(1)} %get-tuple-element.11), channel_id=1, source_target_pairs={{0,4},{1,5},{2,6},{3,7},{4,8},{5,9},{6,10},{7,11},{8,12},{9,13},{1... | collective-permute-start | bytes 393224 | tf_op jit(solution)/shard_map/ppermute | solution.py:30
  64.1 4.6 %collective-permute-start.8 = (bf16[2,16,2048]{2,1,0:T(8,128)(2,1)S(1)}, bf16[2,16,2048]{2,1,0:T(8,128)(2,1)S(1)}, u32[]{:S(2)}, u32[]{:S(2)}) collective-permute-start(bf16[2,16,2048]{2,1,0:T(8,128)(2,1)S(1)} %get-tuple-element.12), channel_id=1, source_target_pairs={{0,12},{1,13},{2,14},{3,15},{4,0},{5,1},{6,2},{7,3},{8,4},{9,5},{1... | collective-permute-start | bytes 393224 | tf_op jit(solution)/shard_map/ppermute | solution.py:30
  68.6 3.1 %collective-permute-start.7 = (bf16[2,16,2048]{2,1,0:T(8,128)(2,1)S(1)}, bf16[2,16,2048]{2,1,0:T(8,128)(2,1)S(1)}, u32[]{:S(2)}, u32[]{:S(2)}) collective-permute-start(bf16[2,16,2048]{2,1,0:T(8,128)(2,1)S(1)} %get-tuple-element.13), channel_id=1, source_target_pairs={{0,8},{1,9},{2,10},{3,11},{4,12},{5,13},{6,14},{7,15},{8,0},{9,1},... | collective-permute-start | bytes 393224 | tf_op jit(solution)/shard_map/ppermute | solution.py:30
  71.8 1.6 %add_convert_fusion = bf16[512,768]{1,0:T(8,128)(2,1)S(1)} fusion(bf16[512,768]{1,0:T(8,128)(2,1)} %collective-permute-done.9, pred[]{:T(512)S(6)} %eq.98, pred[]{:T(512)S(6)} %eq.97, pred[]{:T(512)S(6)} %eq.96, bf16[256,2048]{1,0:T(8,128)(2,1)S(1)} %bitcast.86, bf16[256,384]{1,0:T(8,128)(2,1)S(1)} %get-tuple-element.10, ...), kind=kOutput, calls=%fused_computation.3 | convolution fusion | flops 204472320 | bytes 3014659 | tf_op jit(solution)/shard_map/dot_general | solution.py:94
  73.4 2.7 %collective-permute-start.11 = (bf16[512,768]{1,0:T(8,128)(2,1)S(1)}, bf16[512,768]{1,0:T(8,128)(2,1)S(1)}, u32[]{:S(2)}, u32[]{:S(2)}) collective-permute-start(bf16[512,768]{1,0:T(8,128)(2,1)S(1)} %add_convert_fusion), channel_id=1, source_target_pairs={{0,128},{1,385},{2,130},{3,387},{4,132},{5,389},{6,134},{7,391},{8... | collective-permute-start | bytes 2359304 | tf_op jit(solution)/shard_map/ppermute | solution.py:30
  76.1 0.5 bitcast_select_fusion
  76.5 2.6 %collective-permute-start.10 = (bf16[512,768]{1,0:T(8,128)(2,1)S(1)}, bf16[512,768]{1,0:T(8,128)(2,1)S(1)}, u32[]{:S(2)}, u32[]{:S(2)}) collective-permute-start(bf16[512,768]{1,0:T(8,128)(2,1)S(1)} %bitcast_select_fusion), channel_id=1, source_target_pairs={{0,384},{1,129},{2,386},{3,131},{4,388},{5,133},{6,390},{7,135},{8... | collective-permute-start | bytes 2359304 | tf_op jit(solution)/shard_map/ppermute | solution.py:30
  79.1 0.5 convolution_convert_fusion.3
  79.6 0.0 collective-permute-done.8
  79.6 0.0 collective-permute-done.7
  79.6 0.1 fusion.9
  79.7 12.8 %collective-permute-start.12 = (bf16[16,2048]{1,0:T(8,128)(2,1)S(1)}, bf16[16,2048]{1,0:T(8,128)(2,1)S(1)}, u32[]{:S(2)}, u32[]{:S(2)}) collective-permute-start(bf16[16,2048]{1,0:T(8,128)(2,1)S(1)} %fusion.64), channel_id=1, source_target_pairs={{0,2},{1,3},{2,0},{3,1},{4,6},{5,7},{6,4},{7,5},{8,10},{9,11},{10,... | collective-permute-start | bytes 196616 | tf_op jit(solution)/shard_map/ppermute | solution.py:30
  92.5 3.6 %collective-permute-done.10 = bf16[512,768]{1,0:T(8,128)(2,1)S(1)} collective-permute-done((bf16[512,768]{1,0:T(8,128)(2,1)S(1)}, bf16[512,768]{1,0:T(8,128)(2,1)S(1)}, u32[]{:S(2)}, u32[]{:S(2)}) %collective-permute-start.10) | collective-permute-done | bytes 786464 | tf_op jit(solution)/shard_map/ppermute | solution.py:30
  96.1 0.3 convert_add_fusion
  96.5 0.0 copy-start.3
  96.5 0.0 copy-start.5
  96.5 0.2 fusion.69
  96.7 2.0 %collective-permute-start.13 = (bf16[2,2,64,384]{3,2,0,1:T(8,128)(2,1)S(1)}, bf16[2,2,64,384]{3,2,0,1:T(8,128)(2,1)S(1)}, u32[]{:S(2)}, u32[]{:S(2)}) collective-permute-start(bf16[2,2,64,384]{3,2,0,1:T(8,128)(2,1)S(1)} %fusion.34), channel_id=1, source_target_pairs={{0,16},{16,0},{32,48},{48,32},{64,80},{80,64},{96,112},{112,96},{1... | collective-permute-start | bytes 589832 | tf_op jit(solution)/shard_map/ppermute | solution.py:30
  98.7 3.3 %collective-permute-start.16 = (bf16[2,2,64,384]{3,2,0,1:T(8,128)(2,1)S(1)}, bf16[2,2,64,384]{3,2,0,1:T(8,128)(2,1)S(1)}, u32[]{:S(2)}, u32[]{:S(2)}) collective-permute-start(bf16[2,2,64,384]{3,2,0,1:T(8,128)(2,1)S(1)} %fusion.35), channel_id=1, source_target_pairs={{0,16},{16,0},{32,48},{48,32},{64,80},{80,64},{96,112},{112,96},{1... | collective-permute-start | bytes 589832 | tf_op jit(solution)/shard_map/ppermute | solution.py:30
  102.1 0.0 collective-permute-done.12
  102.1 0.2 fusion.55
  102.3 0.7 fusion.59
  103.1 0.1 constant_dynamic-slice_fusion.1
  103.1 2.3 %collective-permute-done.13 = bf16[2,2,64,384]{3,2,0,1:T(8,128)(2,1)S(1)} collective-permute-done((bf16[2,2,64,384]{3,2,0,1:T(8,128)(2,1)S(1)}, bf16[2,2,64,384]{3,2,0,1:T(8,128)(2,1)S(1)}, u32[]{:S(2)}, u32[]{:S(2)}) %collective-permute-start.13) | collective-permute-done | bytes 196640 | tf_op jit(solution)/shard_map/ppermute | solution.py:30
  105.5 2.6 %collective-permute-start.14 = (bf16[2,64,384]{2,1,0:T(8,128)(2,1)S(1)}, bf16[2,64,384]{2,1,0:T(8,128)(2,1)S(1)}, u32[]{:S(2)}, u32[]{:S(2)}) collective-permute-start(bf16[2,64,384]{2,1,0:T(8,128)(2,1)S(1)} %fusion.62), channel_id=1, source_target_pairs={{0,32},{16,48},{32,0},{48,16},{64,96},{80,112},{96,64},{112,80},{1... | collective-permute-start | bytes 294920 | tf_op jit(solution)/shard_map/ppermute | solution.py:30
  108.1 0.9 collective-permute-done.16
  109.1 2.9 %collective-permute-start.17 = (bf16[2,64,384]{2,1,0:T(8,128)(2,1)S(1)}, bf16[2,64,384]{2,1,0:T(8,128)(2,1)S(1)}, u32[]{:S(2)}, u32[]{:S(2)}) collective-permute-start(bf16[2,64,384]{2,1,0:T(8,128)(2,1)S(1)} %fusion.63), channel_id=1, source_target_pairs={{0,32},{16,48},{32,0},{48,16},{64,96},{80,112},{96,64},{112,80},{1... | collective-permute-start | bytes 294920 | tf_op jit(solution)/shard_map/ppermute | solution.py:30
  112.0 3.2 %collective-permute-done.14 = bf16[2,64,384]{2,1,0:T(8,128)(2,1)S(1)} collective-permute-done((bf16[2,64,384]{2,1,0:T(8,128)(2,1)S(1)}, bf16[2,64,384]{2,1,0:T(8,128)(2,1)S(1)}, u32[]{:S(2)}, u32[]{:S(2)}) %collective-permute-start.14) | collective-permute-done | bytes 98336 | tf_op jit(solution)/shard_map/ppermute | solution.py:30
  115.2 6.6 %collective-permute-start.15 = (bf16[64,384]{1,0:T(8,128)(2,1)S(1)}, bf16[64,384]{1,0:T(8,128)(2,1)S(1)}, u32[]{:S(2)}, u32[]{:S(2)}) collective-permute-start(bf16[64,384]{1,0:T(8,128)(2,1)S(1)} %fusion.65), channel_id=1, source_target_pairs={{0,64},{16,80},{32,96},{48,112},{64,0},{80,16},{96,32},{112,48},{1... | collective-permute-start | bytes 147464 | tf_op jit(solution)/shard_map/ppermute | solution.py:30
  121.9 4.0 %collective-permute-start.18 = (bf16[64,384]{1,0:T(8,128)(2,1)S(1)}, bf16[64,384]{1,0:T(8,128)(2,1)S(1)}, u32[]{:S(2)}, u32[]{:S(2)}) collective-permute-start(bf16[64,384]{1,0:T(8,128)(2,1)S(1)} %fusion.66), channel_id=1, source_target_pairs={{0,64},{16,80},{32,96},{48,112},{64,0},{80,16},{96,32},{112,48},{1... | collective-permute-start | bytes 147464 | tf_op jit(solution)/shard_map/ppermute | solution.py:30
  126.0 0.6 collective-permute-done.15
  126.5 0.7 bitcast_add_fusion.5
  127.2 6.7 %collective-permute-done.18 = bf16[64,384]{1,0:T(8,128)(2,1)S(1)} collective-permute-done((bf16[64,384]{1,0:T(8,128)(2,1)S(1)}, bf16[64,384]{1,0:T(8,128)(2,1)S(1)}, u32[]{:S(2)}, u32[]{:S(2)}) %collective-permute-start.18) | collective-permute-done | bytes 49184 | tf_op jit(solution)/shard_map/ppermute | solution.py:30
  133.9 0.7 bitcast_add_fusion.4
  (32 shorter events, 0.5 us)
Async XLA Ops:
  0.6 47.4 %copy-start = (bf16[2048,384]{1,0:T(8,128)(2,1)S(1)}, bf16[2048,384]{1,0:T(8,128)(2,1)}, u32[]{:S(2)}) copy-start(bf16[2048,384]{1,0:T(8,128)(2,1)} %param.10) | copy-start | bytes 4718596
  3.4 18.1 %collective-permute-start = (bf16[16,2048]{1,0:T(8,128)(2,1)S(1)}, bf16[16,2048]{1,0:T(8,128)(2,1)S(1)}, u32[]{:S(2)}, u32[]{:S(2)}) collective-permute-start(bf16[16,2048]{1,0:T(8,128)(2,1)S(1)} %fusion.54), channel_id=1, source_target_pairs={{0,2},{1,3},{2,0},{3,1},{4,6},{5,7},{6,4},{7,5},{8,10},{9,11},{10,... | collective-permute-start | bytes 196616 | tf_op jit(solution)/shard_map/ppermute | solution.py:30
  21.6 10.2 %collective-permute-start.3 = (bf16[2,16,2048]{2,1,0:T(8,128)(2,1)S(1)}, bf16[2,16,2048]{2,1,0:T(8,128)(2,1)S(1)}, u32[]{:S(2)}, u32[]{:S(2)}) collective-permute-start(bf16[2,16,2048]{2,1,0:T(8,128)(2,1)S(1)} %maximum_select_fusion.1), channel_id=1, source_target_pairs={{0,12},{1,13},{2,14},{3,15},{4,0},{5,1},{6,2},{7,3},{8,4},{9,5},{1... | collective-permute-start | bytes 393224 | tf_op jit(solution)/shard_map/ppermute | solution.py:30
  26.2 6.9 %collective-permute-start.2 = (bf16[2,16,2048]{2,1,0:T(8,128)(2,1)S(1)}, bf16[2,16,2048]{2,1,0:T(8,128)(2,1)S(1)}, u32[]{:S(2)}, u32[]{:S(2)}) collective-permute-start(bf16[2,16,2048]{2,1,0:T(8,128)(2,1)S(1)} %maximum_select_fusion.1), channel_id=1, source_target_pairs={{0,4},{1,5},{2,6},{3,7},{4,8},{5,9},{6,10},{7,11},{8,12},{9,13},{1... | collective-permute-start | bytes 393224 | tf_op jit(solution)/shard_map/ppermute | solution.py:30
  28.1 7.9 %collective-permute-start.1 = (bf16[2,16,2048]{2,1,0:T(8,128)(2,1)S(1)}, bf16[2,16,2048]{2,1,0:T(8,128)(2,1)S(1)}, u32[]{:S(2)}, u32[]{:S(2)}) collective-permute-start(bf16[2,16,2048]{2,1,0:T(8,128)(2,1)S(1)} %maximum_select_fusion.1), channel_id=1, source_target_pairs={{0,8},{1,9},{2,10},{3,11},{4,12},{5,13},{6,14},{7,15},{8,0},{9,1},... | collective-permute-start | bytes 393224 | tf_op jit(solution)/shard_map/ppermute | solution.py:30
  36.2 7.5 %collective-permute-start.4 = (bf16[4,2,16,2048]{3,2,1,0:T(8,128)(2,1)S(1)}, bf16[4,2,16,2048]{3,2,1,0:T(8,128)(2,1)S(1)}, u32[]{:S(2)}, u32[]{:S(2)}) collective-permute-start(bf16[4,2,16,2048]{3,2,1,0:T(8,128)(2,1)S(1)} %get-tuple-element.15), channel_id=1, source_target_pairs={{0,1},{1,0},{2,3},{3,2},{4,5},{5,4},{6,7},{7,6},{8,9},{9,8},{10,11... | collective-permute-start | bytes 1572872 | tf_op jit(solution)/shard_map/ppermute | solution.py:30
  43.7 0.8 copy-start.4
  45.9 2.2 %copy-start.6 = (bf16[256,384]{1,0:T(8,128)(2,1)S(1)}, bf16[256,384]{1,0:T(8,128)(2,1)}, u32[]{:S(2)}) copy-start(bf16[256,384]{1,0:T(8,128)(2,1)} %param.11) | copy-start | bytes 589828
  48.1 1.5 %copy-start.1 = (bf16[2048,384]{1,0:T(8,128)(2,1)S(1)}, bf16[2048,384]{1,0:T(8,128)(2,1)}, u32[]{:S(2)}) copy-start(bf16[2048,384]{1,0:T(8,128)(2,1)} %param.9) | copy-start | bytes 4718596
  51.1 1.0 copy-start.2
  52.1 8.3 %collective-permute-start.5 = (bf16[4,2,16,2048]{3,2,1,0:T(8,128)(2,1)S(1)}, bf16[4,2,16,2048]{3,2,1,0:T(8,128)(2,1)}, u32[]{:S(2)}, u32[]{:S(2)}) collective-permute-start(bf16[4,2,16,2048]{3,2,1,0:T(8,128)(2,1)S(1)} %dynamic-slice_bitcast_fusion), channel_id=1, source_target_pairs={{0,1},{1,0},{2,3},{3,2},{4,5},{5,4},{6,7},{7,6},{8,9},{9,8},{10,11... | collective-permute-start | bytes 1572872 | tf_op jit(solution)/shard_map/ppermute | solution.py:30
  55.8 15.9 %collective-permute-start.9 = (bf16[512,768]{1,0:T(8,128)(2,1)}, bf16[512,768]{1,0:T(8,128)(2,1)}, u32[]{:S(2)}, u32[]{:S(2)}) collective-permute-start(bf16[512,768]{1,0:T(8,128)(2,1)} %convolution_convert_fusion.1), channel_id=1, source_target_pairs={{0,128},{1,385},{2,130},{3,387},{4,132},{5,389},{6,134},{7,391},{8... | collective-permute-start | bytes 2359304 | tf_op jit(solution)/shard_map/ppermute | solution.py:30
  61.9 17.8 %collective-permute-start.6 = (bf16[2,16,2048]{2,1,0:T(8,128)(2,1)S(1)}, bf16[2,16,2048]{2,1,0:T(8,128)(2,1)S(1)}, u32[]{:S(2)}, u32[]{:S(2)}) collective-permute-start(bf16[2,16,2048]{2,1,0:T(8,128)(2,1)S(1)} %get-tuple-element.11), channel_id=1, source_target_pairs={{0,4},{1,5},{2,6},{3,7},{4,8},{5,9},{6,10},{7,11},{8,12},{9,13},{1... | collective-permute-start | bytes 393224 | tf_op jit(solution)/shard_map/ppermute | solution.py:30
  64.1 15.6 %collective-permute-start.8 = (bf16[2,16,2048]{2,1,0:T(8,128)(2,1)S(1)}, bf16[2,16,2048]{2,1,0:T(8,128)(2,1)S(1)}, u32[]{:S(2)}, u32[]{:S(2)}) collective-permute-start(bf16[2,16,2048]{2,1,0:T(8,128)(2,1)S(1)} %get-tuple-element.12), channel_id=1, source_target_pairs={{0,12},{1,13},{2,14},{3,15},{4,0},{5,1},{6,2},{7,3},{8,4},{9,5},{1... | collective-permute-start | bytes 393224 | tf_op jit(solution)/shard_map/ppermute | solution.py:30
  68.6 11.0 %collective-permute-start.7 = (bf16[2,16,2048]{2,1,0:T(8,128)(2,1)S(1)}, bf16[2,16,2048]{2,1,0:T(8,128)(2,1)S(1)}, u32[]{:S(2)}, u32[]{:S(2)}) collective-permute-start(bf16[2,16,2048]{2,1,0:T(8,128)(2,1)S(1)} %get-tuple-element.13), channel_id=1, source_target_pairs={{0,8},{1,9},{2,10},{3,11},{4,12},{5,13},{6,14},{7,15},{8,0},{9,1},... | collective-permute-start | bytes 393224 | tf_op jit(solution)/shard_map/ppermute | solution.py:30
  73.4 22.8 %collective-permute-start.11 = (bf16[512,768]{1,0:T(8,128)(2,1)S(1)}, bf16[512,768]{1,0:T(8,128)(2,1)S(1)}, u32[]{:S(2)}, u32[]{:S(2)}) collective-permute-start(bf16[512,768]{1,0:T(8,128)(2,1)S(1)} %add_convert_fusion), channel_id=1, source_target_pairs={{0,128},{1,385},{2,130},{3,387},{4,132},{5,389},{6,134},{7,391},{8... | collective-permute-start | bytes 2359304 | tf_op jit(solution)/shard_map/ppermute | solution.py:30
  76.5 19.6 %collective-permute-start.10 = (bf16[512,768]{1,0:T(8,128)(2,1)S(1)}, bf16[512,768]{1,0:T(8,128)(2,1)S(1)}, u32[]{:S(2)}, u32[]{:S(2)}) collective-permute-start(bf16[512,768]{1,0:T(8,128)(2,1)S(1)} %bitcast_select_fusion), channel_id=1, source_target_pairs={{0,384},{1,129},{2,386},{3,131},{4,388},{5,133},{6,390},{7,135},{8... | collective-permute-start | bytes 2359304 | tf_op jit(solution)/shard_map/ppermute | solution.py:30
  79.7 22.3 %collective-permute-start.12 = (bf16[16,2048]{1,0:T(8,128)(2,1)S(1)}, bf16[16,2048]{1,0:T(8,128)(2,1)S(1)}, u32[]{:S(2)}, u32[]{:S(2)}) collective-permute-start(bf16[16,2048]{1,0:T(8,128)(2,1)S(1)} %fusion.64), channel_id=1, source_target_pairs={{0,2},{1,3},{2,0},{3,1},{4,6},{5,7},{6,4},{7,5},{8,10},{9,11},{10,... | collective-permute-start | bytes 196616 | tf_op jit(solution)/shard_map/ppermute | solution.py:30
  96.5 5.6 %copy-start.3 = (bf16[16,2048]{1,0:T(8,128)(2,1)S(1)}, bf16[16,2048]{1,0:T(8,128)(2,1)}, u32[]{:S(2)}) copy-start(bf16[16,2048]{1,0:T(8,128)(2,1)} %param.6) | copy-start | bytes 196612
  96.5 5.6 %copy-start.5 = (bf16[2048]{0:T(1024)(128)(2,1)S(1)}, bf16[2048]{0:T(1024)(128)(2,1)}, u32[]{:S(2)}) copy-start(bf16[2048]{0:T(1024)(128)(2,1)} %param.8) | copy-start | bytes 12292
  96.7 8.7 %collective-permute-start.13 = (bf16[2,2,64,384]{3,2,0,1:T(8,128)(2,1)S(1)}, bf16[2,2,64,384]{3,2,0,1:T(8,128)(2,1)S(1)}, u32[]{:S(2)}, u32[]{:S(2)}) collective-permute-start(bf16[2,2,64,384]{3,2,0,1:T(8,128)(2,1)S(1)} %fusion.34), channel_id=1, source_target_pairs={{0,16},{16,0},{32,48},{48,32},{64,80},{80,64},{96,112},{112,96},{1... | collective-permute-start | bytes 589832 | tf_op jit(solution)/shard_map/ppermute | solution.py:30
  98.7 10.3 %collective-permute-start.16 = (bf16[2,2,64,384]{3,2,0,1:T(8,128)(2,1)S(1)}, bf16[2,2,64,384]{3,2,0,1:T(8,128)(2,1)S(1)}, u32[]{:S(2)}, u32[]{:S(2)}) collective-permute-start(bf16[2,2,64,384]{3,2,0,1:T(8,128)(2,1)S(1)} %fusion.35), channel_id=1, source_target_pairs={{0,16},{16,0},{32,48},{48,32},{64,80},{80,64},{96,112},{112,96},{1... | collective-permute-start | bytes 589832 | tf_op jit(solution)/shard_map/ppermute | solution.py:30
  105.5 9.6 %collective-permute-start.14 = (bf16[2,64,384]{2,1,0:T(8,128)(2,1)S(1)}, bf16[2,64,384]{2,1,0:T(8,128)(2,1)S(1)}, u32[]{:S(2)}, u32[]{:S(2)}) collective-permute-start(bf16[2,64,384]{2,1,0:T(8,128)(2,1)S(1)} %fusion.62), channel_id=1, source_target_pairs={{0,32},{16,48},{32,0},{48,16},{64,96},{80,112},{96,64},{112,80},{1... | collective-permute-start | bytes 294920 | tf_op jit(solution)/shard_map/ppermute | solution.py:30
  109.1 12.8 %collective-permute-start.17 = (bf16[2,64,384]{2,1,0:T(8,128)(2,1)S(1)}, bf16[2,64,384]{2,1,0:T(8,128)(2,1)S(1)}, u32[]{:S(2)}, u32[]{:S(2)}) collective-permute-start(bf16[2,64,384]{2,1,0:T(8,128)(2,1)S(1)} %fusion.63), channel_id=1, source_target_pairs={{0,32},{16,48},{32,0},{48,16},{64,96},{80,112},{96,64},{112,80},{1... | collective-permute-start | bytes 294920 | tf_op jit(solution)/shard_map/ppermute | solution.py:30
  115.2 11.3 %collective-permute-start.15 = (bf16[64,384]{1,0:T(8,128)(2,1)S(1)}, bf16[64,384]{1,0:T(8,128)(2,1)S(1)}, u32[]{:S(2)}, u32[]{:S(2)}) collective-permute-start(bf16[64,384]{1,0:T(8,128)(2,1)S(1)} %fusion.65), channel_id=1, source_target_pairs={{0,64},{16,80},{32,96},{48,112},{64,0},{80,16},{96,32},{112,48},{1... | collective-permute-start | bytes 147464 | tf_op jit(solution)/shard_map/ppermute | solution.py:30
  121.9 12.0 %collective-permute-start.18 = (bf16[64,384]{1,0:T(8,128)(2,1)S(1)}, bf16[64,384]{1,0:T(8,128)(2,1)S(1)}, u32[]{:S(2)}, u32[]{:S(2)}) collective-permute-start(bf16[64,384]{1,0:T(8,128)(2,1)S(1)} %fusion.66), channel_id=1, source_target_pairs={{0,64},{16,80},{32,96},{48,112},{64,0},{80,16},{96,32},{112,48},{1... | collective-permute-start | bytes 147464 | tf_op jit(solution)/shard_map/ppermute | solution.py:30

commit v5 on v4

--- a/solution.py
+++ b/solution.py
@@ -19,11 +19,10 @@
     return out
 
 
-def wait(array, early):
-    rows, width = early.shape[0], array.shape[-1]
-    early = jnp.tile(early, (1, -(-width // early.shape[1])))[:, :width]
-    held = jnp.where(early == early, array.reshape(-1, rows, width), 0)
-    return held.reshape(array.shape)
+def wait(array, row):
+    width = array.shape[-1]
+    row = jnp.tile(row, -(-width // row.shape[0]))[:width]
+    return jnp.where(row == row, array, 0)
 
 
 def move(array, axis_name, count, target):
@@ -76,7 +75,7 @@
     total = pick(total, y, 0)
     for part in got:
         total = total + part.astype(F32)
-    return total
+    return total, sent[0, 0, 0]
 
 
 def scatter_high(total, late, high):
@@ -84,21 +83,15 @@
     return pick(total, high, 0) + got.astype(F32)
 
 
-def scatter_x(gathered, deltas, x, core):
-    width = gathered.shape[1] // NX
-    quarters = [gathered[:, i * width : (i + 1) * width] for i in range(NX)]
-
+def scatter_x(gate, up, early, x, core):
     def part(i):
-        rows = choose(i, quarters)
-        dims = (((0,), (0,)), ((), ()))
-        return lax.dot_general(rows, deltas, dims, preferred_element_type=F32).astype(BF16)
+        return jnp.stack([pick(gate, i % NX, 0), pick(up, i % NX, 0)])
 
     ahead = jnp.where(core == 0, 1, 3)
-    far = to_x(part((x + 2) % NX), 1)
-    joined = part((x + ahead) % NX).astype(F32) + far.astype(F32)
-    joined = joined.astype(BF16)
-    last = to_x(joined, 1)
-    near = to_x(wait(part((x + 4 - ahead) % NX), joined[:16]), -1)
+    far = to_x(part(x + 2), 1)
+    near = to_x(wait(part(x + 4 - ahead), early), -1)
+    joined = part(x + ahead).astype(F32) + far.astype(F32)
+    last = to_x(joined.astype(BF16), 1)
     return part(x).astype(F32) + near.astype(F32) + last.astype(F32)
 
 
@@ -128,19 +121,20 @@
     up_delta = (cot * gate * sig).astype(BF16)
     gate_delta = (cot * up * sig * (1.0 + gate * (1.0 - sig))).astype(BF16)
     contract_last = (((1,), (1,)), ((), ()))
-    deltas = jnp.concatenate([gate_delta, up_delta], axis=1)
+    contract_first = (((0,), (0,)), ((), ()))
+    first = lax.dot_general(gathered, gate_delta, contract_first, preferred_element_type=F32)
+    second = lax.dot_general(gathered, up_delta, contract_first, preferred_element_type=F32)
+    gate_parts = first.astype(BF16).reshape(NX, depth // NX, width)
+    up_parts = second.astype(BF16).reshape(NX, depth // NX, width)
     first = lax.dot_general(gate_delta, gate_weight, contract_last, preferred_element_type=F32)
     second = lax.dot_general(up_delta, up_weight, contract_last, preferred_element_type=F32)
-    rows = scatter_rows((first + second).astype(BF16), y, high, core)
-    total = scatter_x(gathered, deltas, x, core)
-    normed_grad = scatter_high(rows, total[:16], high)
-    total = total.reshape(2, 2, 2, depth // (NX * NZ), 2 * width)
-    gate_grad = scatter_z(total[..., :width], z, 1, 2)
-    up_grad = scatter_z(total[..., width:], z, 1, 2)
-    gate_grad = scatter_z(gate_grad, z, 2, 1)
-    up_grad = scatter_z(up_grad, z, 2, 1)
-    gate_grad = scatter_z(gate_grad, z, 4, 0)
-    up_grad = scatter_z(up_grad, z, 4, 0)
+    rows, early = scatter_rows((first + second).astype(BF16), y, high, core)
+    total = scatter_x(gate_parts, up_parts, early, x, core)
+    normed_grad = scatter_high(rows, total[0, 0], high)
+    total = total.reshape(2, 2, 2, 2, depth // (NX * NZ), width)
+    gate_grad, up_grad = scatter_z(total[0], z, 1, 2), scatter_z(total[1], z, 1, 2)
+    gate_grad, up_grad = scatter_z(gate_grad, z, 2, 1), scatter_z(up_grad, z, 2, 1)
+    gate_grad, up_grad = scatter_z(gate_grad, z, 4, 0), scatter_z(up_grad, z, 4, 0)
     inner = jnp.mean(normed_grad * normed_full, axis=-1, keepdims=True)
     token_grad = jnp.where(flag, 0.0, inverse * (normed_grad - normed_full * inner)).astype(BF16)
     return (hidden, token_grad, gate_grad, up_grad)

time: 135 us -> 134 us (level); the launches traced: 135 us -> 132 us
  waiting for transfers between devices: 24 us -> 11.6 us
  other arithmetic: 9.29 us -> 18 us
  matrix products: 8.99 us -> 5.26 us
  starting transfers between devices: 88.3 us -> 91.2 us
  local copies, waits for them, and re-layouts: 2.37 us -> 4.29 us
    ppermute x19, waiting for transfers between devices: 24 us -> 11.6 us  [move(): lax.ppermute(array, axis_name, [(i, target(i)) for i in range(count)])]
    ppermute x19, starting transfers between devices: 88.3 us -> 91.2 us  [move(): lax.ppermute(array, axis_name, [(i, target(i)) for i in range(count)])]
    dot_general x4 -> x2, matrix products: 3.86 us -> 1.56 us  [the longest x1 0.8 us: shards(): lax.dot_general(gathered, up_delta, contract_first, preferred_element_typ...]
    add x6, other arithmetic: 1.42 us -> 3.29 us  [scatter_z(): return pick(total, mine, axis) + to_z(sent, bit).astype(F32)]
    unnamed x15 -> x18, local copies, waits for them, and re-layouts: 1.88 us -> 0.23 us
    dot_general x1, matrix products: 2.15 us -> 0.72 us  [shards(): gate = jnp.dot(gathered, gate_weight, preferred_element_type=F32)]
    add x1, other arithmetic: 0.26 us -> 1.63 us  [scatter_x(): return part(x).astype(F32) + near.astype(F32) + last.astype(F32)]
  transfers between devices with their start and end apart: 19 -> 19, of which waited for: 10 -> 6; matrix products, arithmetic and copies ran while one was open for 6% -> 12% of each run, Pallas kernels for 0% -> 0%
where the time goes in v5:
time: 134 us; the launch traced here: 132 us
  starting transfers between devices  91.2 us (68%)
  other arithmetic  18 us (13%)
  waiting for transfers between devices  11.6 us (9%)
  matrix products  5.26 us (4%)
  local copies, waits for them, and re-layouts  4.29 us (3%)
  between operations  1.52 us (1%)
    ppermute x19, starting transfers between devices, move(): lax.ppermute(array, axis_name, [(i, target(i)) for i in range(count)])  91.2 us
    ppermute x19, waiting for transfers between devices, move(): lax.ppermute(array, axis_name, [(i, target(i)) for i in range(count)])  11.6 us
    add x6, other arithmetic, scatter_z(): return pick(total, mine, axis) + to_z(sent, bit).astype(F32)  3.29 us
  transfers between devices with their start and end apart: 19, of which 6 were waited for; matrix products, arithmetic and copies ran while one was open for 12% of the time, Pallas kernels for 0%

profile of v5, /device:TPU:1, one launch (start us, length us, event | category | flops | bytes accessed | tf_op | source)
XLA Modules:
  0.0 131.8 jit_solution(9802006826563756644)
XLA Ops:
  0.6 0.0 copy-start
  0.6 0.8 broadcast_compare_fusion
  1.4 1.0 fusion.18
  2.5 0.9 fusion.12
  3.4 16.3 %collective-permute-start = (bf16[16,2048]{1,0:T(8,128)(2,1)S(1)}, bf16[16,2048]{1,0:T(8,128)(2,1)S(1)}, u32[]{:S(2)}, u32[]{:S(2)}) collective-permute-start(bf16[16,2048]{1,0:T(8,128)(2,1)S(1)} %fusion.12), channel_id=1, source_target_pairs={{0,2},{1,3},{2,0},{3,1},{4,6},{5,7},{6,4},{7,5},{8,10},{9,11},{10,... | collective-permute-start | bytes 196616 | tf_op jit(solution)/shard_map/ppermute | solution.py:29
  19.7 0.9 fusion.41
  20.7 0.9 collective-permute-done
  21.6 4.8 %collective-permute-start.1 = (bf16[2,16,2048]{2,1,0:T(8,128)(2,1)S(1)}, bf16[2,16,2048]{2,1,0:T(8,128)(2,1)S(1)}, u32[]{:S(2)}, u32[]{:S(2)}) collective-permute-start(bf16[2,16,2048]{2,1,0:T(8,128)(2,1)S(1)} %maximum_select_fusion.2), channel_id=1, source_target_pairs={{0,8},{1,9},{2,10},{3,11},{4,12},{5,13},{6,14},{7,15},{8,0},{9,1},... | collective-permute-start | bytes 393224 | tf_op jit(solution)/shard_map/ppermute | solution.py:29
  26.4 2.3 %collective-permute-start.2 = (bf16[2,16,2048]{2,1,0:T(8,128)(2,1)S(1)}, bf16[2,16,2048]{2,1,0:T(8,128)(2,1)S(1)}, u32[]{:S(2)}, u32[]{:S(2)}) collective-permute-start(bf16[2,16,2048]{2,1,0:T(8,128)(2,1)S(1)} %maximum_select_fusion.2), channel_id=1, source_target_pairs={{0,4},{1,5},{2,6},{3,7},{4,8},{5,9},{6,10},{7,11},{8,12},{9,13},{1... | collective-permute-start | bytes 393224 | tf_op jit(solution)/shard_map/ppermute | solution.py:29
  28.7 4.2 %collective-permute-start.3 = (bf16[2,16,2048]{2,1,0:T(8,128)(2,1)S(1)}, bf16[2,16,2048]{2,1,0:T(8,128)(2,1)S(1)}, u32[]{:S(2)}, u32[]{:S(2)}) collective-permute-start(bf16[2,16,2048]{2,1,0:T(8,128)(2,1)S(1)} %maximum_select_fusion.2), channel_id=1, source_target_pairs={{0,12},{1,13},{2,14},{3,15},{4,0},{5,1},{6,2},{7,3},{8,4},{9,5},{1... | collective-permute-start | bytes 393224 | tf_op jit(solution)/shard_map/ppermute | solution.py:29
  32.9 0.0 collective-permute-done.1
  32.9 1.6 %collective-permute-done.2 = bf16[2,16,2048]{2,1,0:T(8,128)(2,1)S(1)} collective-permute-done((bf16[2,16,2048]{2,1,0:T(8,128)(2,1)S(1)}, bf16[2,16,2048]{2,1,0:T(8,128)(2,1)S(1)}, u32[]{:S(2)}, u32[]{:S(2)}) %collective-permute-start.2) | collective-permute-done | bytes 131104 | tf_op jit(solution)/shard_map/ppermute | solution.py:29
  34.5 0.3 collective-permute-done.3
  34.8 0.1 select_bitcast_fusion.3
  34.9 1.1 fusion.26
  36.0 6.8 %collective-permute-start.4 = (bf16[4,2,16,2048]{3,2,1,0:T(8,128)(2,1)}, bf16[4,2,16,2048]{3,2,1,0:T(8,128)(2,1)}, u32[]{:S(2)}, u32[]{:S(2)}) collective-permute-start(bf16[4,2,16,2048]{3,2,1,0:T(8,128)(2,1)} %get-tuple-element.22), channel_id=1, source_target_pairs={{0,1},{1,0},{2,3},{3,2},{4,5},{5,4},{6,7},{7,6},{8,9},{9,8},{10,11... | collective-permute-start | bytes 1572872 | tf_op jit(solution)/shard_map/ppermute | solution.py:29
  42.9 1.7 %collective-permute-done.4 = bf16[4,2,16,2048]{3,2,1,0:T(8,128)(2,1)} collective-permute-done((bf16[4,2,16,2048]{3,2,1,0:T(8,128)(2,1)}, bf16[4,2,16,2048]{3,2,1,0:T(8,128)(2,1)}, u32[]{:S(2)}, u32[]{:S(2)}) %collective-permute-start.4) | collective-permute-done | bytes 524320 | tf_op jit(solution)/shard_map/ppermute | solution.py:29
  44.6 1.8 %maximum_select_fusion = bf16[4,2,2,16,2048]{4,3,2,1,0:T(8,128)(2,1)S(1)} fusion(bf16[4,2,1,16,2048]{4,3,2,1,0:T(8,128)(2,1)} %bitcast.7, bf16[4,2,1,16,2048]{4,3,2,1,0:T(8,128)(2,1)} %get-tuple-element.21, pred[]{:T(512)S(6)} %eq.59), kind=kLoop, calls=%fused_computation.6 | loop fusion | flops 1572864 | bytes 2097153 | tf_op jit(solution)/shard_map/jit(_where)/select_n | solution.py:64
  46.4 0.0 copy-start.5
  46.4 0.7 fusion.29
  47.2 0.2 copy-done.5
  47.3 0.8 convolution_convert_fusion
  48.2 1.5 %fusion.3 = (bf16[256,384]{1,0:T(8,128)(2,1)S(1)}, bf16[256,384]{1,0:T(8,128)(2,1)}) fusion(bf16[256,384]{1,0:T(8,128)(2,1)S(1)} %copy-done.5, f32[256,384]{1,0:T(8,128)S(1)} %fusion.29, bf16[256,2048]{1,0:T(8,128)(2,1)S(1)} %bitcast.82, bf16[2048,384]{1,0:T(8,128)(2,1)S(1)} %copy-done), kind=kOutput, calls=%fused_computation.16 | convolution fusion | flops 404029440 | bytes 3604480 | tf_op jit(solution)/shard_map/dot_general | solution.py:117
  49.6 0.7 fusion.30
  50.4 0.8 fusion
  51.2 2.3 %collective-permute-start.5 = (bf16[4,2,16,2048]{3,2,1,0:T(8,128)(2,1)S(1)}, bf16[4,2,16,2048]{3,2,1,0:T(8,128)(2,1)S(1)}, u32[]{:S(2)}, u32[]{:S(2)}) collective-permute-start(bf16[4,2,16,2048]{3,2,1,0:T(8,128)(2,1)S(1)} %dynamic-slice_bitcast_fusion), channel_id=1, source_target_pairs={{0,1},{1,0},{2,3},{3,2},{4,5},{5,4},{6,7},{7,6},{8,9},{9,8},{10,11... | collective-permute-start | bytes 1572872 | tf_op jit(solution)/shard_map/ppermute | solution.py:29
  53.5 0.8 convolution_convert_fusion.1
  54.3 0.3 constant_dynamic-slice_fusion.6
  54.6 0.1 pad_maximum_fusion
  54.7 4.4 %collective-permute-start.10 = (bf16[2,512,384]{2,1,0:T(8,128)(2,1)S(1)}, bf16[2,512,384]{2,1,0:T(8,128)(2,1)S(1)}, u32[]{:S(2)}, u32[]{:S(2)}) collective-permute-start(bf16[2,512,384]{2,1,0:T(8,128)(2,1)S(1)} %pad_maximum_fusion), channel_id=1, source_target_pairs={{0,128},{1,385},{2,130},{3,387},{4,132},{5,389},{6,134},{7,391},{8... | collective-permute-start | bytes 2359304 | tf_op jit(solution)/shard_map/ppermute | solution.py:29
  59.1 0.2 fusion.27
  59.3 1.0 maximum_select_fusion.1
  60.4 1.9 %collective-permute-start.9 = (bf16[2,512,384]{2,1,0:T(8,128)(2,1)}, bf16[2,512,384]{2,1,0:T(8,128)(2,1)}, u32[]{:S(2)}, u32[]{:S(2)}) collective-permute-start(bf16[2,512,384]{2,1,0:T(8,128)(2,1)} %maximum_select_fusion.1), channel_id=1, source_target_pairs={{0,384},{1,129},{2,386},{3,131},{4,388},{5,133},{6,390},{7,135},{8... | collective-permute-start | bytes 2359304 | tf_op jit(solution)/shard_map/ppermute | solution.py:29
  62.3 0.8 dynamic-slice_bitcast_fusion.3
  63.0 1.9 %collective-permute-start.6 = (bf16[2,16,2048]{2,1,0:T(8,128)(2,1)}, bf16[2,16,2048]{2,1,0:T(8,128)(2,1)S(1)}, u32[]{:S(2)}, u32[]{:S(2)}) collective-permute-start(bf16[2,16,2048]{2,1,0:T(8,128)(2,1)} %get-tuple-element.18), channel_id=1, source_target_pairs={{0,4},{1,5},{2,6},{3,7},{4,8},{5,9},{6,10},{7,11},{8,12},{9,13},{1... | collective-permute-start | bytes 393224 | tf_op jit(solution)/shard_map/ppermute | solution.py:29
  65.0 6.5 %collective-permute-start.7 = (bf16[2,16,2048]{2,1,0:T(8,128)(2,1)}, bf16[2,16,2048]{2,1,0:T(8,128)(2,1)}, u32[]{:S(2)}, u32[]{:S(2)}) collective-permute-start(bf16[2,16,2048]{2,1,0:T(8,128)(2,1)} %get-tuple-element.20), channel_id=1, source_target_pairs={{0,8},{1,9},{2,10},{3,11},{4,12},{5,13},{6,14},{7,15},{8,0},{9,1},... | collective-permute-start | bytes 393224 | tf_op jit(solution)/shard_map/ppermute | solution.py:29
  71.4 1.9 %collective-permute-start.8 = (bf16[2,16,2048]{2,1,0:T(8,128)(2,1)}, bf16[2,16,2048]{2,1,0:T(8,128)(2,1)}, u32[]{:S(2)}, u32[]{:S(2)}) collective-permute-start(bf16[2,16,2048]{2,1,0:T(8,128)(2,1)} %get-tuple-element.19), channel_id=1, source_target_pairs={{0,12},{1,13},{2,14},{3,15},{4,0},{5,1},{6,2},{7,3},{8,4},{9,5},{1... | collective-permute-start | bytes 393224 | tf_op jit(solution)/shard_map/ppermute | solution.py:29
  73.4 1.1 add_convert_fusion
  74.5 4.6 %collective-permute-start.11 = (bf16[2,512,384]{2,1,0:T(8,128)(2,1)}, bf16[2,512,384]{2,1,0:T(8,128)(2,1)}, u32[]{:S(2)}, u32[]{:S(2)}) collective-permute-start(bf16[2,512,384]{2,1,0:T(8,128)(2,1)} %add_convert_fusion), channel_id=1, source_target_pairs={{0,128},{1,385},{2,130},{3,387},{4,132},{5,389},{6,134},{7,391},{8... | collective-permute-start | bytes 2359304 | tf_op jit(solution)/shard_map/ppermute | solution.py:29
  79.2 1.0 fusion.7
  80.2 0.7 fusion.21
  80.9 12.8 %collective-permute-start.12 = (bf16[16,2048]{1,0:T(8,128)(2,1)}, bf16[16,2048]{1,0:T(8,128)(2,1)S(1)}, u32[]{:S(2)}, u32[]{:S(2)}) collective-permute-start(bf16[16,2048]{1,0:T(8,128)(2,1)} %fusion.21), channel_id=1, source_target_pairs={{0,2},{1,3},{2,0},{3,1},{4,6},{5,7},{6,4},{7,5},{8,10},{9,11},{10,... | collective-permute-start | bytes 196616 | tf_op jit(solution)/shard_map/ppermute | solution.py:29
  93.8 1.6 %convert_add_fusion = f32[2,512,384]{2,1,0:T(8,128)S(1)} fusion(bf16[2,512,384]{2,1,0:T(8,128)(2,1)} %collective-permute-done.11, bf16[2,512,384]{2,1,0:T(8,128)(2,1)} %collective-permute-done.9, bf16[1,512,384]{2,1,0:T(8,128)(2,1)S(1)} %get-tuple-element.12, bf16[1,512,384]{2,1,0:T(8,128)(2,1)S(1)} %get-tuple-element.30), kind=kLoop, calls=%fused_computation.4 | loop fusion | flops 2359296 | bytes 3932160 | tf_op jit(solution)/shard_map/add | solution.py:95
  95.4 0.0 copy-start.2
  95.4 0.0 copy-start.6
  95.4 0.1 fusion.28
  95.6 0.7 fusion.9
  96.3 1.9 %collective-permute-start.16 = (bf16[2,2,64,384]{3,2,1,0:T(8,128)(2,1)}, bf16[2,2,64,384]{3,2,1,0:T(8,128)(2,1)}, u32[]{:S(2)}, u32[]{:S(2)}) collective-permute-start(bf16[2,2,64,384]{3,2,1,0:T(8,128)(2,1)} %fusion.9), channel_id=1, source_target_pairs={{0,16},{16,0},{32,48},{48,32},{64,80},{80,64},{96,112},{112,96},{1... | collective-permute-start | bytes 589832 | tf_op jit(solution)/shard_map/ppermute | solution.py:29
  98.2 0.7 fusion.8
  98.9 3.4 %collective-permute-start.13 = (bf16[2,2,64,384]{3,2,1,0:T(8,128)(2,1)}, bf16[2,2,64,384]{3,2,1,0:T(8,128)(2,1)}, u32[]{:S(2)}, u32[]{:S(2)}) collective-permute-start(bf16[2,2,64,384]{3,2,1,0:T(8,128)(2,1)} %fusion.8), channel_id=1, source_target_pairs={{0,16},{16,0},{32,48},{48,32},{64,80},{80,64},{96,112},{112,96},{1... | collective-permute-start | bytes 589832 | tf_op jit(solution)/shard_map/ppermute | solution.py:29
  102.2 0.6 tile.12
  102.8 0.7 slice_compare_fusion
  103.6 0.9 fusion.13
  104.5 1.4 %fusion.17 = bf16[16,2048]{1,0:T(8,128)(2,1)} fusion(f32[2,16,2048]{2,1,0:T(8,128)S(1)} %copy-done.4, s32[]{:T(128)S(6)} %select_n.289, f32[16]{0:T(128)S(1)} %broadcast_multiply_fusion, f32[16]{0:T(128)} %copy-done.8, pred[16]{0:T(512)(128)(4,1)} %copy-done.7, bf16[16,2048]{1,0:T(8,128)(2,1)S(1)} %collective-permute-done.12, ...), kind=kLoop, calls=%fused_computation.43 | loop fusion | flops 360448 | bytes 333972 | tf_op jit(solution)/shard_map/convert_element_type | solution.py:139
  105.9 1.0 bitcast_add_fusion
  106.9 3.0 %collective-permute-start.17 = (bf16[2,64,384]{2,1,0:T(8,128)(2,1)S(1)}, bf16[2,64,384]{2,1,0:T(8,128)(2,1)S(1)}, u32[]{:S(2)}, u32[]{:S(2)}) collective-permute-start(bf16[2,64,384]{2,1,0:T(8,128)(2,1)S(1)} %fusion.20), channel_id=1, source_target_pairs={{0,32},{16,48},{32,0},{48,16},{64,96},{80,112},{96,64},{112,80},{1... | collective-permute-start | bytes 294920 | tf_op jit(solution)/shard_map/ppermute | solution.py:29
  109.9 1.0 bitcast_add_fusion.1
  110.9 3.2 %collective-permute-start.14 = (bf16[2,64,384]{2,1,0:T(8,128)(2,1)S(1)}, bf16[2,64,384]{2,1,0:T(8,128)(2,1)S(1)}, u32[]{:S(2)}, u32[]{:S(2)}) collective-permute-start(bf16[2,64,384]{2,1,0:T(8,128)(2,1)S(1)} %fusion.19), channel_id=1, source_target_pairs={{0,32},{16,48},{32,0},{48,16},{64,96},{80,112},{96,64},{112,80},{1... | collective-permute-start | bytes 294920 | tf_op jit(solution)/shard_map/ppermute | solution.py:29
  114.1 1.5 %collective-permute-done.17 = bf16[2,64,384]{2,1,0:T(8,128)(2,1)S(1)} collective-permute-done((bf16[2,64,384]{2,1,0:T(8,128)(2,1)S(1)}, bf16[2,64,384]{2,1,0:T(8,128)(2,1)S(1)}, u32[]{:S(2)}, u32[]{:S(2)}) %collective-permute-start.17) | collective-permute-done | bytes 98336 | tf_op jit(solution)/shard_map/ppermute | solution.py:29
  115.6 1.9 %collective-permute-start.18 = (bf16[64,384]{1,0:T(8,128)(2,1)S(1)}, bf16[64,384]{1,0:T(8,128)(2,1)S(1)}, u32[]{:S(2)}, u32[]{:S(2)}) collective-permute-start(bf16[64,384]{1,0:T(8,128)(2,1)S(1)} %fusion.23), channel_id=1, source_target_pairs={{0,64},{16,80},{32,96},{48,112},{64,0},{80,16},{96,32},{112,48},{1... | collective-permute-start | bytes 147464 | tf_op jit(solution)/shard_map/ppermute | solution.py:29
  117.6 7.3 %collective-permute-start.15 = (bf16[64,384]{1,0:T(8,128)(2,1)S(1)}, bf16[64,384]{1,0:T(8,128)(2,1)S(1)}, u32[]{:S(2)}, u32[]{:S(2)}) collective-permute-start(bf16[64,384]{1,0:T(8,128)(2,1)S(1)} %fusion.22), channel_id=1, source_target_pairs={{0,64},{16,80},{32,96},{48,112},{64,0},{80,16},{96,32},{112,48},{1... | collective-permute-start | bytes 147464 | tf_op jit(solution)/shard_map/ppermute | solution.py:29
  124.9 0.7 bitcast_add_fusion.6
  125.5 5.6 %collective-permute-done.15 = bf16[64,384]{1,0:T(8,128)(2,1)S(1)} collective-permute-done((bf16[64,384]{1,0:T(8,128)(2,1)S(1)}, bf16[64,384]{1,0:T(8,128)(2,1)S(1)}, u32[]{:S(2)}, u32[]{:S(2)}) %collective-permute-start.15) | collective-permute-done | bytes 49184 | tf_op jit(solution)/shard_map/ppermute | solution.py:29
  131.2 0.7 bitcast_add_fusion.7
  (38 shorter events, 0.3 us)
Async XLA Ops:
  0.6 47.5 %copy-start = (bf16[2048,384]{1,0:T(8,128)(2,1)S(1)}, bf16[2048,384]{1,0:T(8,128)(2,1)}, u32[]{:S(2)}) copy-start(bf16[2048,384]{1,0:T(8,128)(2,1)} %param.10) | copy-start | bytes 4718596
  1.4 18.3 %copy-start.7 = (pred[16]{0:T(512)(128)(4,1)}, pred[16]{0:T(512)(128)(4,1)S(1)}, u32[]{:S(2)}) copy-start(pred[16]{0:T(512)(128)(4,1)S(1)} %broadcast_compare_fusion) | copy-start | bytes 52
  2.5 18.2 %copy-start.8 = (f32[16]{0:T(128)}, f32[16]{0:T(128)S(1)}, u32[]{:S(2)}) copy-start(f32[16]{0:T(128)S(1)} %add_rsqrt_fusion) | copy-start | bytes 196
  3.4 18.1 %collective-permute-start = (bf16[16,2048]{1,0:T(8,128)(2,1)S(1)}, bf16[16,2048]{1,0:T(8,128)(2,1)S(1)}, u32[]{:S(2)}, u32[]{:S(2)}) collective-permute-start(bf16[16,2048]{1,0:T(8,128)(2,1)S(1)} %fusion.12), channel_id=1, source_target_pairs={{0,2},{1,3},{2,0},{3,1},{4,6},{5,7},{6,4},{7,5},{8,10},{9,11},{10,... | collective-permute-start | bytes 196616 | tf_op jit(solution)/shard_map/ppermute | solution.py:29
  21.6 11.4 %collective-permute-start.1 = (bf16[2,16,2048]{2,1,0:T(8,128)(2,1)S(1)}, bf16[2,16,2048]{2,1,0:T(8,128)(2,1)S(1)}, u32[]{:S(2)}, u32[]{:S(2)}) collective-permute-start(bf16[2,16,2048]{2,1,0:T(8,128)(2,1)S(1)} %maximum_select_fusion.2), channel_id=1, source_target_pairs={{0,8},{1,9},{2,10},{3,11},{4,12},{5,13},{6,14},{7,15},{8,0},{9,1},... | collective-permute-start | bytes 393224 | tf_op jit(solution)/shard_map/ppermute | solution.py:29
  26.4 8.1 %collective-permute-start.2 = (bf16[2,16,2048]{2,1,0:T(8,128)(2,1)S(1)}, bf16[2,16,2048]{2,1,0:T(8,128)(2,1)S(1)}, u32[]{:S(2)}, u32[]{:S(2)}) collective-permute-start(bf16[2,16,2048]{2,1,0:T(8,128)(2,1)S(1)} %maximum_select_fusion.2), channel_id=1, source_target_pairs={{0,4},{1,5},{2,6},{3,7},{4,8},{5,9},{6,10},{7,11},{8,12},{9,13},{1... | collective-permute-start | bytes 393224 | tf_op jit(solution)/shard_map/ppermute | solution.py:29
  28.7 6.1 %collective-permute-start.3 = (bf16[2,16,2048]{2,1,0:T(8,128)(2,1)S(1)}, bf16[2,16,2048]{2,1,0:T(8,128)(2,1)S(1)}, u32[]{:S(2)}, u32[]{:S(2)}) collective-permute-start(bf16[2,16,2048]{2,1,0:T(8,128)(2,1)S(1)} %maximum_select_fusion.2), channel_id=1, source_target_pairs={{0,12},{1,13},{2,14},{3,15},{4,0},{5,1},{6,2},{7,3},{8,4},{9,5},{1... | collective-permute-start | bytes 393224 | tf_op jit(solution)/shard_map/ppermute | solution.py:29
  36.0 10.4 %copy-start.1 = (bf16[2048,384]{1,0:T(8,128)(2,1)S(1)}, bf16[2048,384]{1,0:T(8,128)(2,1)}, u32[]{:S(2)}) copy-start(bf16[2048,384]{1,0:T(8,128)(2,1)} %param.9) | copy-start | bytes 4718596
  36.0 8.6 %collective-permute-start.4 = (bf16[4,2,16,2048]{3,2,1,0:T(8,128)(2,1)}, bf16[4,2,16,2048]{3,2,1,0:T(8,128)(2,1)}, u32[]{:S(2)}, u32[]{:S(2)}) collective-permute-start(bf16[4,2,16,2048]{3,2,1,0:T(8,128)(2,1)} %get-tuple-element.22), channel_id=1, source_target_pairs={{0,1},{1,0},{2,3},{3,2},{4,5},{5,4},{6,7},{7,6},{8,9},{9,8},{10,11... | collective-permute-start | bytes 1572872 | tf_op jit(solution)/shard_map/ppermute | solution.py:29
  46.4 0.9 copy-start.5
  51.2 7.9 %collective-permute-start.5 = (bf16[4,2,16,2048]{3,2,1,0:T(8,128)(2,1)S(1)}, bf16[4,2,16,2048]{3,2,1,0:T(8,128)(2,1)S(1)}, u32[]{:S(2)}, u32[]{:S(2)}) collective-permute-start(bf16[4,2,16,2048]{3,2,1,0:T(8,128)(2,1)S(1)} %dynamic-slice_bitcast_fusion), channel_id=1, source_target_pairs={{0,1},{1,0},{2,3},{3,2},{4,5},{5,4},{6,7},{7,6},{8,9},{9,8},{10,11... | collective-permute-start | bytes 1572872 | tf_op jit(solution)/shard_map/ppermute | solution.py:29
  54.7 18.6 %collective-permute-start.10 = (bf16[2,512,384]{2,1,0:T(8,128)(2,1)S(1)}, bf16[2,512,384]{2,1,0:T(8,128)(2,1)S(1)}, u32[]{:S(2)}, u32[]{:S(2)}) collective-permute-start(bf16[2,512,384]{2,1,0:T(8,128)(2,1)S(1)} %pad_maximum_fusion), channel_id=1, source_target_pairs={{0,128},{1,385},{2,130},{3,387},{4,132},{5,389},{6,134},{7,391},{8... | collective-permute-start | bytes 2359304 | tf_op jit(solution)/shard_map/ppermute | solution.py:29
  60.4 33.4 %collective-permute-start.9 = (bf16[2,512,384]{2,1,0:T(8,128)(2,1)}, bf16[2,512,384]{2,1,0:T(8,128)(2,1)}, u32[]{:S(2)}, u32[]{:S(2)}) collective-permute-start(bf16[2,512,384]{2,1,0:T(8,128)(2,1)} %maximum_select_fusion.1), channel_id=1, source_target_pairs={{0,384},{1,129},{2,386},{3,131},{4,388},{5,133},{6,390},{7,135},{8... | collective-permute-start | bytes 2359304 | tf_op jit(solution)/shard_map/ppermute | solution.py:29
  63.0 16.1 %collective-permute-start.6 = (bf16[2,16,2048]{2,1,0:T(8,128)(2,1)}, bf16[2,16,2048]{2,1,0:T(8,128)(2,1)S(1)}, u32[]{:S(2)}, u32[]{:S(2)}) collective-permute-start(bf16[2,16,2048]{2,1,0:T(8,128)(2,1)} %get-tuple-element.18), channel_id=1, source_target_pairs={{0,4},{1,5},{2,6},{3,7},{4,8},{5,9},{6,10},{7,11},{8,12},{9,13},{1... | collective-permute-start | bytes 393224 | tf_op jit(solution)/shard_map/ppermute | solution.py:29
  65.0 14.2 %collective-permute-start.7 = (bf16[2,16,2048]{2,1,0:T(8,128)(2,1)}, bf16[2,16,2048]{2,1,0:T(8,128)(2,1)}, u32[]{:S(2)}, u32[]{:S(2)}) collective-permute-start(bf16[2,16,2048]{2,1,0:T(8,128)(2,1)} %get-tuple-element.20), channel_id=1, source_target_pairs={{0,8},{1,9},{2,10},{3,11},{4,12},{5,13},{6,14},{7,15},{8,0},{9,1},... | collective-permute-start | bytes 393224 | tf_op jit(solution)/shard_map/ppermute | solution.py:29
  71.4 7.8 %collective-permute-start.8 = (bf16[2,16,2048]{2,1,0:T(8,128)(2,1)}, bf16[2,16,2048]{2,1,0:T(8,128)(2,1)}, u32[]{:S(2)}, u32[]{:S(2)}) collective-permute-start(bf16[2,16,2048]{2,1,0:T(8,128)(2,1)} %get-tuple-element.19), channel_id=1, source_target_pairs={{0,12},{1,13},{2,14},{3,15},{4,0},{5,1},{6,2},{7,3},{8,4},{9,5},{1... | collective-permute-start | bytes 393224 | tf_op jit(solution)/shard_map/ppermute | solution.py:29
  74.5 19.3 %collective-permute-start.11 = (bf16[2,512,384]{2,1,0:T(8,128)(2,1)}, bf16[2,512,384]{2,1,0:T(8,128)(2,1)}, u32[]{:S(2)}, u32[]{:S(2)}) collective-permute-start(bf16[2,512,384]{2,1,0:T(8,128)(2,1)} %add_convert_fusion), channel_id=1, source_target_pairs={{0,128},{1,385},{2,130},{3,387},{4,132},{5,389},{6,134},{7,391},{8... | collective-permute-start | bytes 2359304 | tf_op jit(solution)/shard_map/ppermute | solution.py:29
  80.2 13.5 %copy-start.3 = (f32[2,16,2048]{2,1,0:T(8,128)}, f32[2,16,2048]{2,1,0:T(8,128)S(1)}, u32[]{:S(2)}) copy-start(f32[2,16,2048]{2,1,0:T(8,128)S(1)} %fusion.7) | copy-start | bytes 786436
  80.9 22.6 %collective-permute-start.12 = (bf16[16,2048]{1,0:T(8,128)(2,1)}, bf16[16,2048]{1,0:T(8,128)(2,1)S(1)}, u32[]{:S(2)}, u32[]{:S(2)}) collective-permute-start(bf16[16,2048]{1,0:T(8,128)(2,1)} %fusion.21), channel_id=1, source_target_pairs={{0,2},{1,3},{2,0},{3,1},{4,6},{5,7},{6,4},{7,5},{8,10},{9,11},{10,... | collective-permute-start | bytes 196616 | tf_op jit(solution)/shard_map/ppermute | solution.py:29
  95.4 8.2 %copy-start.2 = (bf16[16,2048]{1,0:T(8,128)(2,1)S(1)}, bf16[16,2048]{1,0:T(8,128)(2,1)}, u32[]{:S(2)}) copy-start(bf16[16,2048]{1,0:T(8,128)(2,1)} %param.6) | copy-start | bytes 196612
  95.4 8.2 %copy-start.4 = (f32[2,16,2048]{2,1,0:T(8,128)S(1)}, f32[2,16,2048]{2,1,0:T(8,128)}, u32[]{:S(2)}) copy-start(f32[2,16,2048]{2,1,0:T(8,128)} %copy-done.3) | copy-start | bytes 786436
  95.4 8.2 %copy-start.6 = (bf16[2048]{0:T(1024)(128)(2,1)S(1)}, bf16[2048]{0:T(1024)(128)(2,1)}, u32[]{:S(2)}) copy-start(bf16[2048]{0:T(1024)(128)(2,1)} %param.8) | copy-start | bytes 12292
  96.3 9.6 %collective-permute-start.16 = (bf16[2,2,64,384]{3,2,1,0:T(8,128)(2,1)}, bf16[2,2,64,384]{3,2,1,0:T(8,128)(2,1)}, u32[]{:S(2)}, u32[]{:S(2)}) collective-permute-start(bf16[2,2,64,384]{3,2,1,0:T(8,128)(2,1)} %fusion.9), channel_id=1, source_target_pairs={{0,16},{16,0},{32,48},{48,32},{64,80},{80,64},{96,112},{112,96},{1... | collective-permute-start | bytes 589832 | tf_op jit(solution)/shard_map/ppermute | solution.py:29
  98.9 11.0 %collective-permute-start.13 = (bf16[2,2,64,384]{3,2,1,0:T(8,128)(2,1)}, bf16[2,2,64,384]{3,2,1,0:T(8,128)(2,1)}, u32[]{:S(2)}, u32[]{:S(2)}) collective-permute-start(bf16[2,2,64,384]{3,2,1,0:T(8,128)(2,1)} %fusion.8), channel_id=1, source_target_pairs={{0,16},{16,0},{32,48},{48,32},{64,80},{80,64},{96,112},{112,96},{1... | collective-permute-start | bytes 589832 | tf_op jit(solution)/shard_map/ppermute | solution.py:29
  106.9 8.7 %collective-permute-start.17 = (bf16[2,64,384]{2,1,0:T(8,128)(2,1)S(1)}, bf16[2,64,384]{2,1,0:T(8,128)(2,1)S(1)}, u32[]{:S(2)}, u32[]{:S(2)}) collective-permute-start(bf16[2,64,384]{2,1,0:T(8,128)(2,1)S(1)} %fusion.20), channel_id=1, source_target_pairs={{0,32},{16,48},{32,0},{48,16},{64,96},{80,112},{96,64},{112,80},{1... | collective-permute-start | bytes 294920 | tf_op jit(solution)/shard_map/ppermute | solution.py:29
  110.9 6.6 %collective-permute-start.14 = (bf16[2,64,384]{2,1,0:T(8,128)(2,1)S(1)}, bf16[2,64,384]{2,1,0:T(8,128)(2,1)S(1)}, u32[]{:S(2)}, u32[]{:S(2)}) collective-permute-start(bf16[2,64,384]{2,1,0:T(8,128)(2,1)S(1)} %fusion.19), channel_id=1, source_target_pairs={{0,32},{16,48},{32,0},{48,16},{64,96},{80,112},{96,64},{112,80},{1... | collective-permute-start | bytes 294920 | tf_op jit(solution)/shard_map/ppermute | solution.py:29
  115.6 9.3 %collective-permute-start.18 = (bf16[64,384]{1,0:T(8,128)(2,1)S(1)}, bf16[64,384]{1,0:T(8,128)(2,1)S(1)}, u32[]{:S(2)}, u32[]{:S(2)}) collective-permute-start(bf16[64,384]{1,0:T(8,128)(2,1)S(1)} %fusion.23), channel_id=1, source_target_pairs={{0,64},{16,80},{32,96},{48,112},{64,0},{80,16},{96,32},{112,48},{1... | collective-permute-start | bytes 147464 | tf_op jit(solution)/shard_map/ppermute | solution.py:29
  117.6 13.6 %collective-permute-start.15 = (bf16[64,384]{1,0:T(8,128)(2,1)S(1)}, bf16[64,384]{1,0:T(8,128)(2,1)S(1)}, u32[]{:S(2)}, u32[]{:S(2)}) collective-permute-start(bf16[64,384]{1,0:T(8,128)(2,1)S(1)} %fusion.22), channel_id=1, source_target_pairs={{0,64},{16,80},{32,96},{48,112},{64,0},{80,16},{96,32},{112,48},{1... | collective-permute-start | bytes 147464 | tf_op jit(solution)/shard_map/ppermute | solution.py:29

commit v6 on v5

--- a/solution.py
+++ b/solution.py
@@ -10,13 +10,6 @@
 
 def pick(array, index, axis):
     return lax.dynamic_index_in_dim(array, index, axis, keepdims=False)
-
-
-def choose(index, options):
-    out = options[-1]
-    for i in range(len(options) - 1):
-        out = jnp.where(index == i, options[i], out)
-    return out
 
 
 def wait(array, row):
@@ -58,8 +51,8 @@
     other = to_high(normed)
     pair = jnp.where(high == 0, jnp.stack([normed, other]), jnp.stack([other, normed]))
     got = [to_y(pair, step) for step in (1, 2, 3)]
-    ring = [pair, got[2], got[1], got[0]]
-    quad = jnp.stack([choose(y, [ring[(i - j) % NY] for j in range(NY)]) for i in range(NY)])
+    ring = jnp.stack([pair, got[2], got[1], got[0]])
+    quad = lax.dynamic_slice_in_dim(jnp.concatenate([ring, ring]), (NY - y) % NY, NY, 0)
     far = to_core(quad)
     both = jnp.where(core == 0, jnp.stack([quad, far], axis=2), jnp.stack([far, quad], axis=2))
     return both.reshape(16 * rows, depth)
@@ -92,13 +85,17 @@
     near = to_x(wait(part(x + 4 - ahead), early), -1)
     joined = part(x + ahead).astype(F32) + far.astype(F32)
     last = to_x(joined.astype(BF16), 1)
-    return part(x).astype(F32) + near.astype(F32) + last.astype(F32)
+    return part(x), near, last
 
 
-def scatter_z(total, z, bit, axis):
+def scatter_z(terms, z, bit, axis):
     mine = (z // bit) % 2
-    sent = pick(total, 1 - mine, axis).astype(BF16)
-    return pick(total, mine, axis) + to_z(sent, bit).astype(F32)
+
+    def total(index):
+        return sum(pick(term, index, axis).astype(F32) for term in terms)
+
+    sent = total(1 - mine).astype(BF16)
+    return total(mine) + to_z(sent, bit).astype(F32), sent
 
 
 def shards(tokens, masked, mask_vector, gate_weight, up_weight, cotangent):
@@ -129,12 +126,13 @@
     first = lax.dot_general(gate_delta, gate_weight, contract_last, preferred_element_type=F32)
     second = lax.dot_general(up_delta, up_weight, contract_last, preferred_element_type=F32)
     rows, early = scatter_rows((first + second).astype(BF16), y, high, core)
-    total = scatter_x(gate_parts, up_parts, early, x, core)
-    normed_grad = scatter_high(rows, total[0, 0], high)
-    total = total.reshape(2, 2, 2, 2, depth // (NX * NZ), width)
-    gate_grad, up_grad = scatter_z(total[0], z, 1, 2), scatter_z(total[1], z, 1, 2)
-    gate_grad, up_grad = scatter_z(gate_grad, z, 2, 1), scatter_z(up_grad, z, 2, 1)
-    gate_grad, up_grad = scatter_z(gate_grad, z, 4, 0), scatter_z(up_grad, z, 4, 0)
+    terms = scatter_x(gate_parts, up_parts, early, x, core)
+    terms = [term.reshape(2, 2, 2, 2, depth // (NX * NZ), width) for term in terms]
+    gate_grad, _ = scatter_z([term[0] for term in terms], z, 1, 2)
+    up_grad, late = scatter_z([term[1] for term in terms], z, 1, 2)
+    normed_grad = scatter_high(rows, late[0, 0, 0], high)
+    gate_grad, up_grad = scatter_z([gate_grad], z, 2, 1)[0], scatter_z([up_grad], z, 2, 1)[0]
+    gate_grad, up_grad = scatter_z([gate_grad], z, 4, 0)[0], scatter_z([up_grad], z, 4, 0)[0]
     inner = jnp.mean(normed_grad * normed_full, axis=-1, keepdims=True)
     token_grad = jnp.where(flag, 0.0, inverse * (normed_grad - normed_full * inner)).astype(BF16)
     return (hidden, token_grad, gate_grad, up_grad)

time: 134 us -> 129 us (0.963)
  waiting for transfers between devices: 11.6 us -> 16.3 us
  other arithmetic: 18 us -> 13.6 us
  starting transfers between devices: 91.2 us -> 86.9 us
    ppermute x19, waiting for transfers between devices: 11.6 us -> 16.3 us  [move(): lax.ppermute(array, axis_name, [(i, target(i)) for i in range(count)])]
    ppermute x19, starting transfers between devices: 91.2 us -> 86.9 us  [move(): lax.ppermute(array, axis_name, [(i, target(i)) for i in range(count)])]
    select_n x1, other arithmetic: 1.81 us -> 0.11 us  [gather_rows(): jnp.where(core == 0, jnp.stack([quad, far], axis=2), jnp.stack([far, quad...]
    convert_element_type x0 -> x2, other arithmetic: none -> 1.57 us  [scatter_z(): sent = total(1 - mine).astype(BF16)]
    convert_element_type x6 -> x4, local copies, waits for them, and re-layouts: 1.48 us -> 0.08 us  [scatter_z(): sent = total(1 - mine).astype(BF16)]
    add x7 -> x6, other arithmetic: 4.91 us -> 3.62 us  [scatter_z(): return (total(mine) + to_z(sent, bit).astype(F32), sent)]
  transfers between devices with their start and end apart: 19 -> 19, of which waited for: 6 -> 10; matrix products, arithmetic and copies ran while one was open for 12% -> 11% of each run, Pallas kernels for 0% -> 0%
where the time goes in v6:
time: 129 us; the launch traced here: 127 us
  starting transfers between devices  86.9 us (67%)
  waiting for transfers between devices  16.3 us (13%)
  other arithmetic  13.6 us (11%)
  matrix products  5.3 us (4%)
  local copies, waits for them, and re-layouts  3.83 us (3%)
  between operations  1.57 us (1%)
    ppermute x19, starting transfers between devices, move(): lax.ppermute(array, axis_name, [(i, target(i)) for i in range(count)])  86.9 us
    ppermute x19, waiting for transfers between devices, move(): lax.ppermute(array, axis_name, [(i, target(i)) for i in range(count)])  16.3 us
    add x6, other arithmetic, scatter_z(): return (total(mine) + to_z(sent, bit).astype(F32), sent)  3.62 us
  transfers between devices with their start and end apart: 19, of which 10 were waited for; matrix products, arithmetic and copies ran while one was open for 11% of the time, Pallas kernels for 0%

profile of v6, /device:TPU:1, one launch (start us, length us, event | category | flops | bytes accessed | tf_op | source)
XLA Modules:
  0.0 127.5 jit_solution(14039694929855884368)
XLA Ops:
  0.6 0.0 copy-start
  0.6 0.8 broadcast_compare_fusion
  1.4 1.0 fusion.18
  2.5 0.9 fusion.12
  3.4 16.3 %collective-permute-start = (bf16[16,2048]{1,0:T(8,128)(2,1)S(1)}, bf16[16,2048]{1,0:T(8,128)(2,1)S(1)}, u32[]{:S(2)}, u32[]{:S(2)}) collective-permute-start(bf16[16,2048]{1,0:T(8,128)(2,1)S(1)} %fusion.12), channel_id=1, source_target_pairs={{0,2},{1,3},{2,0},{3,1},{4,6},{5,7},{6,4},{7,5},{8,10},{9,11},{10,... | collective-permute-start | bytes 196616 | tf_op jit(solution)/shard_map/ppermute | solution.py:22
  19.7 0.9 fusion.45
  20.6 0.9 fusion.44
  21.7 4.6 %collective-permute-start.1 = (bf16[2,16,2048]{2,1,0:T(8,128)(2,1)S(1)}, bf16[2,16,2048]{2,1,0:T(8,128)(2,1)S(1)}, u32[]{:S(2)}, u32[]{:S(2)}) collective-permute-start(bf16[2,16,2048]{2,1,0:T(8,128)(2,1)S(1)} %maximum_select_fusion.3), channel_id=1, source_target_pairs={{0,12},{1,13},{2,14},{3,15},{4,0},{5,1},{6,2},{7,3},{8,4},{9,5},{1... | collective-permute-start | bytes 393224 | tf_op jit(solution)/shard_map/ppermute | solution.py:22
  26.3 2.3 %collective-permute-start.2 = (bf16[2,16,2048]{2,1,0:T(8,128)(2,1)S(1)}, bf16[2,16,2048]{2,1,0:T(8,128)(2,1)S(1)}, u32[]{:S(2)}, u32[]{:S(2)}) collective-permute-start(bf16[2,16,2048]{2,1,0:T(8,128)(2,1)S(1)} %maximum_select_fusion.3), channel_id=1, source_target_pairs={{0,8},{1,9},{2,10},{3,11},{4,12},{5,13},{6,14},{7,15},{8,0},{9,1},... | collective-permute-start | bytes 393224 | tf_op jit(solution)/shard_map/ppermute | solution.py:22
  28.6 2.6 %collective-permute-start.3 = (bf16[2,16,2048]{2,1,0:T(8,128)(2,1)S(1)}, bf16[2,16,2048]{2,1,0:T(8,128)(2,1)S(1)}, u32[]{:S(2)}, u32[]{:S(2)}) collective-permute-start(bf16[2,16,2048]{2,1,0:T(8,128)(2,1)S(1)} %maximum_select_fusion.3), channel_id=1, source_target_pairs={{0,4},{1,5},{2,6},{3,7},{4,8},{5,9},{6,10},{7,11},{8,12},{9,13},{1... | collective-permute-start | bytes 393224 | tf_op jit(solution)/shard_map/ppermute | solution.py:22
  31.2 2.3 %collective-permute-done.2 = bf16[2,16,2048]{2,1,0:T(8,128)(2,1)S(1)} collective-permute-done((bf16[2,16,2048]{2,1,0:T(8,128)(2,1)S(1)}, bf16[2,16,2048]{2,1,0:T(8,128)(2,1)S(1)}, u32[]{:S(2)}, u32[]{:S(2)}) %collective-permute-start.2) | collective-permute-done | bytes 131104 | tf_op jit(solution)/shard_map/ppermute | solution.py:22
  33.5 2.0 %collective-permute-done.3 = bf16[2,16,2048]{2,1,0:T(8,128)(2,1)S(1)} collective-permute-done((bf16[2,16,2048]{2,1,0:T(8,128)(2,1)S(1)}, bf16[2,16,2048]{2,1,0:T(8,128)(2,1)S(1)}, u32[]{:S(2)}, u32[]{:S(2)}) %collective-permute-start.3) | collective-permute-done | bytes 131104 | tf_op jit(solution)/shard_map/ppermute | solution.py:22
  35.6 0.9 constant_dynamic-slice_fusion.8
  36.5 6.8 %collective-permute-start.4 = (bf16[4,2,16,2048]{3,2,1,0:T(8,128)(2,1)}, bf16[4,2,16,2048]{3,2,1,0:T(8,128)(2,1)S(1)}, u32[]{:S(2)}, u32[]{:S(2)}) collective-permute-start(bf16[4,2,16,2048]{3,2,1,0:T(8,128)(2,1)} %constant_dynamic-slice_fusion.8), channel_id=1, source_target_pairs={{0,1},{1,0},{2,3},{3,2},{4,5},{5,4},{6,7},{7,6},{8,9},{9,8},{10,11... | collective-permute-start | bytes 1572872 | tf_op jit(solution)/shard_map/ppermute | solution.py:22
  43.7 1.4 %collective-permute-done.4 = bf16[4,2,16,2048]{3,2,1,0:T(8,128)(2,1)S(1)} collective-permute-done((bf16[4,2,16,2048]{3,2,1,0:T(8,128)(2,1)}, bf16[4,2,16,2048]{3,2,1,0:T(8,128)(2,1)S(1)}, u32[]{:S(2)}, u32[]{:S(2)}) %collective-permute-start.4) | collective-permute-done | bytes 524320 | tf_op jit(solution)/shard_map/ppermute | solution.py:22
  45.0 0.1 maximum_select_fusion
  45.2 0.7 fusion.31
  45.9 0.2 copy-done.5
  46.1 0.8 convolution_convert_fusion.1
  46.9 1.5 %fusion.3 = (bf16[256,384]{1,0:T(8,128)(2,1)S(1)}, bf16[256,384]{1,0:T(8,128)(2,1)}) fusion(bf16[256,384]{1,0:T(8,128)(2,1)S(1)} %copy-done.5, f32[256,384]{1,0:T(8,128)S(1)} %fusion.31, bf16[256,2048]{1,0:T(8,128)(2,1)S(1)} %bitcast.102, bf16[2048,384]{1,0:T(8,128)(2,1)S(1)} %copy-done), kind=kOutput, calls=%fused_computation.14 | convolution fusion | flops 404029440 | bytes 3604480 | tf_op jit(solution)/shard_map/dot_general | solution.py:114
  48.4 0.7 fusion.32
  49.1 0.8 fusion
  50.0 2.3 %collective-permute-start.5 = (bf16[4,2,16,2048]{3,2,1,0:T(8,128)(2,1)S(1)}, bf16[4,2,16,2048]{3,2,1,0:T(8,128)(2,1)S(1)}, u32[]{:S(2)}, u32[]{:S(2)}) collective-permute-start(bf16[4,2,16,2048]{3,2,1,0:T(8,128)(2,1)S(1)} %dynamic-slice_bitcast_fusion), channel_id=1, source_target_pairs={{0,1},{1,0},{2,3},{3,2},{4,5},{5,4},{6,7},{7,6},{8,9},{9,8},{10,11... | collective-permute-start | bytes 1572872 | tf_op jit(solution)/shard_map/ppermute | solution.py:22
  52.3 0.7 convolution_convert_fusion
  53.0 0.3 constant_dynamic-slice_fusion
  53.4 0.1 pad_maximum_fusion
  53.5 4.4 %collective-permute-start.10 = (bf16[2,512,384]{2,1,0:T(8,128)(2,1)S(1)}, bf16[2,512,384]{2,1,0:T(8,128)(2,1)S(1)}, u32[]{:S(2)}, u32[]{:S(2)}) collective-permute-start(bf16[2,512,384]{2,1,0:T(8,128)(2,1)S(1)} %pad_maximum_fusion), channel_id=1, source_target_pairs={{0,128},{1,385},{2,130},{3,387},{4,132},{5,389},{6,134},{7,391},{8... | collective-permute-start | bytes 2359304 | tf_op jit(solution)/shard_map/ppermute | solution.py:22
  57.9 0.2 fusion.28
  58.1 0.1 maximum_select_fusion.1
  58.2 1.9 %collective-permute-start.9 = (bf16[2,512,384]{2,1,0:T(8,128)(2,1)S(1)}, bf16[2,512,384]{2,1,0:T(8,128)(2,1)S(1)}, u32[]{:S(2)}, u32[]{:S(2)}) collective-permute-start(bf16[2,512,384]{2,1,0:T(8,128)(2,1)S(1)} %maximum_select_fusion.1), channel_id=1, source_target_pairs={{0,384},{1,129},{2,386},{3,131},{4,388},{5,133},{6,390},{7,135},{8... | collective-permute-start | bytes 2359304 | tf_op jit(solution)/shard_map/ppermute | solution.py:22
  60.2 1.9 %collective-permute-start.6 = (bf16[2,16,2048]{2,1,0:T(8,128)(2,1)S(1)}, bf16[2,16,2048]{2,1,0:T(8,128)(2,1)S(1)}, u32[]{:S(2)}, u32[]{:S(2)}) collective-permute-start(bf16[2,16,2048]{2,1,0:T(8,128)(2,1)S(1)} %get-tuple-element.20), channel_id=1, source_target_pairs={{0,4},{1,5},{2,6},{3,7},{4,8},{5,9},{6,10},{7,11},{8,12},{9,13},{1... | collective-permute-start | bytes 393224 | tf_op jit(solution)/shard_map/ppermute | solution.py:22
  62.1 3.3 %collective-permute-start.7 = (bf16[2,16,2048]{2,1,0:T(8,128)(2,1)S(1)}, bf16[2,16,2048]{2,1,0:T(8,128)(2,1)S(1)}, u32[]{:S(2)}, u32[]{:S(2)}) collective-permute-start(bf16[2,16,2048]{2,1,0:T(8,128)(2,1)S(1)} %get-tuple-element.22), channel_id=1, source_target_pairs={{0,8},{1,9},{2,10},{3,11},{4,12},{5,13},{6,14},{7,15},{8,0},{9,1},... | collective-permute-start | bytes 393224 | tf_op jit(solution)/shard_map/ppermute | solution.py:22
  65.4 4.0 %collective-permute-start.8 = (bf16[2,16,2048]{2,1,0:T(8,128)(2,1)S(1)}, bf16[2,16,2048]{2,1,0:T(8,128)(2,1)S(1)}, u32[]{:S(2)}, u32[]{:S(2)}) collective-permute-start(bf16[2,16,2048]{2,1,0:T(8,128)(2,1)S(1)} %get-tuple-element.21), channel_id=1, source_target_pairs={{0,12},{1,13},{2,14},{3,15},{4,0},{5,1},{6,2},{7,3},{8,4},{9,5},{1... | collective-permute-start | bytes 393224 | tf_op jit(solution)/shard_map/ppermute | solution.py:22
  69.4 2.4 %collective-permute-done.10 = bf16[2,512,384]{2,1,0:T(8,128)(2,1)S(1)} collective-permute-done((bf16[2,512,384]{2,1,0:T(8,128)(2,1)S(1)}, bf16[2,512,384]{2,1,0:T(8,128)(2,1)S(1)}, u32[]{:S(2)}, u32[]{:S(2)}) %collective-permute-start.10) | collective-permute-done | bytes 786464 | tf_op jit(solution)/shard_map/ppermute | solution.py:22
  71.8 0.2 add_convert_fusion
  72.1 5.3 %collective-permute-start.11 = (bf16[2,512,384]{2,1,0:T(8,128)(2,1)S(1)}, bf16[2,512,384]{2,1,0:T(8,128)(2,1)S(1)}, u32[]{:S(2)}, u32[]{:S(2)}) collective-permute-start(bf16[2,512,384]{2,1,0:T(8,128)(2,1)S(1)} %add_convert_fusion), channel_id=1, source_target_pairs={{0,128},{1,385},{2,130},{3,387},{4,132},{5,389},{6,134},{7,391},{8... | collective-permute-start | bytes 2359304 | tf_op jit(solution)/shard_map/ppermute | solution.py:22
  77.4 0.1 fusion.7
  77.5 0.6 fusion.21
  78.1 12.8 %collective-permute-start.12 = (bf16[16,2048]{1,0:T(8,128)(2,1)}, bf16[16,2048]{1,0:T(8,128)(2,1)S(1)}, u32[]{:S(2)}, u32[]{:S(2)}) collective-permute-start(bf16[16,2048]{1,0:T(8,128)(2,1)} %fusion.21), channel_id=1, source_target_pairs={{0,2},{1,3},{2,0},{3,1},{4,6},{5,7},{6,4},{7,5},{8,10},{9,11},{10,... | collective-permute-start | bytes 196616 | tf_op jit(solution)/shard_map/ppermute | solution.py:22
  90.9 0.1 fusion.29
  91.0 0.1 fusion.30
  91.1 0.8 fusion.8
  92.0 1.9 %collective-permute-start.16 = (bf16[2,2,64,384]{3,2,1,0:T(8,128)(2,1)}, bf16[2,2,64,384]{3,2,1,0:T(8,128)(2,1)}, u32[]{:S(2)}, u32[]{:S(2)}) collective-permute-start(bf16[2,2,64,384]{3,2,1,0:T(8,128)(2,1)} %fusion.8), channel_id=1, source_target_pairs={{0,16},{16,0},{32,48},{48,32},{64,80},{80,64},{96,112},{112,96},{1... | collective-permute-start | bytes 589832 | tf_op jit(solution)/shard_map/ppermute | solution.py:22
  93.9 0.7 slice_reduce_fusion
  94.6 0.8 fusion.9
  95.4 3.4 %collective-permute-start.13 = (bf16[2,2,64,384]{3,2,1,0:T(8,128)(2,1)}, bf16[2,2,64,384]{3,2,1,0:T(8,128)(2,1)}, u32[]{:S(2)}, u32[]{:S(2)}) collective-permute-start(bf16[2,2,64,384]{3,2,1,0:T(8,128)(2,1)} %fusion.9), channel_id=1, source_target_pairs={{0,16},{16,0},{32,48},{48,32},{64,80},{80,64},{96,112},{112,96},{1... | collective-permute-start | bytes 589832 | tf_op jit(solution)/shard_map/ppermute | solution.py:22
  98.7 0.6 tile.12
  99.3 0.7 slice_compare_fusion
  100.0 0.9 fusion.13
  100.9 1.4 %fusion.17 = bf16[16,2048]{1,0:T(8,128)(2,1)} fusion(f32[2,16,2048]{2,1,0:T(8,128)S(1)} %fusion.7, s32[]{:T(128)S(6)} %select_n.250, f32[16]{0:T(128)S(1)} %broadcast_multiply_fusion, f32[16]{0:T(128)} %copy-done.7, pred[16]{0:T(512)(128)(4,1)S(1)} %broadcast_compare_fusion, bf16[16,2048]{1,0:T(8,128)(2,1)S(1)} %collective-permute-done.12, ...), kind=kLoop, calls=%fused_computation.41 | loop fusion | flops 360448 | bytes 333972 | tf_op jit(solution)/shard_map/convert_element_type | solution.py:137
  102.3 0.5 collective-permute-done.16
  102.8 1.2 bitcast_add_fusion
  104.1 2.5 %collective-permute-start.17 = (bf16[2,64,384]{2,1,0:T(8,128)(2,1)S(1)}, bf16[2,64,384]{2,1,0:T(8,128)(2,1)S(1)}, u32[]{:S(2)}, u32[]{:S(2)}) collective-permute-start(bf16[2,64,384]{2,1,0:T(8,128)(2,1)S(1)} %fusion.20), channel_id=1, source_target_pairs={{0,32},{16,48},{32,0},{48,16},{64,96},{80,112},{96,64},{112,80},{1... | collective-permute-start | bytes 294920 | tf_op jit(solution)/shard_map/ppermute | solution.py:22
  106.6 0.4 collective-permute-done.13
  107.0 1.0 bitcast_add_fusion.1
  108.1 3.3 %collective-permute-start.14 = (bf16[2,64,384]{2,1,0:T(8,128)(2,1)S(1)}, bf16[2,64,384]{2,1,0:T(8,128)(2,1)S(1)}, u32[]{:S(2)}, u32[]{:S(2)}) collective-permute-start(bf16[2,64,384]{2,1,0:T(8,128)(2,1)S(1)} %fusion.19), channel_id=1, source_target_pairs={{0,32},{16,48},{32,0},{48,16},{64,96},{80,112},{96,64},{112,80},{1... | collective-permute-start | bytes 294920 | tf_op jit(solution)/shard_map/ppermute | solution.py:22
  111.4 1.8 %collective-permute-done.17 = bf16[2,64,384]{2,1,0:T(8,128)(2,1)S(1)} collective-permute-done((bf16[2,64,384]{2,1,0:T(8,128)(2,1)S(1)}, bf16[2,64,384]{2,1,0:T(8,128)(2,1)S(1)}, u32[]{:S(2)}, u32[]{:S(2)}) %collective-permute-start.17) | collective-permute-done | bytes 98336 | tf_op jit(solution)/shard_map/ppermute | solution.py:22
  113.2 1.9 %collective-permute-start.18 = (bf16[64,384]{1,0:T(8,128)(2,1)S(1)}, bf16[64,384]{1,0:T(8,128)(2,1)S(1)}, u32[]{:S(2)}, u32[]{:S(2)}) collective-permute-start(bf16[64,384]{1,0:T(8,128)(2,1)S(1)} %fusion.23), channel_id=1, source_target_pairs={{0,64},{16,80},{32,96},{48,112},{64,0},{80,16},{96,32},{112,48},{1... | collective-permute-start | bytes 147464 | tf_op jit(solution)/shard_map/ppermute | solution.py:22
  115.1 1.9 %collective-permute-done.14 = bf16[2,64,384]{2,1,0:T(8,128)(2,1)S(1)} collective-permute-done((bf16[2,64,384]{2,1,0:T(8,128)(2,1)S(1)}, bf16[2,64,384]{2,1,0:T(8,128)(2,1)S(1)}, u32[]{:S(2)}, u32[]{:S(2)}) %collective-permute-start.14) | collective-permute-done | bytes 98336 | tf_op jit(solution)/shard_map/ppermute | solution.py:22
  117.1 5.4 %collective-permute-start.15 = (bf16[64,384]{1,0:T(8,128)(2,1)S(1)}, bf16[64,384]{1,0:T(8,128)(2,1)S(1)}, u32[]{:S(2)}, u32[]{:S(2)}) collective-permute-start(bf16[64,384]{1,0:T(8,128)(2,1)S(1)} %fusion.22), channel_id=1, source_target_pairs={{0,64},{16,80},{32,96},{48,112},{64,0},{80,16},{96,32},{112,48},{1... | collective-permute-start | bytes 147464 | tf_op jit(solution)/shard_map/ppermute | solution.py:22
  122.5 1.8 %collective-permute-done.18 = bf16[64,384]{1,0:T(8,128)(2,1)S(1)} collective-permute-done((bf16[64,384]{1,0:T(8,128)(2,1)S(1)}, bf16[64,384]{1,0:T(8,128)(2,1)S(1)}, u32[]{:S(2)}, u32[]{:S(2)}) %collective-permute-start.18) | collective-permute-done | bytes 49184 | tf_op jit(solution)/shard_map/ppermute | solution.py:22
  124.3 0.7 bitcast_add_fusion.6
  125.0 1.9 %collective-permute-done.15 = bf16[64,384]{1,0:T(8,128)(2,1)S(1)} collective-permute-done((bf16[64,384]{1,0:T(8,128)(2,1)S(1)}, bf16[64,384]{1,0:T(8,128)(2,1)S(1)}, u32[]{:S(2)}, u32[]{:S(2)}) %collective-permute-start.15) | collective-permute-done | bytes 49184 | tf_op jit(solution)/shard_map/ppermute | solution.py:22
  126.8 0.7 bitcast_add_fusion.7
  (45 shorter events, 0.5 us)
Async XLA Ops:
  0.6 46.3 %copy-start = (bf16[2048,384]{1,0:T(8,128)(2,1)S(1)}, bf16[2048,384]{1,0:T(8,128)(2,1)}, u32[]{:S(2)}) copy-start(bf16[2048,384]{1,0:T(8,128)(2,1)} %param.10) | copy-start | bytes 4718596
  2.5 19.2 %copy-start.7 = (f32[16]{0:T(128)}, f32[16]{0:T(128)S(1)}, u32[]{:S(2)}) copy-start(f32[16]{0:T(128)S(1)} %add_rsqrt_fusion) | copy-start | bytes 196
  3.4 18.2 %collective-permute-start = (bf16[16,2048]{1,0:T(8,128)(2,1)S(1)}, bf16[16,2048]{1,0:T(8,128)(2,1)S(1)}, u32[]{:S(2)}, u32[]{:S(2)}) collective-permute-start(bf16[16,2048]{1,0:T(8,128)(2,1)S(1)} %fusion.12), channel_id=1, source_target_pairs={{0,2},{1,3},{2,0},{3,1},{4,6},{5,7},{6,4},{7,5},{8,10},{9,11},{10,... | collective-permute-start | bytes 196616 | tf_op jit(solution)/shard_map/ppermute | solution.py:22
  21.7 9.6 %collective-permute-start.1 = (bf16[2,16,2048]{2,1,0:T(8,128)(2,1)S(1)}, bf16[2,16,2048]{2,1,0:T(8,128)(2,1)S(1)}, u32[]{:S(2)}, u32[]{:S(2)}) collective-permute-start(bf16[2,16,2048]{2,1,0:T(8,128)(2,1)S(1)} %maximum_select_fusion.3), channel_id=1, source_target_pairs={{0,12},{1,13},{2,14},{3,15},{4,0},{5,1},{6,2},{7,3},{8,4},{9,5},{1... | collective-permute-start | bytes 393224 | tf_op jit(solution)/shard_map/ppermute | solution.py:22
  26.3 7.2 %collective-permute-start.2 = (bf16[2,16,2048]{2,1,0:T(8,128)(2,1)S(1)}, bf16[2,16,2048]{2,1,0:T(8,128)(2,1)S(1)}, u32[]{:S(2)}, u32[]{:S(2)}) collective-permute-start(bf16[2,16,2048]{2,1,0:T(8,128)(2,1)S(1)} %maximum_select_fusion.3), channel_id=1, source_target_pairs={{0,8},{1,9},{2,10},{3,11},{4,12},{5,13},{6,14},{7,15},{8,0},{9,1},... | collective-permute-start | bytes 393224 | tf_op jit(solution)/shard_map/ppermute | solution.py:22
  28.6 6.9 %collective-permute-start.3 = (bf16[2,16,2048]{2,1,0:T(8,128)(2,1)S(1)}, bf16[2,16,2048]{2,1,0:T(8,128)(2,1)S(1)}, u32[]{:S(2)}, u32[]{:S(2)}) collective-permute-start(bf16[2,16,2048]{2,1,0:T(8,128)(2,1)S(1)} %maximum_select_fusion.3), channel_id=1, source_target_pairs={{0,4},{1,5},{2,6},{3,7},{4,8},{5,9},{6,10},{7,11},{8,12},{9,13},{1... | collective-permute-start | bytes 393224 | tf_op jit(solution)/shard_map/ppermute | solution.py:22
  36.5 8.6 %collective-permute-start.4 = (bf16[4,2,16,2048]{3,2,1,0:T(8,128)(2,1)}, bf16[4,2,16,2048]{3,2,1,0:T(8,128)(2,1)S(1)}, u32[]{:S(2)}, u32[]{:S(2)}) collective-permute-start(bf16[4,2,16,2048]{3,2,1,0:T(8,128)(2,1)} %constant_dynamic-slice_fusion.8), channel_id=1, source_target_pairs={{0,1},{1,0},{2,3},{3,2},{4,5},{5,4},{6,7},{7,6},{8,9},{9,8},{10,11... | collective-permute-start | bytes 1572872 | tf_op jit(solution)/shard_map/ppermute | solution.py:22
  43.6 1.5 %copy-start.1 = (bf16[2048,384]{1,0:T(8,128)(2,1)S(1)}, bf16[2048,384]{1,0:T(8,128)(2,1)}, u32[]{:S(2)}) copy-start(bf16[2048,384]{1,0:T(8,128)(2,1)} %param.9) | copy-start | bytes 4718596
  45.1 0.9 copy-start.5
  50.0 7.9 %collective-permute-start.5 = (bf16[4,2,16,2048]{3,2,1,0:T(8,128)(2,1)S(1)}, bf16[4,2,16,2048]{3,2,1,0:T(8,128)(2,1)S(1)}, u32[]{:S(2)}, u32[]{:S(2)}) collective-permute-start(bf16[4,2,16,2048]{3,2,1,0:T(8,128)(2,1)S(1)} %dynamic-slice_bitcast_fusion), channel_id=1, source_target_pairs={{0,1},{1,0},{2,3},{3,2},{4,5},{5,4},{6,7},{7,6},{8,9},{9,8},{10,11... | collective-permute-start | bytes 1572872 | tf_op jit(solution)/shard_map/ppermute | solution.py:22
  53.5 18.4 %collective-permute-start.10 = (bf16[2,512,384]{2,1,0:T(8,128)(2,1)S(1)}, bf16[2,512,384]{2,1,0:T(8,128)(2,1)S(1)}, u32[]{:S(2)}, u32[]{:S(2)}) collective-permute-start(bf16[2,512,384]{2,1,0:T(8,128)(2,1)S(1)} %pad_maximum_fusion), channel_id=1, source_target_pairs={{0,128},{1,385},{2,130},{3,387},{4,132},{5,389},{6,134},{7,391},{8... | collective-permute-start | bytes 2359304 | tf_op jit(solution)/shard_map/ppermute | solution.py:22
  58.2 32.7 %collective-permute-start.9 = (bf16[2,512,384]{2,1,0:T(8,128)(2,1)S(1)}, bf16[2,512,384]{2,1,0:T(8,128)(2,1)S(1)}, u32[]{:S(2)}, u32[]{:S(2)}) collective-permute-start(bf16[2,512,384]{2,1,0:T(8,128)(2,1)S(1)} %maximum_select_fusion.1), channel_id=1, source_target_pairs={{0,384},{1,129},{2,386},{3,131},{4,388},{5,133},{6,390},{7,135},{8... | collective-permute-start | bytes 2359304 | tf_op jit(solution)/shard_map/ppermute | solution.py:22
  60.2 17.2 %collective-permute-start.6 = (bf16[2,16,2048]{2,1,0:T(8,128)(2,1)S(1)}, bf16[2,16,2048]{2,1,0:T(8,128)(2,1)S(1)}, u32[]{:S(2)}, u32[]{:S(2)}) collective-permute-start(bf16[2,16,2048]{2,1,0:T(8,128)(2,1)S(1)} %get-tuple-element.20), channel_id=1, source_target_pairs={{0,4},{1,5},{2,6},{3,7},{4,8},{5,9},{6,10},{7,11},{8,12},{9,13},{1... | collective-permute-start | bytes 393224 | tf_op jit(solution)/shard_map/ppermute | solution.py:22
  62.1 15.3 %collective-permute-start.7 = (bf16[2,16,2048]{2,1,0:T(8,128)(2,1)S(1)}, bf16[2,16,2048]{2,1,0:T(8,128)(2,1)S(1)}, u32[]{:S(2)}, u32[]{:S(2)}) collective-permute-start(bf16[2,16,2048]{2,1,0:T(8,128)(2,1)S(1)} %get-tuple-element.22), channel_id=1, source_target_pairs={{0,8},{1,9},{2,10},{3,11},{4,12},{5,13},{6,14},{7,15},{8,0},{9,1},... | collective-permute-start | bytes 393224 | tf_op jit(solution)/shard_map/ppermute | solution.py:22
  65.4 12.0 %collective-permute-start.8 = (bf16[2,16,2048]{2,1,0:T(8,128)(2,1)S(1)}, bf16[2,16,2048]{2,1,0:T(8,128)(2,1)S(1)}, u32[]{:S(2)}, u32[]{:S(2)}) collective-permute-start(bf16[2,16,2048]{2,1,0:T(8,128)(2,1)S(1)} %get-tuple-element.21), channel_id=1, source_target_pairs={{0,12},{1,13},{2,14},{3,15},{4,0},{5,1},{6,2},{7,3},{8,4},{9,5},{1... | collective-permute-start | bytes 393224 | tf_op jit(solution)/shard_map/ppermute | solution.py:22
  72.1 19.0 %collective-permute-start.11 = (bf16[2,512,384]{2,1,0:T(8,128)(2,1)S(1)}, bf16[2,512,384]{2,1,0:T(8,128)(2,1)S(1)}, u32[]{:S(2)}, u32[]{:S(2)}) collective-permute-start(bf16[2,512,384]{2,1,0:T(8,128)(2,1)S(1)} %add_convert_fusion), channel_id=1, source_target_pairs={{0,128},{1,385},{2,130},{3,387},{4,132},{5,389},{6,134},{7,391},{8... | collective-permute-start | bytes 2359304 | tf_op jit(solution)/shard_map/ppermute | solution.py:22
  78.1 21.9 %collective-permute-start.12 = (bf16[16,2048]{1,0:T(8,128)(2,1)}, bf16[16,2048]{1,0:T(8,128)(2,1)S(1)}, u32[]{:S(2)}, u32[]{:S(2)}) collective-permute-start(bf16[16,2048]{1,0:T(8,128)(2,1)} %fusion.21), channel_id=1, source_target_pairs={{0,2},{1,3},{2,0},{3,1},{4,6},{5,7},{6,4},{7,5},{8,10},{9,11},{10,... | collective-permute-start | bytes 196616 | tf_op jit(solution)/shard_map/ppermute | solution.py:22
  91.0 4.4 %copy-start.3 = (bf16[1,512,384]{2,1,0:T(8,128)(2,1)}, bf16[1,512,384]{2,1,0:T(8,128)(2,1)S(1)}, u32[]{:S(2)}) copy-start(bf16[1,512,384]{2,1,0:T(8,128)(2,1)S(1)} %get-tuple-element.15) | copy-start | bytes 1179652
  91.0 9.0 %copy-start.2 = (bf16[16,2048]{1,0:T(8,128)(2,1)S(1)}, bf16[16,2048]{1,0:T(8,128)(2,1)}, u32[]{:S(2)}) copy-start(bf16[16,2048]{1,0:T(8,128)(2,1)} %param.6) | copy-start | bytes 196612
  91.0 9.0 %copy-start.6 = (bf16[2048]{0:T(1024)(128)(2,1)S(1)}, bf16[2048]{0:T(1024)(128)(2,1)}, u32[]{:S(2)}) copy-start(bf16[2048]{0:T(1024)(128)(2,1)} %param.8) | copy-start | bytes 12292
  91.1 7.6 %copy-start.4 = (bf16[1,512,384]{2,1,0:T(8,128)(2,1)}, bf16[1,512,384]{2,1,0:T(8,128)(2,1)S(1)}, u32[]{:S(2)}) copy-start(bf16[1,512,384]{2,1,0:T(8,128)(2,1)S(1)} %get-tuple-element.17) | copy-start | bytes 1179652
  92.0 10.9 %collective-permute-start.16 = (bf16[2,2,64,384]{3,2,1,0:T(8,128)(2,1)}, bf16[2,2,64,384]{3,2,1,0:T(8,128)(2,1)}, u32[]{:S(2)}, u32[]{:S(2)}) collective-permute-start(bf16[2,2,64,384]{3,2,1,0:T(8,128)(2,1)} %fusion.8), channel_id=1, source_target_pairs={{0,16},{16,0},{32,48},{48,32},{64,80},{80,64},{96,112},{112,96},{1... | collective-permute-start | bytes 589832 | tf_op jit(solution)/shard_map/ppermute | solution.py:22
  95.4 11.7 %collective-permute-start.13 = (bf16[2,2,64,384]{3,2,1,0:T(8,128)(2,1)}, bf16[2,2,64,384]{3,2,1,0:T(8,128)(2,1)}, u32[]{:S(2)}, u32[]{:S(2)}) collective-permute-start(bf16[2,2,64,384]{3,2,1,0:T(8,128)(2,1)} %fusion.9), channel_id=1, source_target_pairs={{0,16},{16,0},{32,48},{48,32},{64,80},{80,64},{96,112},{112,96},{1... | collective-permute-start | bytes 589832 | tf_op jit(solution)/shard_map/ppermute | solution.py:22
  104.1 9.1 %collective-permute-start.17 = (bf16[2,64,384]{2,1,0:T(8,128)(2,1)S(1)}, bf16[2,64,384]{2,1,0:T(8,128)(2,1)S(1)}, u32[]{:S(2)}, u32[]{:S(2)}) collective-permute-start(bf16[2,64,384]{2,1,0:T(8,128)(2,1)S(1)} %fusion.20), channel_id=1, source_target_pairs={{0,32},{16,48},{32,0},{48,16},{64,96},{80,112},{96,64},{112,80},{1... | collective-permute-start | bytes 294920 | tf_op jit(solution)/shard_map/ppermute | solution.py:22
  108.1 8.9 %collective-permute-start.14 = (bf16[2,64,384]{2,1,0:T(8,128)(2,1)S(1)}, bf16[2,64,384]{2,1,0:T(8,128)(2,1)S(1)}, u32[]{:S(2)}, u32[]{:S(2)}) collective-permute-start(bf16[2,64,384]{2,1,0:T(8,128)(2,1)S(1)} %fusion.19), channel_id=1, source_target_pairs={{0,32},{16,48},{32,0},{48,16},{64,96},{80,112},{96,64},{112,80},{1... | collective-permute-start | bytes 294920 | tf_op jit(solution)/shard_map/ppermute | solution.py:22
  113.2 11.1 %collective-permute-start.18 = (bf16[64,384]{1,0:T(8,128)(2,1)S(1)}, bf16[64,384]{1,0:T(8,128)(2,1)S(1)}, u32[]{:S(2)}, u32[]{:S(2)}) collective-permute-start(bf16[64,384]{1,0:T(8,128)(2,1)S(1)} %fusion.23), channel_id=1, source_target_pairs={{0,64},{16,80},{32,96},{48,112},{64,0},{80,16},{96,32},{112,48},{1... | collective-permute-start | bytes 147464 | tf_op jit(solution)/shard_map/ppermute | solution.py:22
  117.1 9.8 %collective-permute-start.15 = (bf16[64,384]{1,0:T(8,128)(2,1)S(1)}, bf16[64,384]{1,0:T(8,128)(2,1)S(1)}, u32[]{:S(2)}, u32[]{:S(2)}) collective-permute-start(bf16[64,384]{1,0:T(8,128)(2,1)S(1)} %fusion.22), channel_id=1, source_target_pairs={{0,64},{16,80},{32,96},{48,112},{64,0},{80,16},{96,32},{112,48},{1... | collective-permute-start | bytes 147464 | tf_op jit(solution)/shard_map/ppermute | solution.py:22

commit v7 on v6

--- a/solution.py
+++ b/solution.py
@@ -128,9 +128,9 @@
     rows, early = scatter_rows((first + second).astype(BF16), y, high, core)
     terms = scatter_x(gate_parts, up_parts, early, x, core)
     terms = [term.reshape(2, 2, 2, 2, depth // (NX * NZ), width) for term in terms]
-    gate_grad, _ = scatter_z([term[0] for term in terms], z, 1, 2)
-    up_grad, late = scatter_z([term[1] for term in terms], z, 1, 2)
-    normed_grad = scatter_high(rows, late[0, 0, 0], high)
+    total, late = scatter_z(terms, z, 1, 3)
+    normed_grad = scatter_high(rows, late[0, 0, 0, 0], high)
+    gate_grad, up_grad = total[0], total[1]
     gate_grad, up_grad = scatter_z([gate_grad], z, 2, 1)[0], scatter_z([up_grad], z, 2, 1)[0]
     gate_grad, up_grad = scatter_z([gate_grad], z, 4, 0)[0], scatter_z([up_grad], z, 4, 0)[0]
     inner = jnp.mean(normed_grad * normed_full, axis=-1, keepdims=True)

time: 129 us -> 132 us (1.023)
  waiting for transfers between devices: 16.3 us -> 24.2 us
  starting transfers between devices: 86.9 us -> 83.6 us
    ppermute x19 -> x18, waiting for transfers between devices: 16.3 us -> 24.2 us  [move(): lax.ppermute(array, axis_name, [(i, target(i)) for i in range(count)])]
    ppermute x19 -> x18, starting transfers between devices: 86.9 us -> 83.6 us  [move(): lax.ppermute(array, axis_name, [(i, target(i)) for i in range(count)])]
    add x6 -> x5, other arithmetic: 3.62 us -> 2.64 us  [scatter_z(): return (total(mine) + to_z(sent, bit).astype(F32), sent)]
  transfers between devices with their start and end apart: 19 -> 18, of which waited for: 10 -> 9; matrix products, arithmetic and copies ran while one was open for 11% -> 9% of each run, Pallas kernels for 0% -> 0%
where the time goes in v7:
time: 132 us; the launch traced here: 131 us
  starting transfers between devices  83.6 us (63%)
  waiting for transfers between devices  24.2 us (18%)
  other arithmetic  13.1 us (10%)
  matrix products  5.28 us (4%)
  local copies, waits for them, and re-layouts  3.68 us (3%)
  between operations  1.54 us (1%)
    ppermute x18, starting transfers between devices, move(): lax.ppermute(array, axis_name, [(i, target(i)) for i in range(count)])  83.6 us
    ppermute x18, waiting for transfers between devices, move(): lax.ppermute(array, axis_name, [(i, target(i)) for i in range(count)])  24.2 us
    add x5, other arithmetic, scatter_z(): return (total(mine) + to_z(sent, bit).astype(F32), sent)  2.64 us
  transfers between devices with their start and end apart: 18, of which 9 were waited for; matrix products, arithmetic and copies ran while one was open for 9% of the time, Pallas kernels for 0%

profile of v7, /device:TPU:1, one launch (start us, length us, event | category | flops | bytes accessed | tf_op | source)
XLA Modules:
  0.0 131.3 jit_solution(12382269287434473209)
XLA Ops:
  0.6 0.0 copy-start
  0.6 0.8 broadcast_compare_fusion
  1.4 1.0 fusion.17
  2.5 0.9 fusion.11
  3.4 16.3 %collective-permute-start = (bf16[16,2048]{1,0:T(8,128)(2,1)S(1)}, bf16[16,2048]{1,0:T(8,128)(2,1)S(1)}, u32[]{:S(2)}, u32[]{:S(2)}) collective-permute-start(bf16[16,2048]{1,0:T(8,128)(2,1)S(1)} %fusion.11), channel_id=1, source_target_pairs={{0,2},{1,3},{2,0},{3,1},{4,6},{5,7},{6,4},{7,5},{8,10},{9,11},{10,... | collective-permute-start | bytes 196616 | tf_op jit(solution)/shard_map/ppermute | solution.py:22
  19.7 0.9 fusion.43
  20.6 0.9 fusion.42
  21.6 4.6 %collective-permute-start.1 = (bf16[2,16,2048]{2,1,0:T(8,128)(2,1)S(1)}, bf16[2,16,2048]{2,1,0:T(8,128)(2,1)S(1)}, u32[]{:S(2)}, u32[]{:S(2)}) collective-permute-start(bf16[2,16,2048]{2,1,0:T(8,128)(2,1)S(1)} %maximum_select_fusion.3), channel_id=1, source_target_pairs={{0,12},{1,13},{2,14},{3,15},{4,0},{5,1},{6,2},{7,3},{8,4},{9,5},{1... | collective-permute-start | bytes 393224 | tf_op jit(solution)/shard_map/ppermute | solution.py:22
  26.3 2.3 %collective-permute-start.2 = (bf16[2,16,2048]{2,1,0:T(8,128)(2,1)S(1)}, bf16[2,16,2048]{2,1,0:T(8,128)(2,1)S(1)}, u32[]{:S(2)}, u32[]{:S(2)}) collective-permute-start(bf16[2,16,2048]{2,1,0:T(8,128)(2,1)S(1)} %maximum_select_fusion.3), channel_id=1, source_target_pairs={{0,8},{1,9},{2,10},{3,11},{4,12},{5,13},{6,14},{7,15},{8,0},{9,1},... | collective-permute-start | bytes 393224 | tf_op jit(solution)/shard_map/ppermute | solution.py:22
  28.6 2.6 %collective-permute-start.3 = (bf16[2,16,2048]{2,1,0:T(8,128)(2,1)S(1)}, bf16[2,16,2048]{2,1,0:T(8,128)(2,1)S(1)}, u32[]{:S(2)}, u32[]{:S(2)}) collective-permute-start(bf16[2,16,2048]{2,1,0:T(8,128)(2,1)S(1)} %maximum_select_fusion.3), channel_id=1, source_target_pairs={{0,4},{1,5},{2,6},{3,7},{4,8},{5,9},{6,10},{7,11},{8,12},{9,13},{1... | collective-permute-start | bytes 393224 | tf_op jit(solution)/shard_map/ppermute | solution.py:22
  31.2 2.3 %collective-permute-done.2 = bf16[2,16,2048]{2,1,0:T(8,128)(2,1)S(1)} collective-permute-done((bf16[2,16,2048]{2,1,0:T(8,128)(2,1)S(1)}, bf16[2,16,2048]{2,1,0:T(8,128)(2,1)S(1)}, u32[]{:S(2)}, u32[]{:S(2)}) %collective-permute-start.2) | collective-permute-done | bytes 131104 | tf_op jit(solution)/shard_map/ppermute | solution.py:22
  33.5 2.0 %collective-permute-done.3 = bf16[2,16,2048]{2,1,0:T(8,128)(2,1)S(1)} collective-permute-done((bf16[2,16,2048]{2,1,0:T(8,128)(2,1)S(1)}, bf16[2,16,2048]{2,1,0:T(8,128)(2,1)S(1)}, u32[]{:S(2)}, u32[]{:S(2)}) %collective-permute-start.3) | collective-permute-done | bytes 131104 | tf_op jit(solution)/shard_map/ppermute | solution.py:22
  35.6 0.8 constant_dynamic-slice_fusion.8
  36.4 6.8 %collective-permute-start.4 = (bf16[4,2,16,2048]{3,2,1,0:T(8,128)(2,1)}, bf16[4,2,16,2048]{3,2,1,0:T(8,128)(2,1)S(1)}, u32[]{:S(2)}, u32[]{:S(2)}) collective-permute-start(bf16[4,2,16,2048]{3,2,1,0:T(8,128)(2,1)} %constant_dynamic-slice_fusion.8), channel_id=1, source_target_pairs={{0,1},{1,0},{2,3},{3,2},{4,5},{5,4},{6,7},{7,6},{8,9},{9,8},{10,11... | collective-permute-start | bytes 1572872 | tf_op jit(solution)/shard_map/ppermute | solution.py:22
  43.6 0.0 copy-start.1
  43.6 1.4 %collective-permute-done.4 = bf16[4,2,16,2048]{3,2,1,0:T(8,128)(2,1)S(1)} collective-permute-done((bf16[4,2,16,2048]{3,2,1,0:T(8,128)(2,1)}, bf16[4,2,16,2048]{3,2,1,0:T(8,128)(2,1)S(1)}, u32[]{:S(2)}, u32[]{:S(2)}) %collective-permute-start.4) | collective-permute-done | bytes 524320 | tf_op jit(solution)/shard_map/ppermute | solution.py:22
  45.0 0.1 maximum_select_fusion
  45.1 0.0 copy-start.3
  45.1 0.7 fusion.29
  45.9 0.2 copy-done.3
  46.0 0.8 convolution_convert_fusion
  46.9 1.5 %fusion.3 = (bf16[256,384]{1,0:T(8,128)(2,1)S(1)}, bf16[256,384]{1,0:T(8,128)(2,1)}) fusion(bf16[256,384]{1,0:T(8,128)(2,1)S(1)} %copy-done.3, f32[256,384]{1,0:T(8,128)S(1)} %fusion.29, bf16[256,2048]{1,0:T(8,128)(2,1)S(1)} %bitcast.89, bf16[2048,384]{1,0:T(8,128)(2,1)S(1)} %copy-done), kind=kOutput, calls=%fused_computation.17 | convolution fusion | flops 404029440 | bytes 3604480 | tf_op jit(solution)/shard_map/dot_general | solution.py:114
  48.3 0.7 fusion.30
  49.1 0.8 fusion
  49.9 2.3 %collective-permute-start.5 = (bf16[4,2,16,2048]{3,2,1,0:T(8,128)(2,1)S(1)}, bf16[4,2,16,2048]{3,2,1,0:T(8,128)(2,1)S(1)}, u32[]{:S(2)}, u32[]{:S(2)}) collective-permute-start(bf16[4,2,16,2048]{3,2,1,0:T(8,128)(2,1)S(1)} %dynamic-slice_bitcast_fusion), channel_id=1, source_target_pairs={{0,1},{1,0},{2,3},{3,2},{4,5},{5,4},{6,7},{7,6},{8,9},{9,8},{10,11... | collective-permute-start | bytes 1572872 | tf_op jit(solution)/shard_map/ppermute | solution.py:22
  52.2 0.8 convolution_convert_fusion.1
  53.0 0.3 constant_dynamic-slice_fusion.6
  53.3 0.1 pad_maximum_fusion.1
  53.4 4.4 %collective-permute-start.10 = (bf16[2,512,384]{2,1,0:T(8,128)(2,1)S(1)}, bf16[2,512,384]{2,1,0:T(8,128)(2,1)S(1)}, u32[]{:S(2)}, u32[]{:S(2)}) collective-permute-start(bf16[2,512,384]{2,1,0:T(8,128)(2,1)S(1)} %pad_maximum_fusion.1), channel_id=1, source_target_pairs={{0,128},{1,385},{2,130},{3,387},{4,132},{5,389},{6,134},{7,391},{8... | collective-permute-start | bytes 2359304 | tf_op jit(solution)/shard_map/ppermute | solution.py:22
  57.8 0.2 fusion.27
  58.0 0.1 maximum_select_fusion.1
  58.1 1.9 %collective-permute-start.9 = (bf16[2,512,384]{2,1,0:T(8,128)(2,1)S(1)}, bf16[2,512,384]{2,1,0:T(8,128)(2,1)S(1)}, u32[]{:S(2)}, u32[]{:S(2)}) collective-permute-start(bf16[2,512,384]{2,1,0:T(8,128)(2,1)S(1)} %maximum_select_fusion.1), channel_id=1, source_target_pairs={{0,384},{1,129},{2,386},{3,131},{4,388},{5,133},{6,390},{7,135},{8... | collective-permute-start | bytes 2359304 | tf_op jit(solution)/shard_map/ppermute | solution.py:22
  60.1 1.9 %collective-permute-start.6 = (bf16[2,16,2048]{2,1,0:T(8,128)(2,1)S(1)}, bf16[2,16,2048]{2,1,0:T(8,128)(2,1)S(1)}, u32[]{:S(2)}, u32[]{:S(2)}) collective-permute-start(bf16[2,16,2048]{2,1,0:T(8,128)(2,1)S(1)} %get-tuple-element.18), channel_id=1, source_target_pairs={{0,4},{1,5},{2,6},{3,7},{4,8},{5,9},{6,10},{7,11},{8,12},{9,13},{1... | collective-permute-start | bytes 393224 | tf_op jit(solution)/shard_map/ppermute | solution.py:22
  62.0 3.3 %collective-permute-start.7 = (bf16[2,16,2048]{2,1,0:T(8,128)(2,1)S(1)}, bf16[2,16,2048]{2,1,0:T(8,128)(2,1)S(1)}, u32[]{:S(2)}, u32[]{:S(2)}) collective-permute-start(bf16[2,16,2048]{2,1,0:T(8,128)(2,1)S(1)} %get-tuple-element.20), channel_id=1, source_target_pairs={{0,8},{1,9},{2,10},{3,11},{4,12},{5,13},{6,14},{7,15},{8,0},{9,1},... | collective-permute-start | bytes 393224 | tf_op jit(solution)/shard_map/ppermute | solution.py:22
  65.4 4.0 %collective-permute-start.8 = (bf16[2,16,2048]{2,1,0:T(8,128)(2,1)S(1)}, bf16[2,16,2048]{2,1,0:T(8,128)(2,1)S(1)}, u32[]{:S(2)}, u32[]{:S(2)}) collective-permute-start(bf16[2,16,2048]{2,1,0:T(8,128)(2,1)S(1)} %get-tuple-element.19), channel_id=1, source_target_pairs={{0,12},{1,13},{2,14},{3,15},{4,0},{5,1},{6,2},{7,3},{8,4},{9,5},{1... | collective-permute-start | bytes 393224 | tf_op jit(solution)/shard_map/ppermute | solution.py:22
  69.3 2.4 %collective-permute-done.10 = bf16[2,512,384]{2,1,0:T(8,128)(2,1)S(1)} collective-permute-done((bf16[2,512,384]{2,1,0:T(8,128)(2,1)S(1)}, bf16[2,512,384]{2,1,0:T(8,128)(2,1)S(1)}, u32[]{:S(2)}, u32[]{:S(2)}) %collective-permute-start.10) | collective-permute-done | bytes 786464 | tf_op jit(solution)/shard_map/ppermute | solution.py:22
  71.7 0.2 add_convert_fusion
  72.0 5.3 %collective-permute-start.11 = (bf16[2,512,384]{2,1,0:T(8,128)(2,1)S(1)}, bf16[2,512,384]{2,1,0:T(8,128)(2,1)}, u32[]{:S(2)}, u32[]{:S(2)}) collective-permute-start(bf16[2,512,384]{2,1,0:T(8,128)(2,1)S(1)} %add_convert_fusion), channel_id=1, source_target_pairs={{0,128},{1,385},{2,130},{3,387},{4,132},{5,389},{6,134},{7,391},{8... | collective-permute-start | bytes 2359304 | tf_op jit(solution)/shard_map/ppermute | solution.py:22
  77.3 0.1 pad_maximum_fusion
  77.4 0.0 copy-start.2
  77.4 0.0 copy-start.4
  77.4 0.1 fusion.8
  77.5 0.6 fusion.20
  78.2 12.8 %collective-permute-start.12 = (bf16[16,2048]{1,0:T(8,128)(2,1)}, bf16[16,2048]{1,0:T(8,128)(2,1)S(1)}, u32[]{:S(2)}, u32[]{:S(2)}) collective-permute-start(bf16[16,2048]{1,0:T(8,128)(2,1)} %fusion.20), channel_id=1, source_target_pairs={{0,2},{1,3},{2,0},{3,1},{4,6},{5,7},{6,4},{7,5},{8,10},{9,11},{10,... | collective-permute-start | bytes 196616 | tf_op jit(solution)/shard_map/ppermute | solution.py:22
  91.0 1.9 %fusion.6 = bf16[2,2,2,64,384]{4,3,2,1,0:T(8,128)(2,1)} fusion(bf16[2,2,2,2,64,384]{5,4,3,2,1,0:T(8,128)(2,1)} %bitcast.22, s32[]{:T(128)S(6)} %select_n.247, bf16[2,2,2,2,64,384]{5,4,3,2,1,0:T(8,128)(2,1)S(1)} %bitcast.97, bf16[2,2,2,2,64,384]{5,4,3,2,1,0:T(8,128)(2,1)S(1)} %bitcast.94), kind=kLoop, calls=%fused_computation.20 | loop fusion | flops 1179648 | bytes 1572868 | tf_op jit(solution)/shard_map/convert_element_type | solution.py:97
  92.9 1.9 %collective-permute-start.13 = (bf16[2,2,2,64,384]{4,3,2,1,0:T(8,128)(2,1)}, bf16[2,2,2,64,384]{4,3,2,1,0:T(8,128)(2,1)}, u32[]{:S(2)}, u32[]{:S(2)}) collective-permute-start(bf16[2,2,2,64,384]{4,3,2,1,0:T(8,128)(2,1)} %fusion.6), channel_id=1, source_target_pairs={{0,16},{16,0},{32,48},{48,32},{64,80},{80,64},{96,112},{112,96},{1... | collective-permute-start | bytes 1179656 | tf_op jit(solution)/shard_map/ppermute | solution.py:22
  94.8 0.7 slice_reduce_fusion
  95.5 0.6 tile.12
  96.1 0.7 slice_compare_fusion
  96.8 0.9 fusion.12
  97.7 1.4 %fusion.16 = bf16[16,2048]{1,0:T(8,128)(2,1)} fusion(f32[2,16,2048]{2,1,0:T(8,128)S(1)} %fusion.8, s32[]{:T(128)S(6)} %select_n.241, f32[16]{0:T(128)S(1)} %broadcast_multiply_fusion, f32[16]{0:T(128)} %copy-done.5, pred[16]{0:T(512)(128)(4,1)S(1)} %broadcast_compare_fusion, bf16[16,2048]{1,0:T(8,128)(2,1)S(1)} %collective-permute-done.12, ...), kind=kLoop, calls=%fused_computation.39 | loop fusion | flops 360448 | bytes 333972 | tf_op jit(solution)/shard_map/convert_element_type | solution.py:137
  99.1 7.9 %collective-permute-done.13 = bf16[2,2,2,64,384]{4,3,2,1,0:T(8,128)(2,1)} collective-permute-done((bf16[2,2,2,64,384]{4,3,2,1,0:T(8,128)(2,1)}, bf16[2,2,2,64,384]{4,3,2,1,0:T(8,128)(2,1)}, u32[]{:S(2)}, u32[]{:S(2)}) %collective-permute-start.13) | collective-permute-done | bytes 393248 | tf_op jit(solution)/shard_map/ppermute | solution.py:22
  107.1 1.3 bitcast_add_fusion
  108.4 0.1 fusion.28
  108.5 1.9 %collective-permute-start.16 = (bf16[2,64,384]{2,1,0:T(8,128)(2,1)S(1)}, bf16[2,64,384]{2,1,0:T(8,128)(2,1)S(1)}, u32[]{:S(2)}, u32[]{:S(2)}) collective-permute-start(bf16[2,64,384]{2,1,0:T(8,128)(2,1)S(1)} %fusion.19), channel_id=1, source_target_pairs={{0,32},{16,48},{32,0},{48,16},{64,96},{80,112},{96,64},{112,80},{1... | collective-permute-start | bytes 294920 | tf_op jit(solution)/shard_map/ppermute | solution.py:22
  110.4 4.2 %collective-permute-start.14 = (bf16[2,64,384]{2,1,0:T(8,128)(2,1)S(1)}, bf16[2,64,384]{2,1,0:T(8,128)(2,1)S(1)}, u32[]{:S(2)}, u32[]{:S(2)}) collective-permute-start(bf16[2,64,384]{2,1,0:T(8,128)(2,1)S(1)} %fusion.18), channel_id=1, source_target_pairs={{0,32},{16,48},{32,0},{48,16},{64,96},{80,112},{96,64},{112,80},{1... | collective-permute-start | bytes 294920 | tf_op jit(solution)/shard_map/ppermute | solution.py:22
  114.7 2.4 %collective-permute-done.16 = bf16[2,64,384]{2,1,0:T(8,128)(2,1)S(1)} collective-permute-done((bf16[2,64,384]{2,1,0:T(8,128)(2,1)S(1)}, bf16[2,64,384]{2,1,0:T(8,128)(2,1)S(1)}, u32[]{:S(2)}, u32[]{:S(2)}) %collective-permute-start.16) | collective-permute-done | bytes 98336 | tf_op jit(solution)/shard_map/ppermute | solution.py:22
  117.1 1.9 %collective-permute-start.17 = (bf16[64,384]{1,0:T(8,128)(2,1)S(1)}, bf16[64,384]{1,0:T(8,128)(2,1)S(1)}, u32[]{:S(2)}, u32[]{:S(2)}) collective-permute-start(bf16[64,384]{1,0:T(8,128)(2,1)S(1)} %fusion.22), channel_id=1, source_target_pairs={{0,64},{16,80},{32,96},{48,112},{64,0},{80,16},{96,32},{112,48},{1... | collective-permute-start | bytes 147464 | tf_op jit(solution)/shard_map/ppermute | solution.py:22
  119.1 2.2 %collective-permute-done.14 = bf16[2,64,384]{2,1,0:T(8,128)(2,1)S(1)} collective-permute-done((bf16[2,64,384]{2,1,0:T(8,128)(2,1)S(1)}, bf16[2,64,384]{2,1,0:T(8,128)(2,1)S(1)}, u32[]{:S(2)}, u32[]{:S(2)}) %collective-permute-start.14) | collective-permute-done | bytes 98336 | tf_op jit(solution)/shard_map/ppermute | solution.py:22
  121.4 5.1 %collective-permute-start.15 = (bf16[64,384]{1,0:T(8,128)(2,1)S(1)}, bf16[64,384]{1,0:T(8,128)(2,1)S(1)}, u32[]{:S(2)}, u32[]{:S(2)}) collective-permute-start(bf16[64,384]{1,0:T(8,128)(2,1)S(1)} %fusion.21), channel_id=1, source_target_pairs={{0,64},{16,80},{32,96},{48,112},{64,0},{80,16},{96,32},{112,48},{1... | collective-permute-start | bytes 147464 | tf_op jit(solution)/shard_map/ppermute | solution.py:22
  126.4 1.7 %collective-permute-done.17 = bf16[64,384]{1,0:T(8,128)(2,1)S(1)} collective-permute-done((bf16[64,384]{1,0:T(8,128)(2,1)S(1)}, bf16[64,384]{1,0:T(8,128)(2,1)S(1)}, u32[]{:S(2)}, u32[]{:S(2)}) %collective-permute-start.17) | collective-permute-done | bytes 49184 | tf_op jit(solution)/shard_map/ppermute | solution.py:22
  128.1 0.7 bitcast_add_fusion.5
  128.7 1.9 %collective-permute-done.15 = bf16[64,384]{1,0:T(8,128)(2,1)S(1)} collective-permute-done((bf16[64,384]{1,0:T(8,128)(2,1)S(1)}, bf16[64,384]{1,0:T(8,128)(2,1)S(1)}, u32[]{:S(2)}, u32[]{:S(2)}) %collective-permute-start.15) | collective-permute-done | bytes 49184 | tf_op jit(solution)/shard_map/ppermute | solution.py:22
  130.7 0.7 bitcast_add_fusion.6
  (37 shorter events, 0.5 us)
Async XLA Ops:
  0.6 46.2 %copy-start = (bf16[2048,384]{1,0:T(8,128)(2,1)S(1)}, bf16[2048,384]{1,0:T(8,128)(2,1)}, u32[]{:S(2)}) copy-start(bf16[2048,384]{1,0:T(8,128)(2,1)} %param.10) | copy-start | bytes 4718596
  2.5 33.1 %copy-start.5 = (f32[16]{0:T(128)}, f32[16]{0:T(128)S(1)}, u32[]{:S(2)}) copy-start(f32[16]{0:T(128)S(1)} %add_rsqrt_fusion) | copy-start | bytes 196
  3.4 18.2 %collective-permute-start = (bf16[16,2048]{1,0:T(8,128)(2,1)S(1)}, bf16[16,2048]{1,0:T(8,128)(2,1)S(1)}, u32[]{:S(2)}, u32[]{:S(2)}) collective-permute-start(bf16[16,2048]{1,0:T(8,128)(2,1)S(1)} %fusion.11), channel_id=1, source_target_pairs={{0,2},{1,3},{2,0},{3,1},{4,6},{5,7},{6,4},{7,5},{8,10},{9,11},{10,... | collective-permute-start | bytes 196616 | tf_op jit(solution)/shard_map/ppermute | solution.py:22
  21.6 9.6 %collective-permute-start.1 = (bf16[2,16,2048]{2,1,0:T(8,128)(2,1)S(1)}, bf16[2,16,2048]{2,1,0:T(8,128)(2,1)S(1)}, u32[]{:S(2)}, u32[]{:S(2)}) collective-permute-start(bf16[2,16,2048]{2,1,0:T(8,128)(2,1)S(1)} %maximum_select_fusion.3), channel_id=1, source_target_pairs={{0,12},{1,13},{2,14},{3,15},{4,0},{5,1},{6,2},{7,3},{8,4},{9,5},{1... | collective-permute-start | bytes 393224 | tf_op jit(solution)/shard_map/ppermute | solution.py:22
  26.3 7.2 %collective-permute-start.2 = (bf16[2,16,2048]{2,1,0:T(8,128)(2,1)S(1)}, bf16[2,16,2048]{2,1,0:T(8,128)(2,1)S(1)}, u32[]{:S(2)}, u32[]{:S(2)}) collective-permute-start(bf16[2,16,2048]{2,1,0:T(8,128)(2,1)S(1)} %maximum_select_fusion.3), channel_id=1, source_target_pairs={{0,8},{1,9},{2,10},{3,11},{4,12},{5,13},{6,14},{7,15},{8,0},{9,1},... | collective-permute-start | bytes 393224 | tf_op jit(solution)/shard_map/ppermute | solution.py:22
  28.6 6.9 %collective-permute-start.3 = (bf16[2,16,2048]{2,1,0:T(8,128)(2,1)S(1)}, bf16[2,16,2048]{2,1,0:T(8,128)(2,1)S(1)}, u32[]{:S(2)}, u32[]{:S(2)}) collective-permute-start(bf16[2,16,2048]{2,1,0:T(8,128)(2,1)S(1)} %maximum_select_fusion.3), channel_id=1, source_target_pairs={{0,4},{1,5},{2,6},{3,7},{4,8},{5,9},{6,10},{7,11},{8,12},{9,13},{1... | collective-permute-start | bytes 393224 | tf_op jit(solution)/shard_map/ppermute | solution.py:22
  36.4 8.6 %collective-permute-start.4 = (bf16[4,2,16,2048]{3,2,1,0:T(8,128)(2,1)}, bf16[4,2,16,2048]{3,2,1,0:T(8,128)(2,1)S(1)}, u32[]{:S(2)}, u32[]{:S(2)}) collective-permute-start(bf16[4,2,16,2048]{3,2,1,0:T(8,128)(2,1)} %constant_dynamic-slice_fusion.8), channel_id=1, source_target_pairs={{0,1},{1,0},{2,3},{3,2},{4,5},{5,4},{6,7},{7,6},{8,9},{9,8},{10,11... | collective-permute-start | bytes 1572872 | tf_op jit(solution)/shard_map/ppermute | solution.py:22
  43.6 1.5 %copy-start.1 = (bf16[2048,384]{1,0:T(8,128)(2,1)S(1)}, bf16[2048,384]{1,0:T(8,128)(2,1)}, u32[]{:S(2)}) copy-start(bf16[2048,384]{1,0:T(8,128)(2,1)} %param.9) | copy-start | bytes 4718596
  45.1 0.9 copy-start.3
  49.9 7.9 %collective-permute-start.5 = (bf16[4,2,16,2048]{3,2,1,0:T(8,128)(2,1)S(1)}, bf16[4,2,16,2048]{3,2,1,0:T(8,128)(2,1)S(1)}, u32[]{:S(2)}, u32[]{:S(2)}) collective-permute-start(bf16[4,2,16,2048]{3,2,1,0:T(8,128)(2,1)S(1)} %dynamic-slice_bitcast_fusion), channel_id=1, source_target_pairs={{0,1},{1,0},{2,3},{3,2},{4,5},{5,4},{6,7},{7,6},{8,9},{9,8},{10,11... | collective-permute-start | bytes 1572872 | tf_op jit(solution)/shard_map/ppermute | solution.py:22
  53.4 18.3 %collective-permute-start.10 = (bf16[2,512,384]{2,1,0:T(8,128)(2,1)S(1)}, bf16[2,512,384]{2,1,0:T(8,128)(2,1)S(1)}, u32[]{:S(2)}, u32[]{:S(2)}) collective-permute-start(bf16[2,512,384]{2,1,0:T(8,128)(2,1)S(1)} %pad_maximum_fusion.1), channel_id=1, source_target_pairs={{0,128},{1,385},{2,130},{3,387},{4,132},{5,389},{6,134},{7,391},{8... | collective-permute-start | bytes 2359304 | tf_op jit(solution)/shard_map/ppermute | solution.py:22
  58.1 32.8 %collective-permute-start.9 = (bf16[2,512,384]{2,1,0:T(8,128)(2,1)S(1)}, bf16[2,512,384]{2,1,0:T(8,128)(2,1)S(1)}, u32[]{:S(2)}, u32[]{:S(2)}) collective-permute-start(bf16[2,512,384]{2,1,0:T(8,128)(2,1)S(1)} %maximum_select_fusion.1), channel_id=1, source_target_pairs={{0,384},{1,129},{2,386},{3,131},{4,388},{5,133},{6,390},{7,135},{8... | collective-permute-start | bytes 2359304 | tf_op jit(solution)/shard_map/ppermute | solution.py:22
  60.1 17.3 %collective-permute-start.6 = (bf16[2,16,2048]{2,1,0:T(8,128)(2,1)S(1)}, bf16[2,16,2048]{2,1,0:T(8,128)(2,1)S(1)}, u32[]{:S(2)}, u32[]{:S(2)}) collective-permute-start(bf16[2,16,2048]{2,1,0:T(8,128)(2,1)S(1)} %get-tuple-element.18), channel_id=1, source_target_pairs={{0,4},{1,5},{2,6},{3,7},{4,8},{5,9},{6,10},{7,11},{8,12},{9,13},{1... | collective-permute-start | bytes 393224 | tf_op jit(solution)/shard_map/ppermute | solution.py:22
  62.0 15.4 %collective-permute-start.7 = (bf16[2,16,2048]{2,1,0:T(8,128)(2,1)S(1)}, bf16[2,16,2048]{2,1,0:T(8,128)(2,1)S(1)}, u32[]{:S(2)}, u32[]{:S(2)}) collective-permute-start(bf16[2,16,2048]{2,1,0:T(8,128)(2,1)S(1)} %get-tuple-element.20), channel_id=1, source_target_pairs={{0,8},{1,9},{2,10},{3,11},{4,12},{5,13},{6,14},{7,15},{8,0},{9,1},... | collective-permute-start | bytes 393224 | tf_op jit(solution)/shard_map/ppermute | solution.py:22
  65.4 12.1 %collective-permute-start.8 = (bf16[2,16,2048]{2,1,0:T(8,128)(2,1)S(1)}, bf16[2,16,2048]{2,1,0:T(8,128)(2,1)S(1)}, u32[]{:S(2)}, u32[]{:S(2)}) collective-permute-start(bf16[2,16,2048]{2,1,0:T(8,128)(2,1)S(1)} %get-tuple-element.19), channel_id=1, source_target_pairs={{0,12},{1,13},{2,14},{3,15},{4,0},{5,1},{6,2},{7,3},{8,4},{9,5},{1... | collective-permute-start | bytes 393224 | tf_op jit(solution)/shard_map/ppermute | solution.py:22
  72.0 19.0 %collective-permute-start.11 = (bf16[2,512,384]{2,1,0:T(8,128)(2,1)S(1)}, bf16[2,512,384]{2,1,0:T(8,128)(2,1)}, u32[]{:S(2)}, u32[]{:S(2)}) collective-permute-start(bf16[2,512,384]{2,1,0:T(8,128)(2,1)S(1)} %add_convert_fusion), channel_id=1, source_target_pairs={{0,128},{1,385},{2,130},{3,387},{4,132},{5,389},{6,134},{7,391},{8... | collective-permute-start | bytes 2359304 | tf_op jit(solution)/shard_map/ppermute | solution.py:22
  77.4 19.4 %copy-start.2 = (bf16[16,2048]{1,0:T(8,128)(2,1)S(1)}, bf16[16,2048]{1,0:T(8,128)(2,1)}, u32[]{:S(2)}) copy-start(bf16[16,2048]{1,0:T(8,128)(2,1)} %param.6) | copy-start | bytes 196612
  77.4 19.4 %copy-start.4 = (bf16[2048]{0:T(1024)(128)(2,1)S(1)}, bf16[2048]{0:T(1024)(128)(2,1)}, u32[]{:S(2)}) copy-start(bf16[2048]{0:T(1024)(128)(2,1)} %param.8) | copy-start | bytes 12292
  78.2 18.7 %collective-permute-start.12 = (bf16[16,2048]{1,0:T(8,128)(2,1)}, bf16[16,2048]{1,0:T(8,128)(2,1)S(1)}, u32[]{:S(2)}, u32[]{:S(2)}) collective-permute-start(bf16[16,2048]{1,0:T(8,128)(2,1)} %fusion.20), channel_id=1, source_target_pairs={{0,2},{1,3},{2,0},{3,1},{4,6},{5,7},{6,4},{7,5},{8,10},{9,11},{10,... | collective-permute-start | bytes 196616 | tf_op jit(solution)/shard_map/ppermute | solution.py:22
  92.9 14.2 %collective-permute-start.13 = (bf16[2,2,2,64,384]{4,3,2,1,0:T(8,128)(2,1)}, bf16[2,2,2,64,384]{4,3,2,1,0:T(8,128)(2,1)}, u32[]{:S(2)}, u32[]{:S(2)}) collective-permute-start(bf16[2,2,2,64,384]{4,3,2,1,0:T(8,128)(2,1)} %fusion.6), channel_id=1, source_target_pairs={{0,16},{16,0},{32,48},{48,32},{64,80},{80,64},{96,112},{112,96},{1... | collective-permute-start | bytes 1179656 | tf_op jit(solution)/shard_map/ppermute | solution.py:22
  108.5 8.6 %collective-permute-start.16 = (bf16[2,64,384]{2,1,0:T(8,128)(2,1)S(1)}, bf16[2,64,384]{2,1,0:T(8,128)(2,1)S(1)}, u32[]{:S(2)}, u32[]{:S(2)}) collective-permute-start(bf16[2,64,384]{2,1,0:T(8,128)(2,1)S(1)} %fusion.19), channel_id=1, source_target_pairs={{0,32},{16,48},{32,0},{48,16},{64,96},{80,112},{96,64},{112,80},{1... | collective-permute-start | bytes 294920 | tf_op jit(solution)/shard_map/ppermute | solution.py:22
  110.4 10.9 %collective-permute-start.14 = (bf16[2,64,384]{2,1,0:T(8,128)(2,1)S(1)}, bf16[2,64,384]{2,1,0:T(8,128)(2,1)S(1)}, u32[]{:S(2)}, u32[]{:S(2)}) collective-permute-start(bf16[2,64,384]{2,1,0:T(8,128)(2,1)S(1)} %fusion.18), channel_id=1, source_target_pairs={{0,32},{16,48},{32,0},{48,16},{64,96},{80,112},{96,64},{112,80},{1... | collective-permute-start | bytes 294920 | tf_op jit(solution)/shard_map/ppermute | solution.py:22
  117.1 10.9 %collective-permute-start.17 = (bf16[64,384]{1,0:T(8,128)(2,1)S(1)}, bf16[64,384]{1,0:T(8,128)(2,1)S(1)}, u32[]{:S(2)}, u32[]{:S(2)}) collective-permute-start(bf16[64,384]{1,0:T(8,128)(2,1)S(1)} %fusion.22), channel_id=1, source_target_pairs={{0,64},{16,80},{32,96},{48,112},{64,0},{80,16},{96,32},{112,48},{1... | collective-permute-start | bytes 147464 | tf_op jit(solution)/shard_map/ppermute | solution.py:22
  121.4 9.3 %collective-permute-start.15 = (bf16[64,384]{1,0:T(8,128)(2,1)S(1)}, bf16[64,384]{1,0:T(8,128)(2,1)S(1)}, u32[]{:S(2)}, u32[]{:S(2)}) collective-permute-start(bf16[64,384]{1,0:T(8,128)(2,1)S(1)} %fusion.21), channel_id=1, source_target_pairs={{0,64},{16,80},{32,96},{48,112},{64,0},{80,16},{96,32},{112,48},{1... | collective-permute-start | bytes 147464 | tf_op jit(solution)/shard_map/ppermute | solution.py:22

commit v8 on v6

--- a/solution.py
+++ b/solution.py
@@ -1,6 +1,8 @@
 import jax
 import jax.numpy as jnp
 from jax import lax
+from jax.experimental import pallas as pl
+from jax.experimental.pallas import tpu as pltpu
 from jax.sharding import PartitionSpec as P
 
 NX, NZ = 4, 8
@@ -98,6 +100,27 @@
     return total(mine) + to_z(sent, bit).astype(F32), sent
 
 
+def norm_kernel(masked_ref, tokens_ref, vector_ref, normed_ref):
+    rows = tokens_ref.shape[0]
+    index = lax.broadcasted_iota(jnp.int32, (rows, 1), 0)
+    flag = jnp.zeros((rows, 1), jnp.int32)
+    for i in range(rows):
+        flag = jnp.where(index == i, masked_ref[i], flag)
+    mixed = jnp.where(flag == 1, vector_ref[...].astype(F32), tokens_ref[...].astype(F32))
+    inverse = lax.rsqrt(jnp.mean(mixed * mixed, axis=-1, keepdims=True) + 1e-06)
+    normed_ref[...] = (mixed * inverse).astype(BF16)
+
+
+def norm(masked, tokens, mask_vector):
+    return pl.pallas_call(
+        norm_kernel,
+        out_shape=jax.ShapeDtypeStruct(tokens.shape, BF16),
+        in_specs=[pl.BlockSpec(memory_space=pltpu.SMEM)] + [pl.BlockSpec(memory_space=pltpu.VMEM)] * 2,
+        out_specs=pl.BlockSpec(memory_space=pltpu.VMEM),
+        compiler_params=pltpu.CompilerParams(vmem_limit_bytes=4 * 2**20),
+    )(masked, tokens, mask_vector[None, :])
+
+
 def shards(tokens, masked, mask_vector, gate_weight, up_weight, cotangent):
     depth, width = gate_weight.shape
     dp = lax.axis_index("dp")
@@ -109,7 +132,7 @@
     mixed_f = mixed_in.astype(F32)
     inverse = lax.rsqrt(jnp.mean(mixed_f * mixed_f, axis=-1, keepdims=True) + 1e-06)
     normed_full = mixed_f * inverse
-    gathered = gather_rows(normed_full.astype(BF16), y, high, core)
+    gathered = gather_rows(norm(masked, tokens, mask_vector), y, high, core)
     gate = jnp.dot(gathered, gate_weight, preferred_element_type=F32)
     up = jnp.dot(gathered, up_weight, preferred_element_type=F32)
     sig = jax.nn.sigmoid(gate)

time: 129 us -> 129 us (level)
  other arithmetic: 13.6 us -> 10.4 us
  local copies, waits for them, and re-layouts: 3.83 us -> 6.5 us
    unnamed x21 -> x23, local copies, waits for them, and re-layouts: 0.27 us -> 2.9 us
    another operation x2 -> x0, other arithmetic: 1.85 us -> none  [gather_rows(): jnp.stack([normed, other])]
  transfers between devices with their start and end apart: 19 -> 19, of which waited for: 10 -> 11; matrix products, arithmetic and copies ran while one was open for 11% -> 10% of each run, Pallas kernels for 0% -> 0%
where the time goes in v8:
time: 129 us; the launch traced here: 128 us
  starting transfers between devices  86.9 us (67%)
  waiting for transfers between devices  17 us (13%)
  other arithmetic  10.4 us (8%)
  local copies, waits for them, and re-layouts  6.5 us (5%)
  matrix products  5.25 us (4%)
    ppermute x19, starting transfers between devices, move(): lax.ppermute(array, axis_name, [(i, target(i)) for i in range(count)])  86.9 us
    ppermute x19, waiting for transfers between devices, move(): lax.ppermute(array, axis_name, [(i, target(i)) for i in range(count)])  17 us
    add x6, other arithmetic, scatter_z(): return (total(mine) + to_z(sent, bit).astype(F32), sent)  3.58 us
    unnamed x23, local copies, waits for them, and re-layouts  2.9 us
  transfers between devices with their start and end apart: 19, of which 11 were waited for; matrix products, arithmetic and copies ran while one was open for 10% of the time, Pallas kernels for 0%

profile of v8, /device:TPU:1, one launch (start us, length us, event | category | flops | bytes accessed | tf_op | source)
XLA Modules:
  0.0 127.9 jit_solution(5044594275054302495)
XLA Ops:
  0.6 0.8 broadcast_in_dim.49.vector_ref
  1.5 0.8 copy-done.1
  2.3 0.7 copy-done.3
  3.0 0.7 shard_map.93
  3.6 16.3 %collective-permute-start = (bf16[16,2048]{1,0:T(8,128)(2,1)S(1)}, bf16[16,2048]{1,0:T(8,128)(2,1)S(1)}, u32[]{:S(2)}, u32[]{:S(2)}) collective-permute-start(bf16[16,2048]{1,0:T(8,128)(2,1)S(1)} %shard_map.93), channel_id=1, source_target_pairs={{0,2},{1,3},{2,0},{3,1},{4,6},{5,7},{6,4},{7,5},{8,10},{9,11},{10,... | collective-permute-start | bytes 196616 | tf_op jit(solution)/shard_map/ppermute | solution.py:24
  19.9 0.7 broadcast_compare_fusion
  20.6 1.2 collective-permute-done
  21.8 4.6 %collective-permute-start.1 = (bf16[2,16,2048]{2,1,0:T(8,128)(2,1)S(1)}, bf16[2,16,2048]{2,1,0:T(8,128)(2,1)S(1)}, u32[]{:S(2)}, u32[]{:S(2)}) collective-permute-start(bf16[2,16,2048]{2,1,0:T(8,128)(2,1)S(1)} %maximum_select_fusion.3), channel_id=1, source_target_pairs={{0,12},{1,13},{2,14},{3,15},{4,0},{5,1},{6,2},{7,3},{8,4},{9,5},{1... | collective-permute-start | bytes 393224 | tf_op jit(solution)/shard_map/ppermute | solution.py:24
  26.4 2.3 %collective-permute-start.2 = (bf16[2,16,2048]{2,1,0:T(8,128)(2,1)S(1)}, bf16[2,16,2048]{2,1,0:T(8,128)(2,1)S(1)}, u32[]{:S(2)}, u32[]{:S(2)}) collective-permute-start(bf16[2,16,2048]{2,1,0:T(8,128)(2,1)S(1)} %maximum_select_fusion.3), channel_id=1, source_target_pairs={{0,8},{1,9},{2,10},{3,11},{4,12},{5,13},{6,14},{7,15},{8,0},{9,1},... | collective-permute-start | bytes 393224 | tf_op jit(solution)/shard_map/ppermute | solution.py:24
  28.7 2.6 %collective-permute-start.3 = (bf16[2,16,2048]{2,1,0:T(8,128)(2,1)S(1)}, bf16[2,16,2048]{2,1,0:T(8,128)(2,1)S(1)}, u32[]{:S(2)}, u32[]{:S(2)}) collective-permute-start(bf16[2,16,2048]{2,1,0:T(8,128)(2,1)S(1)} %maximum_select_fusion.3), channel_id=1, source_target_pairs={{0,4},{1,5},{2,6},{3,7},{4,8},{5,9},{6,10},{7,11},{8,12},{9,13},{1... | collective-permute-start | bytes 393224 | tf_op jit(solution)/shard_map/ppermute | solution.py:24
  31.4 2.3 %collective-permute-done.2 = bf16[2,16,2048]{2,1,0:T(8,128)(2,1)S(1)} collective-permute-done((bf16[2,16,2048]{2,1,0:T(8,128)(2,1)S(1)}, bf16[2,16,2048]{2,1,0:T(8,128)(2,1)S(1)}, u32[]{:S(2)}, u32[]{:S(2)}) %collective-permute-start.2) | collective-permute-done | bytes 131104 | tf_op jit(solution)/shard_map/ppermute | solution.py:24
  33.6 2.0 %collective-permute-done.3 = bf16[2,16,2048]{2,1,0:T(8,128)(2,1)S(1)} collective-permute-done((bf16[2,16,2048]{2,1,0:T(8,128)(2,1)S(1)}, bf16[2,16,2048]{2,1,0:T(8,128)(2,1)S(1)}, u32[]{:S(2)}, u32[]{:S(2)}) %collective-permute-start.3) | collective-permute-done | bytes 131104 | tf_op jit(solution)/shard_map/ppermute | solution.py:24
  35.8 6.9 %collective-permute-start.4 = (bf16[4,2,16,2048]{3,2,1,0:T(8,128)(2,1)S(1)}, bf16[4,2,16,2048]{3,2,1,0:T(8,128)(2,1)S(1)}, u32[]{:S(2)}, u32[]{:S(2)}) collective-permute-start(bf16[4,2,16,2048]{3,2,1,0:T(8,128)(2,1)S(1)} %constant_dynamic-slice_fusion.8), channel_id=1, source_target_pairs={{0,1},{1,0},{2,3},{3,2},{4,5},{5,4},{6,7},{7,6},{8,9},{9,8},{10,11... | collective-permute-start | bytes 1572872 | tf_op jit(solution)/shard_map/ppermute | solution.py:24
  42.7 0.2 fusion.17
  42.9 0.5 add_rsqrt_fusion
  43.5 0.7 collective-permute-done.4
  44.2 0.2 maximum_select_fusion
  44.5 1.3 %copy-done.4 = bf16[2048,384]{1,0:T(8,128)(2,1)S(1)} copy-done((bf16[2048,384]{1,0:T(8,128)(2,1)S(1)}, bf16[2048,384]{1,0:T(8,128)(2,1)}, u32[]{:S(2)}) %copy-start.4) | copy-done | bytes 1572888
  45.8 0.7 fusion.30
  46.5 0.8 convolution_convert_fusion.1
  47.4 1.5 %fusion.3 = (bf16[256,384]{1,0:T(8,128)(2,1)S(1)}, bf16[256,384]{1,0:T(8,128)(2,1)}) fusion(bf16[256,384]{1,0:T(8,128)(2,1)S(1)} %copy-done.7, f32[256,384]{1,0:T(8,128)S(1)} %fusion.30, bf16[256,2048]{1,0:T(8,128)(2,1)S(1)} %bitcast.103, bf16[2048,384]{1,0:T(8,128)(2,1)S(1)} %copy-done), kind=kOutput, calls=%fused_computation.14 | convolution fusion | flops 404029440 | bytes 3604480 | tf_op jit(solution)/shard_map/dot_general | solution.py:137
  48.8 0.7 fusion.31
  49.6 0.8 fusion
  50.4 2.3 %collective-permute-start.5 = (bf16[4,2,16,2048]{3,2,1,0:T(8,128)(2,1)S(1)}, bf16[4,2,16,2048]{3,2,1,0:T(8,128)(2,1)S(1)}, u32[]{:S(2)}, u32[]{:S(2)}) collective-permute-start(bf16[4,2,16,2048]{3,2,1,0:T(8,128)(2,1)S(1)} %dynamic-slice_bitcast_fusion), channel_id=1, source_target_pairs={{0,1},{1,0},{2,3},{3,2},{4,5},{5,4},{6,7},{7,6},{8,9},{9,8},{10,11... | collective-permute-start | bytes 1572872 | tf_op jit(solution)/shard_map/ppermute | solution.py:24
  52.7 0.7 convolution_convert_fusion
  53.5 0.3 constant_dynamic-slice_fusion
  53.8 0.1 pad_maximum_fusion
  53.9 4.4 %collective-permute-start.10 = (bf16[2,512,384]{2,1,0:T(8,128)(2,1)S(1)}, bf16[2,512,384]{2,1,0:T(8,128)(2,1)S(1)}, u32[]{:S(2)}, u32[]{:S(2)}) collective-permute-start(bf16[2,512,384]{2,1,0:T(8,128)(2,1)S(1)} %pad_maximum_fusion), channel_id=1, source_target_pairs={{0,128},{1,385},{2,130},{3,387},{4,132},{5,389},{6,134},{7,391},{8... | collective-permute-start | bytes 2359304 | tf_op jit(solution)/shard_map/ppermute | solution.py:24
  58.3 0.2 fusion.27
  58.5 0.1 maximum_select_fusion.1
  58.6 1.9 %collective-permute-start.9 = (bf16[2,512,384]{2,1,0:T(8,128)(2,1)S(1)}, bf16[2,512,384]{2,1,0:T(8,128)(2,1)S(1)}, u32[]{:S(2)}, u32[]{:S(2)}) collective-permute-start(bf16[2,512,384]{2,1,0:T(8,128)(2,1)S(1)} %maximum_select_fusion.1), channel_id=1, source_target_pairs={{0,384},{1,129},{2,386},{3,131},{4,388},{5,133},{6,390},{7,135},{8... | collective-permute-start | bytes 2359304 | tf_op jit(solution)/shard_map/ppermute | solution.py:24
  60.6 1.9 %collective-permute-start.6 = (bf16[2,16,2048]{2,1,0:T(8,128)(2,1)S(1)}, bf16[2,16,2048]{2,1,0:T(8,128)(2,1)S(1)}, u32[]{:S(2)}, u32[]{:S(2)}) collective-permute-start(bf16[2,16,2048]{2,1,0:T(8,128)(2,1)S(1)} %get-tuple-element.20), channel_id=1, source_target_pairs={{0,4},{1,5},{2,6},{3,7},{4,8},{5,9},{6,10},{7,11},{8,12},{9,13},{1... | collective-permute-start | bytes 393224 | tf_op jit(solution)/shard_map/ppermute | solution.py:24
  62.5 3.3 %collective-permute-start.7 = (bf16[2,16,2048]{2,1,0:T(8,128)(2,1)S(1)}, bf16[2,16,2048]{2,1,0:T(8,128)(2,1)S(1)}, u32[]{:S(2)}, u32[]{:S(2)}) collective-permute-start(bf16[2,16,2048]{2,1,0:T(8,128)(2,1)S(1)} %get-tuple-element.22), channel_id=1, source_target_pairs={{0,8},{1,9},{2,10},{3,11},{4,12},{5,13},{6,14},{7,15},{8,0},{9,1},... | collective-permute-start | bytes 393224 | tf_op jit(solution)/shard_map/ppermute | solution.py:24
  65.8 4.0 %collective-permute-start.8 = (bf16[2,16,2048]{2,1,0:T(8,128)(2,1)S(1)}, bf16[2,16,2048]{2,1,0:T(8,128)(2,1)S(1)}, u32[]{:S(2)}, u32[]{:S(2)}) collective-permute-start(bf16[2,16,2048]{2,1,0:T(8,128)(2,1)S(1)} %get-tuple-element.21), channel_id=1, source_target_pairs={{0,12},{1,13},{2,14},{3,15},{4,0},{5,1},{6,2},{7,3},{8,4},{9,5},{1... | collective-permute-start | bytes 393224 | tf_op jit(solution)/shard_map/ppermute | solution.py:24
  69.8 2.4 %collective-permute-done.10 = bf16[2,512,384]{2,1,0:T(8,128)(2,1)S(1)} collective-permute-done((bf16[2,512,384]{2,1,0:T(8,128)(2,1)S(1)}, bf16[2,512,384]{2,1,0:T(8,128)(2,1)S(1)}, u32[]{:S(2)}, u32[]{:S(2)}) %collective-permute-start.10) | collective-permute-done | bytes 786464 | tf_op jit(solution)/shard_map/ppermute | solution.py:24
  72.3 0.2 add_convert_fusion
  72.5 5.3 %collective-permute-start.11 = (bf16[2,512,384]{2,1,0:T(8,128)(2,1)S(1)}, bf16[2,512,384]{2,1,0:T(8,128)(2,1)S(1)}, u32[]{:S(2)}, u32[]{:S(2)}) collective-permute-start(bf16[2,512,384]{2,1,0:T(8,128)(2,1)S(1)} %add_convert_fusion), channel_id=1, source_target_pairs={{0,128},{1,385},{2,130},{3,387},{4,132},{5,389},{6,134},{7,391},{8... | collective-permute-start | bytes 2359304 | tf_op jit(solution)/shard_map/ppermute | solution.py:24
  77.9 0.6 fusion.20
  78.6 12.8 %collective-permute-start.12 = (bf16[16,2048]{1,0:T(8,128)(2,1)}, bf16[16,2048]{1,0:T(8,128)(2,1)S(1)}, u32[]{:S(2)}, u32[]{:S(2)}) collective-permute-start(bf16[16,2048]{1,0:T(8,128)(2,1)} %fusion.20), channel_id=1, source_target_pairs={{0,2},{1,3},{2,0},{3,1},{4,6},{5,7},{6,4},{7,5},{8,10},{9,11},{10,... | collective-permute-start | bytes 196616 | tf_op jit(solution)/shard_map/ppermute | solution.py:24
  91.3 0.1 fusion.28
  91.4 0.1 fusion.29
  91.5 0.8 fusion.8
  92.4 1.9 %collective-permute-start.16 = (bf16[2,2,64,384]{3,2,1,0:T(8,128)(2,1)}, bf16[2,2,64,384]{3,2,1,0:T(8,128)(2,1)}, u32[]{:S(2)}, u32[]{:S(2)}) collective-permute-start(bf16[2,2,64,384]{3,2,1,0:T(8,128)(2,1)} %fusion.8), channel_id=1, source_target_pairs={{0,16},{16,0},{32,48},{48,32},{64,80},{80,64},{96,112},{112,96},{1... | collective-permute-start | bytes 589832 | tf_op jit(solution)/shard_map/ppermute | solution.py:24
  94.3 0.7 slice_reduce_fusion
  95.0 0.8 fusion.9
  95.8 3.4 %collective-permute-start.13 = (bf16[2,2,64,384]{3,2,1,0:T(8,128)(2,1)}, bf16[2,2,64,384]{3,2,1,0:T(8,128)(2,1)}, u32[]{:S(2)}, u32[]{:S(2)}) collective-permute-start(bf16[2,2,64,384]{3,2,1,0:T(8,128)(2,1)} %fusion.9), channel_id=1, source_target_pairs={{0,16},{16,0},{32,48},{48,32},{64,80},{80,64},{96,112},{112,96},{1... | collective-permute-start | bytes 589832 | tf_op jit(solution)/shard_map/ppermute | solution.py:24
  99.2 0.6 tile.12
  99.8 0.7 slice_compare_fusion
  100.5 0.9 fusion.12
  101.3 1.4 %fusion.16 = bf16[16,2048]{1,0:T(8,128)(2,1)} fusion(f32[2,16,2048]{2,1,0:T(8,128)S(1)} %fusion.7, s32[]{:T(128)S(6)} %select_n.250, f32[16]{0:T(128)S(1)} %broadcast_multiply_fusion, f32[16]{0:T(128)} %add_rsqrt_fusion, pred[16]{0:T(512)(128)(4,1)S(1)} %broadcast_compare_fusion, bf16[16,2048]{1,0:T(8,128)(2,1)S(1)} %collective-permute-done.12, ...), kind=kLoop, calls=%fused_computation.40 | loop fusion | flops 360448 | bytes 333972 | tf_op jit(solution)/shard_map/convert_element_type | solution.py:160
  102.7 0.5 collective-permute-done.16
  103.3 1.2 bitcast_add_fusion
  104.5 2.5 %collective-permute-start.17 = (bf16[2,64,384]{2,1,0:T(8,128)(2,1)S(1)}, bf16[2,64,384]{2,1,0:T(8,128)(2,1)S(1)}, u32[]{:S(2)}, u32[]{:S(2)}) collective-permute-start(bf16[2,64,384]{2,1,0:T(8,128)(2,1)S(1)} %fusion.19), channel_id=1, source_target_pairs={{0,32},{16,48},{32,0},{48,16},{64,96},{80,112},{96,64},{112,80},{1... | collective-permute-start | bytes 294920 | tf_op jit(solution)/shard_map/ppermute | solution.py:24
  107.0 0.5 collective-permute-done.13
  107.5 1.0 bitcast_add_fusion.1
  108.5 3.2 %collective-permute-start.14 = (bf16[2,64,384]{2,1,0:T(8,128)(2,1)S(1)}, bf16[2,64,384]{2,1,0:T(8,128)(2,1)S(1)}, u32[]{:S(2)}, u32[]{:S(2)}) collective-permute-start(bf16[2,64,384]{2,1,0:T(8,128)(2,1)S(1)} %fusion.18), channel_id=1, source_target_pairs={{0,32},{16,48},{32,0},{48,16},{64,96},{80,112},{96,64},{112,80},{1... | collective-permute-start | bytes 294920 | tf_op jit(solution)/shard_map/ppermute | solution.py:24
  111.8 1.8 %collective-permute-done.17 = bf16[2,64,384]{2,1,0:T(8,128)(2,1)S(1)} collective-permute-done((bf16[2,64,384]{2,1,0:T(8,128)(2,1)S(1)}, bf16[2,64,384]{2,1,0:T(8,128)(2,1)S(1)}, u32[]{:S(2)}, u32[]{:S(2)}) %collective-permute-start.17) | collective-permute-done | bytes 98336 | tf_op jit(solution)/shard_map/ppermute | solution.py:24
  113.6 1.9 %collective-permute-start.18 = (bf16[64,384]{1,0:T(8,128)(2,1)S(1)}, bf16[64,384]{1,0:T(8,128)(2,1)S(1)}, u32[]{:S(2)}, u32[]{:S(2)}) collective-permute-start(bf16[64,384]{1,0:T(8,128)(2,1)S(1)} %fusion.22), channel_id=1, source_target_pairs={{0,64},{16,80},{32,96},{48,112},{64,0},{80,16},{96,32},{112,48},{1... | collective-permute-start | bytes 147464 | tf_op jit(solution)/shard_map/ppermute | solution.py:24
  115.5 1.9 %collective-permute-done.14 = bf16[2,64,384]{2,1,0:T(8,128)(2,1)S(1)} collective-permute-done((bf16[2,64,384]{2,1,0:T(8,128)(2,1)S(1)}, bf16[2,64,384]{2,1,0:T(8,128)(2,1)S(1)}, u32[]{:S(2)}, u32[]{:S(2)}) %collective-permute-start.14) | collective-permute-done | bytes 98336 | tf_op jit(solution)/shard_map/ppermute | solution.py:24
  117.5 5.4 %collective-permute-start.15 = (bf16[64,384]{1,0:T(8,128)(2,1)S(1)}, bf16[64,384]{1,0:T(8,128)(2,1)S(1)}, u32[]{:S(2)}, u32[]{:S(2)}) collective-permute-start(bf16[64,384]{1,0:T(8,128)(2,1)S(1)} %fusion.21), channel_id=1, source_target_pairs={{0,64},{16,80},{32,96},{48,112},{64,0},{80,16},{96,32},{112,48},{1... | collective-permute-start | bytes 147464 | tf_op jit(solution)/shard_map/ppermute | solution.py:24
  122.9 1.8 %collective-permute-done.18 = bf16[64,384]{1,0:T(8,128)(2,1)S(1)} collective-permute-done((bf16[64,384]{1,0:T(8,128)(2,1)S(1)}, bf16[64,384]{1,0:T(8,128)(2,1)S(1)}, u32[]{:S(2)}, u32[]{:S(2)}) %collective-permute-start.18) | collective-permute-done | bytes 49184 | tf_op jit(solution)/shard_map/ppermute | solution.py:24
  124.7 0.7 bitcast_add_fusion.6
  125.3 1.9 %collective-permute-done.15 = bf16[64,384]{1,0:T(8,128)(2,1)S(1)} collective-permute-done((bf16[64,384]{1,0:T(8,128)(2,1)S(1)}, bf16[64,384]{1,0:T(8,128)(2,1)S(1)}, u32[]{:S(2)}, u32[]{:S(2)}) %collective-permute-start.15) | collective-permute-done | bytes 49184 | tf_op jit(solution)/shard_map/ppermute | solution.py:24
  127.2 0.7 bitcast_add_fusion.7
  (47 shorter events, 0.6 us)
Async XLA Ops:
  0.6 46.7 %copy-start = (bf16[2048,384]{1,0:T(8,128)(2,1)S(1)}, bf16[2048,384]{1,0:T(8,128)(2,1)}, u32[]{:S(2)}) copy-start(bf16[2048,384]{1,0:T(8,128)(2,1)} %param.10) | copy-start | bytes 4718596
  1.5 0.8 copy-start.1
  2.3 0.7 copy-start.3
  3.6 18.1 %collective-permute-start = (bf16[16,2048]{1,0:T(8,128)(2,1)S(1)}, bf16[16,2048]{1,0:T(8,128)(2,1)S(1)}, u32[]{:S(2)}, u32[]{:S(2)}) collective-permute-start(bf16[16,2048]{1,0:T(8,128)(2,1)S(1)} %shard_map.93), channel_id=1, source_target_pairs={{0,2},{1,3},{2,0},{3,1},{4,6},{5,7},{6,4},{7,5},{8,10},{9,11},{10,... | collective-permute-start | bytes 196616 | tf_op jit(solution)/shard_map/ppermute | solution.py:24
  21.8 9.6 %collective-permute-start.1 = (bf16[2,16,2048]{2,1,0:T(8,128)(2,1)S(1)}, bf16[2,16,2048]{2,1,0:T(8,128)(2,1)S(1)}, u32[]{:S(2)}, u32[]{:S(2)}) collective-permute-start(bf16[2,16,2048]{2,1,0:T(8,128)(2,1)S(1)} %maximum_select_fusion.3), channel_id=1, source_target_pairs={{0,12},{1,13},{2,14},{3,15},{4,0},{5,1},{6,2},{7,3},{8,4},{9,5},{1... | collective-permute-start | bytes 393224 | tf_op jit(solution)/shard_map/ppermute | solution.py:24
  26.4 7.2 %collective-permute-start.2 = (bf16[2,16,2048]{2,1,0:T(8,128)(2,1)S(1)}, bf16[2,16,2048]{2,1,0:T(8,128)(2,1)S(1)}, u32[]{:S(2)}, u32[]{:S(2)}) collective-permute-start(bf16[2,16,2048]{2,1,0:T(8,128)(2,1)S(1)} %maximum_select_fusion.3), channel_id=1, source_target_pairs={{0,8},{1,9},{2,10},{3,11},{4,12},{5,13},{6,14},{7,15},{8,0},{9,1},... | collective-permute-start | bytes 393224 | tf_op jit(solution)/shard_map/ppermute | solution.py:24
  28.7 6.9 %collective-permute-start.3 = (bf16[2,16,2048]{2,1,0:T(8,128)(2,1)S(1)}, bf16[2,16,2048]{2,1,0:T(8,128)(2,1)S(1)}, u32[]{:S(2)}, u32[]{:S(2)}) collective-permute-start(bf16[2,16,2048]{2,1,0:T(8,128)(2,1)S(1)} %maximum_select_fusion.3), channel_id=1, source_target_pairs={{0,4},{1,5},{2,6},{3,7},{4,8},{5,9},{6,10},{7,11},{8,12},{9,13},{1... | collective-permute-start | bytes 393224 | tf_op jit(solution)/shard_map/ppermute | solution.py:24
  31.3 11.4 %copy-start.2 = (bf16[16,2048]{1,0:T(8,128)(2,1)S(1)}, bf16[16,2048]{1,0:T(8,128)(2,1)}, u32[]{:S(2)}) copy-start(bf16[16,2048]{1,0:T(8,128)(2,1)} %tokens_ref.1) | copy-start | bytes 196612
  31.3 11.4 %copy-start.8 = (bf16[2048]{0:T(1024)(128)(2,1)S(1)}, bf16[2048]{0:T(1024)(128)(2,1)}, u32[]{:S(2)}) copy-start(bf16[2048]{0:T(1024)(128)(2,1)} %param.8) | copy-start | bytes 12292
  35.8 8.5 %collective-permute-start.4 = (bf16[4,2,16,2048]{3,2,1,0:T(8,128)(2,1)S(1)}, bf16[4,2,16,2048]{3,2,1,0:T(8,128)(2,1)S(1)}, u32[]{:S(2)}, u32[]{:S(2)}) collective-permute-start(bf16[4,2,16,2048]{3,2,1,0:T(8,128)(2,1)S(1)} %constant_dynamic-slice_fusion.8), channel_id=1, source_target_pairs={{0,1},{1,0},{2,3},{3,2},{4,5},{5,4},{6,7},{7,6},{8,9},{9,8},{10,11... | collective-permute-start | bytes 1572872 | tf_op jit(solution)/shard_map/ppermute | solution.py:24
  44.4 1.4 %copy-start.4 = (bf16[2048,384]{1,0:T(8,128)(2,1)S(1)}, bf16[2048,384]{1,0:T(8,128)(2,1)}, u32[]{:S(2)}) copy-start(bf16[2048,384]{1,0:T(8,128)(2,1)} %param.9) | copy-start | bytes 4718596
  44.5 2.0 %copy-start.7 = (bf16[256,384]{1,0:T(8,128)(2,1)S(1)}, bf16[256,384]{1,0:T(8,128)(2,1)}, u32[]{:S(2)}) copy-start(bf16[256,384]{1,0:T(8,128)(2,1)} %param.11) | copy-start | bytes 589828
  50.4 7.9 %collective-permute-start.5 = (bf16[4,2,16,2048]{3,2,1,0:T(8,128)(2,1)S(1)}, bf16[4,2,16,2048]{3,2,1,0:T(8,128)(2,1)S(1)}, u32[]{:S(2)}, u32[]{:S(2)}) collective-permute-start(bf16[4,2,16,2048]{3,2,1,0:T(8,128)(2,1)S(1)} %dynamic-slice_bitcast_fusion), channel_id=1, source_target_pairs={{0,1},{1,0},{2,3},{3,2},{4,5},{5,4},{6,7},{7,6},{8,9},{9,8},{10,11... | collective-permute-start | bytes 1572872 | tf_op jit(solution)/shard_map/ppermute | solution.py:24
  53.9 18.4 %collective-permute-start.10 = (bf16[2,512,384]{2,1,0:T(8,128)(2,1)S(1)}, bf16[2,512,384]{2,1,0:T(8,128)(2,1)S(1)}, u32[]{:S(2)}, u32[]{:S(2)}) collective-permute-start(bf16[2,512,384]{2,1,0:T(8,128)(2,1)S(1)} %pad_maximum_fusion), channel_id=1, source_target_pairs={{0,128},{1,385},{2,130},{3,387},{4,132},{5,389},{6,134},{7,391},{8... | collective-permute-start | bytes 2359304 | tf_op jit(solution)/shard_map/ppermute | solution.py:24
  58.6 32.7 %collective-permute-start.9 = (bf16[2,512,384]{2,1,0:T(8,128)(2,1)S(1)}, bf16[2,512,384]{2,1,0:T(8,128)(2,1)S(1)}, u32[]{:S(2)}, u32[]{:S(2)}) collective-permute-start(bf16[2,512,384]{2,1,0:T(8,128)(2,1)S(1)} %maximum_select_fusion.1), channel_id=1, source_target_pairs={{0,384},{1,129},{2,386},{3,131},{4,388},{5,133},{6,390},{7,135},{8... | collective-permute-start | bytes 2359304 | tf_op jit(solution)/shard_map/ppermute | solution.py:24
  60.6 17.2 %collective-permute-start.6 = (bf16[2,16,2048]{2,1,0:T(8,128)(2,1)S(1)}, bf16[2,16,2048]{2,1,0:T(8,128)(2,1)S(1)}, u32[]{:S(2)}, u32[]{:S(2)}) collective-permute-start(bf16[2,16,2048]{2,1,0:T(8,128)(2,1)S(1)} %get-tuple-element.20), channel_id=1, source_target_pairs={{0,4},{1,5},{2,6},{3,7},{4,8},{5,9},{6,10},{7,11},{8,12},{9,13},{1... | collective-permute-start | bytes 393224 | tf_op jit(solution)/shard_map/ppermute | solution.py:24
  62.5 15.3 %collective-permute-start.7 = (bf16[2,16,2048]{2,1,0:T(8,128)(2,1)S(1)}, bf16[2,16,2048]{2,1,0:T(8,128)(2,1)S(1)}, u32[]{:S(2)}, u32[]{:S(2)}) collective-permute-start(bf16[2,16,2048]{2,1,0:T(8,128)(2,1)S(1)} %get-tuple-element.22), channel_id=1, source_target_pairs={{0,8},{1,9},{2,10},{3,11},{4,12},{5,13},{6,14},{7,15},{8,0},{9,1},... | collective-permute-start | bytes 393224 | tf_op jit(solution)/shard_map/ppermute | solution.py:24
  65.8 12.0 %collective-permute-start.8 = (bf16[2,16,2048]{2,1,0:T(8,128)(2,1)S(1)}, bf16[2,16,2048]{2,1,0:T(8,128)(2,1)S(1)}, u32[]{:S(2)}, u32[]{:S(2)}) collective-permute-start(bf16[2,16,2048]{2,1,0:T(8,128)(2,1)S(1)} %get-tuple-element.21), channel_id=1, source_target_pairs={{0,12},{1,13},{2,14},{3,15},{4,0},{5,1},{6,2},{7,3},{8,4},{9,5},{1... | collective-permute-start | bytes 393224 | tf_op jit(solution)/shard_map/ppermute | solution.py:24
  72.5 18.9 %collective-permute-start.11 = (bf16[2,512,384]{2,1,0:T(8,128)(2,1)S(1)}, bf16[2,512,384]{2,1,0:T(8,128)(2,1)S(1)}, u32[]{:S(2)}, u32[]{:S(2)}) collective-permute-start(bf16[2,512,384]{2,1,0:T(8,128)(2,1)S(1)} %add_convert_fusion), channel_id=1, source_target_pairs={{0,128},{1,385},{2,130},{3,387},{4,132},{5,389},{6,134},{7,391},{8... | collective-permute-start | bytes 2359304 | tf_op jit(solution)/shard_map/ppermute | solution.py:24
  78.6 21.9 %collective-permute-start.12 = (bf16[16,2048]{1,0:T(8,128)(2,1)}, bf16[16,2048]{1,0:T(8,128)(2,1)S(1)}, u32[]{:S(2)}, u32[]{:S(2)}) collective-permute-start(bf16[16,2048]{1,0:T(8,128)(2,1)} %fusion.20), channel_id=1, source_target_pairs={{0,2},{1,3},{2,0},{3,1},{4,6},{5,7},{6,4},{7,5},{8,10},{9,11},{10,... | collective-permute-start | bytes 196616 | tf_op jit(solution)/shard_map/ppermute | solution.py:24
  91.4 4.3 %copy-start.5 = (bf16[1,512,384]{2,1,0:T(8,128)(2,1)}, bf16[1,512,384]{2,1,0:T(8,128)(2,1)S(1)}, u32[]{:S(2)}) copy-start(bf16[1,512,384]{2,1,0:T(8,128)(2,1)S(1)} %get-tuple-element.15) | copy-start | bytes 1179652
  91.5 7.6 %copy-start.6 = (bf16[1,512,384]{2,1,0:T(8,128)(2,1)}, bf16[1,512,384]{2,1,0:T(8,128)(2,1)S(1)}, u32[]{:S(2)}) copy-start(bf16[1,512,384]{2,1,0:T(8,128)(2,1)S(1)} %get-tuple-element.17) | copy-start | bytes 1179652
  92.4 10.9 %collective-permute-start.16 = (bf16[2,2,64,384]{3,2,1,0:T(8,128)(2,1)}, bf16[2,2,64,384]{3,2,1,0:T(8,128)(2,1)}, u32[]{:S(2)}, u32[]{:S(2)}) collective-permute-start(bf16[2,2,64,384]{3,2,1,0:T(8,128)(2,1)} %fusion.8), channel_id=1, source_target_pairs={{0,16},{16,0},{32,48},{48,32},{64,80},{80,64},{96,112},{112,96},{1... | collective-permute-start | bytes 589832 | tf_op jit(solution)/shard_map/ppermute | solution.py:24
  95.8 11.7 %collective-permute-start.13 = (bf16[2,2,64,384]{3,2,1,0:T(8,128)(2,1)}, bf16[2,2,64,384]{3,2,1,0:T(8,128)(2,1)}, u32[]{:S(2)}, u32[]{:S(2)}) collective-permute-start(bf16[2,2,64,384]{3,2,1,0:T(8,128)(2,1)} %fusion.9), channel_id=1, source_target_pairs={{0,16},{16,0},{32,48},{48,32},{64,80},{80,64},{96,112},{112,96},{1... | collective-permute-start | bytes 589832 | tf_op jit(solution)/shard_map/ppermute | solution.py:24
  104.5 9.0 %collective-permute-start.17 = (bf16[2,64,384]{2,1,0:T(8,128)(2,1)S(1)}, bf16[2,64,384]{2,1,0:T(8,128)(2,1)S(1)}, u32[]{:S(2)}, u32[]{:S(2)}) collective-permute-start(bf16[2,64,384]{2,1,0:T(8,128)(2,1)S(1)} %fusion.19), channel_id=1, source_target_pairs={{0,32},{16,48},{32,0},{48,16},{64,96},{80,112},{96,64},{112,80},{1... | collective-permute-start | bytes 294920 | tf_op jit(solution)/shard_map/ppermute | solution.py:24
  108.5 8.9 %collective-permute-start.14 = (bf16[2,64,384]{2,1,0:T(8,128)(2,1)S(1)}, bf16[2,64,384]{2,1,0:T(8,128)(2,1)S(1)}, u32[]{:S(2)}, u32[]{:S(2)}) collective-permute-start(bf16[2,64,384]{2,1,0:T(8,128)(2,1)S(1)} %fusion.18), channel_id=1, source_target_pairs={{0,32},{16,48},{32,0},{48,16},{64,96},{80,112},{96,64},{112,80},{1... | collective-permute-start | bytes 294920 | tf_op jit(solution)/shard_map/ppermute | solution.py:24
  113.6 11.1 %collective-permute-start.18 = (bf16[64,384]{1,0:T(8,128)(2,1)S(1)}, bf16[64,384]{1,0:T(8,128)(2,1)S(1)}, u32[]{:S(2)}, u32[]{:S(2)}) collective-permute-start(bf16[64,384]{1,0:T(8,128)(2,1)S(1)} %fusion.22), channel_id=1, source_target_pairs={{0,64},{16,80},{32,96},{48,112},{64,0},{80,16},{96,32},{112,48},{1... | collective-permute-start | bytes 147464 | tf_op jit(solution)/shard_map/ppermute | solution.py:24
  117.5 9.7 %collective-permute-start.15 = (bf16[64,384]{1,0:T(8,128)(2,1)S(1)}, bf16[64,384]{1,0:T(8,128)(2,1)S(1)}, u32[]{:S(2)}, u32[]{:S(2)}) collective-permute-start(bf16[64,384]{1,0:T(8,128)(2,1)S(1)} %fusion.21), channel_id=1, source_target_pairs={{0,64},{16,80},{32,96},{48,112},{64,0},{80,16},{96,32},{112,48},{1... | collective-permute-start | bytes 147464 | tf_op jit(solution)/shard_map/ppermute | solution.py:24

commit v9 on v6

--- a/solution.py
+++ b/solution.py
@@ -129,8 +129,8 @@
     terms = scatter_x(gate_parts, up_parts, early, x, core)
     terms = [term.reshape(2, 2, 2, 2, depth // (NX * NZ), width) for term in terms]
     gate_grad, _ = scatter_z([term[0] for term in terms], z, 1, 2)
-    up_grad, late = scatter_z([term[1] for term in terms], z, 1, 2)
-    normed_grad = scatter_high(rows, late[0, 0, 0], high)
+    up_grad, _ = scatter_z([term[1] for term in terms], z, 1, 2)
+    normed_grad = scatter_high(rows, terms[2][0, 0, 0, 0, 0], high)
     gate_grad, up_grad = scatter_z([gate_grad], z, 2, 1)[0], scatter_z([up_grad], z, 2, 1)[0]
     gate_grad, up_grad = scatter_z([gate_grad], z, 4, 0)[0], scatter_z([up_grad], z, 4, 0)[0]
     inner = jnp.mean(normed_grad * normed_full, axis=-1, keepdims=True)

time: 129 us -> 130 us (level)
  waiting for transfers between devices: 16.3 us -> 19.3 us
    ppermute x19, waiting for transfers between devices: 16.3 us -> 19.3 us  [move(): lax.ppermute(array, axis_name, [(i, target(i)) for i in range(count)])]
  transfers between devices with their start and end apart: 19 -> 19, of which waited for: 10 -> 10; matrix products, arithmetic and copies ran while one was open for 11% -> 10% of each run, Pallas kernels for 0% -> 0%
where the time goes in v9:
time: 130 us; the launch traced here: 129 us
  starting transfers between devices  85.7 us (66%)
  waiting for transfers between devices  19.3 us (15%)
  other arithmetic  13.6 us (10%)
  matrix products  5.3 us (4%)
  local copies, waits for them, and re-layouts  3.13 us (2%)
  between operations  1.57 us (1%)
    ppermute x19, starting transfers between devices, move(): lax.ppermute(array, axis_name, [(i, target(i)) for i in range(count)])  85.7 us
    ppermute x19, waiting for transfers between devices, move(): lax.ppermute(array, axis_name, [(i, target(i)) for i in range(count)])  19.3 us
    add x6, other arithmetic, scatter_z(): return (total(mine) + to_z(sent, bit).astype(F32), sent)  3.62 us
  transfers between devices with their start and end apart: 19, of which 10 were waited for; matrix products, arithmetic and copies ran while one was open for 10% of the time, Pallas kernels for 0%

profile of v9, /device:TPU:1, one launch (start us, length us, event | category | flops | bytes accessed | tf_op | source)
XLA Modules:
  0.0 128.7 jit_solution(65709563880695994)
XLA Ops:
  0.6 0.0 copy-start
  0.6 0.8 broadcast_compare_fusion
  1.4 1.0 fusion.18
  2.5 0.9 fusion.12
  3.4 16.3 %collective-permute-start = (bf16[16,2048]{1,0:T(8,128)(2,1)S(1)}, bf16[16,2048]{1,0:T(8,128)(2,1)S(1)}, u32[]{:S(2)}, u32[]{:S(2)}) collective-permute-start(bf16[16,2048]{1,0:T(8,128)(2,1)S(1)} %fusion.12), channel_id=1, source_target_pairs={{0,2},{1,3},{2,0},{3,1},{4,6},{5,7},{6,4},{7,5},{8,10},{9,11},{10,... | collective-permute-start | bytes 196616 | tf_op jit(solution)/shard_map/ppermute | solution.py:22
  19.7 0.9 fusion.45
  20.6 0.9 fusion.44
  21.7 4.6 %collective-permute-start.1 = (bf16[2,16,2048]{2,1,0:T(8,128)(2,1)S(1)}, bf16[2,16,2048]{2,1,0:T(8,128)(2,1)S(1)}, u32[]{:S(2)}, u32[]{:S(2)}) collective-permute-start(bf16[2,16,2048]{2,1,0:T(8,128)(2,1)S(1)} %maximum_select_fusion.3), channel_id=1, source_target_pairs={{0,12},{1,13},{2,14},{3,15},{4,0},{5,1},{6,2},{7,3},{8,4},{9,5},{1... | collective-permute-start | bytes 393224 | tf_op jit(solution)/shard_map/ppermute | solution.py:22
  26.3 2.3 %collective-permute-start.2 = (bf16[2,16,2048]{2,1,0:T(8,128)(2,1)S(1)}, bf16[2,16,2048]{2,1,0:T(8,128)(2,1)S(1)}, u32[]{:S(2)}, u32[]{:S(2)}) collective-permute-start(bf16[2,16,2048]{2,1,0:T(8,128)(2,1)S(1)} %maximum_select_fusion.3), channel_id=1, source_target_pairs={{0,8},{1,9},{2,10},{3,11},{4,12},{5,13},{6,14},{7,15},{8,0},{9,1},... | collective-permute-start | bytes 393224 | tf_op jit(solution)/shard_map/ppermute | solution.py:22
  28.6 2.6 %collective-permute-start.3 = (bf16[2,16,2048]{2,1,0:T(8,128)(2,1)S(1)}, bf16[2,16,2048]{2,1,0:T(8,128)(2,1)S(1)}, u32[]{:S(2)}, u32[]{:S(2)}) collective-permute-start(bf16[2,16,2048]{2,1,0:T(8,128)(2,1)S(1)} %maximum_select_fusion.3), channel_id=1, source_target_pairs={{0,4},{1,5},{2,6},{3,7},{4,8},{5,9},{6,10},{7,11},{8,12},{9,13},{1... | collective-permute-start | bytes 393224 | tf_op jit(solution)/shard_map/ppermute | solution.py:22
  31.2 2.3 %collective-permute-done.2 = bf16[2,16,2048]{2,1,0:T(8,128)(2,1)S(1)} collective-permute-done((bf16[2,16,2048]{2,1,0:T(8,128)(2,1)S(1)}, bf16[2,16,2048]{2,1,0:T(8,128)(2,1)S(1)}, u32[]{:S(2)}, u32[]{:S(2)}) %collective-permute-start.2) | collective-permute-done | bytes 131104 | tf_op jit(solution)/shard_map/ppermute | solution.py:22
  33.5 2.0 %collective-permute-done.3 = bf16[2,16,2048]{2,1,0:T(8,128)(2,1)S(1)} collective-permute-done((bf16[2,16,2048]{2,1,0:T(8,128)(2,1)S(1)}, bf16[2,16,2048]{2,1,0:T(8,128)(2,1)S(1)}, u32[]{:S(2)}, u32[]{:S(2)}) %collective-permute-start.3) | collective-permute-done | bytes 131104 | tf_op jit(solution)/shard_map/ppermute | solution.py:22
  35.6 0.9 constant_dynamic-slice_fusion.8
  36.5 6.8 %collective-permute-start.4 = (bf16[4,2,16,2048]{3,2,1,0:T(8,128)(2,1)}, bf16[4,2,16,2048]{3,2,1,0:T(8,128)(2,1)S(1)}, u32[]{:S(2)}, u32[]{:S(2)}) collective-permute-start(bf16[4,2,16,2048]{3,2,1,0:T(8,128)(2,1)} %constant_dynamic-slice_fusion.8), channel_id=1, source_target_pairs={{0,1},{1,0},{2,3},{3,2},{4,5},{5,4},{6,7},{7,6},{8,9},{9,8},{10,11... | collective-permute-start | bytes 1572872 | tf_op jit(solution)/shard_map/ppermute | solution.py:22
  43.6 0.0 copy-start.1
  43.7 1.4 %collective-permute-done.4 = bf16[4,2,16,2048]{3,2,1,0:T(8,128)(2,1)S(1)} collective-permute-done((bf16[4,2,16,2048]{3,2,1,0:T(8,128)(2,1)}, bf16[4,2,16,2048]{3,2,1,0:T(8,128)(2,1)S(1)}, u32[]{:S(2)}, u32[]{:S(2)}) %collective-permute-start.4) | collective-permute-done | bytes 524320 | tf_op jit(solution)/shard_map/ppermute | solution.py:22
  45.0 0.1 maximum_select_fusion
  45.2 0.7 fusion.31
  45.9 0.2 copy-done.5
  46.1 0.8 convolution_convert_fusion
  46.9 1.5 %fusion.3 = (bf16[256,384]{1,0:T(8,128)(2,1)S(1)}, bf16[256,384]{1,0:T(8,128)(2,1)}) fusion(bf16[256,384]{1,0:T(8,128)(2,1)S(1)} %copy-done.5, f32[256,384]{1,0:T(8,128)S(1)} %fusion.31, bf16[256,2048]{1,0:T(8,128)(2,1)S(1)} %bitcast.103, bf16[2048,384]{1,0:T(8,128)(2,1)S(1)} %copy-done), kind=kOutput, calls=%fused_computation.14 | convolution fusion | flops 404029440 | bytes 3604480 | tf_op jit(solution)/shard_map/dot_general | solution.py:114
  48.4 0.7 fusion.32
  49.1 0.8 fusion
  50.0 2.3 %collective-permute-start.5 = (bf16[4,2,16,2048]{3,2,1,0:T(8,128)(2,1)S(1)}, bf16[4,2,16,2048]{3,2,1,0:T(8,128)(2,1)S(1)}, u32[]{:S(2)}, u32[]{:S(2)}) collective-permute-start(bf16[4,2,16,2048]{3,2,1,0:T(8,128)(2,1)S(1)} %dynamic-slice_bitcast_fusion), channel_id=1, source_target_pairs={{0,1},{1,0},{2,3},{3,2},{4,5},{5,4},{6,7},{7,6},{8,9},{9,8},{10,11... | collective-permute-start | bytes 1572872 | tf_op jit(solution)/shard_map/ppermute | solution.py:22
  52.3 0.7 convolution_convert_fusion.1
  53.0 0.3 constant_dynamic-slice_fusion
  53.4 0.1 pad_maximum_fusion
  53.5 4.4 %collective-permute-start.9 = (bf16[2,512,384]{2,1,0:T(8,128)(2,1)S(1)}, bf16[2,512,384]{2,1,0:T(8,128)(2,1)S(1)}, u32[]{:S(2)}, u32[]{:S(2)}) collective-permute-start(bf16[2,512,384]{2,1,0:T(8,128)(2,1)S(1)} %pad_maximum_fusion), channel_id=1, source_target_pairs={{0,128},{1,385},{2,130},{3,387},{4,132},{5,389},{6,134},{7,391},{8... | collective-permute-start | bytes 2359304 | tf_op jit(solution)/shard_map/ppermute | solution.py:22
  57.9 0.2 fusion.28
  58.1 0.1 maximum_select_fusion.1
  58.2 1.9 %collective-permute-start.12 = (bf16[2,512,384]{2,1,0:T(8,128)(2,1)S(1)}, bf16[2,512,384]{2,1,0:T(8,128)(2,1)S(1)}, u32[]{:S(2)}, u32[]{:S(2)}) collective-permute-start(bf16[2,512,384]{2,1,0:T(8,128)(2,1)S(1)} %maximum_select_fusion.1), channel_id=1, source_target_pairs={{0,384},{1,129},{2,386},{3,131},{4,388},{5,133},{6,390},{7,135},{8... | collective-permute-start | bytes 2359304 | tf_op jit(solution)/shard_map/ppermute | solution.py:22
  60.2 1.9 %collective-permute-start.6 = (bf16[2,16,2048]{2,1,0:T(8,128)(2,1)S(1)}, bf16[2,16,2048]{2,1,0:T(8,128)(2,1)S(1)}, u32[]{:S(2)}, u32[]{:S(2)}) collective-permute-start(bf16[2,16,2048]{2,1,0:T(8,128)(2,1)S(1)} %get-tuple-element.20), channel_id=1, source_target_pairs={{0,4},{1,5},{2,6},{3,7},{4,8},{5,9},{6,10},{7,11},{8,12},{9,13},{1... | collective-permute-start | bytes 393224 | tf_op jit(solution)/shard_map/ppermute | solution.py:22
  62.1 3.3 %collective-permute-start.7 = (bf16[2,16,2048]{2,1,0:T(8,128)(2,1)S(1)}, bf16[2,16,2048]{2,1,0:T(8,128)(2,1)S(1)}, u32[]{:S(2)}, u32[]{:S(2)}) collective-permute-start(bf16[2,16,2048]{2,1,0:T(8,128)(2,1)S(1)} %get-tuple-element.22), channel_id=1, source_target_pairs={{0,8},{1,9},{2,10},{3,11},{4,12},{5,13},{6,14},{7,15},{8,0},{9,1},... | collective-permute-start | bytes 393224 | tf_op jit(solution)/shard_map/ppermute | solution.py:22
  65.4 4.0 %collective-permute-start.8 = (bf16[2,16,2048]{2,1,0:T(8,128)(2,1)S(1)}, bf16[2,16,2048]{2,1,0:T(8,128)(2,1)S(1)}, u32[]{:S(2)}, u32[]{:S(2)}) collective-permute-start(bf16[2,16,2048]{2,1,0:T(8,128)(2,1)S(1)} %get-tuple-element.21), channel_id=1, source_target_pairs={{0,12},{1,13},{2,14},{3,15},{4,0},{5,1},{6,2},{7,3},{8,4},{9,5},{1... | collective-permute-start | bytes 393224 | tf_op jit(solution)/shard_map/ppermute | solution.py:22
  69.4 2.4 %collective-permute-done.9 = bf16[2,512,384]{2,1,0:T(8,128)(2,1)S(1)} collective-permute-done((bf16[2,512,384]{2,1,0:T(8,128)(2,1)S(1)}, bf16[2,512,384]{2,1,0:T(8,128)(2,1)S(1)}, u32[]{:S(2)}, u32[]{:S(2)}) %collective-permute-start.9) | collective-permute-done | bytes 786464 | tf_op jit(solution)/shard_map/ppermute | solution.py:22
  71.8 0.2 add_convert_fusion
  72.0 5.3 %collective-permute-start.10 = (bf16[2,512,384]{2,1,0:T(8,128)(2,1)S(1)}, bf16[2,512,384]{2,1,0:T(8,128)(2,1)S(1)}, u32[]{:S(2)}, u32[]{:S(2)}) collective-permute-start(bf16[2,512,384]{2,1,0:T(8,128)(2,1)S(1)} %add_convert_fusion), channel_id=1, source_target_pairs={{0,128},{1,385},{2,130},{3,387},{4,132},{5,389},{6,134},{7,391},{8... | collective-permute-start | bytes 2359304 | tf_op jit(solution)/shard_map/ppermute | solution.py:22
  77.4 0.1 fusion.7
  77.5 0.6 fusion.21
  78.1 12.8 %collective-permute-start.11 = (bf16[16,2048]{1,0:T(8,128)(2,1)}, bf16[16,2048]{1,0:T(8,128)(2,1)S(1)}, u32[]{:S(2)}, u32[]{:S(2)}) collective-permute-start(bf16[16,2048]{1,0:T(8,128)(2,1)} %fusion.21), channel_id=1, source_target_pairs={{0,2},{1,3},{2,0},{3,1},{4,6},{5,7},{6,4},{7,5},{8,10},{9,11},{10,... | collective-permute-start | bytes 196616 | tf_op jit(solution)/shard_map/ppermute | solution.py:22
  90.9 0.1 fusion.29
  91.0 0.1 fusion.30
  91.1 0.8 fusion.9
  92.0 1.9 %collective-permute-start.16 = (bf16[2,2,64,384]{3,2,1,0:T(8,128)(2,1)}, bf16[2,2,64,384]{3,2,1,0:T(8,128)(2,1)}, u32[]{:S(2)}, u32[]{:S(2)}) collective-permute-start(bf16[2,2,64,384]{3,2,1,0:T(8,128)(2,1)} %fusion.9), channel_id=1, source_target_pairs={{0,16},{16,0},{32,48},{48,32},{64,80},{80,64},{96,112},{112,96},{1... | collective-permute-start | bytes 589832 | tf_op jit(solution)/shard_map/ppermute | solution.py:22
  93.9 0.8 fusion.8
  94.6 3.4 %collective-permute-start.13 = (bf16[2,2,64,384]{3,2,1,0:T(8,128)(2,1)}, bf16[2,2,64,384]{3,2,1,0:T(8,128)(2,1)}, u32[]{:S(2)}, u32[]{:S(2)}) collective-permute-start(bf16[2,2,64,384]{3,2,1,0:T(8,128)(2,1)} %fusion.8), channel_id=1, source_target_pairs={{0,16},{16,0},{32,48},{48,32},{64,80},{80,64},{96,112},{112,96},{1... | collective-permute-start | bytes 589832 | tf_op jit(solution)/shard_map/ppermute | solution.py:22
  98.0 0.6 tile.12
  98.6 0.7 slice_compare_fusion
  99.4 0.9 fusion.13
  100.2 1.4 %fusion.17 = bf16[16,2048]{1,0:T(8,128)(2,1)} fusion(f32[2,16,2048]{2,1,0:T(8,128)S(1)} %fusion.7, s32[]{:T(128)S(6)} %select_n.250, f32[16]{0:T(128)S(1)} %broadcast_multiply_fusion, f32[16]{0:T(128)} %copy-done.7, pred[16]{0:T(512)(128)(4,1)S(1)} %broadcast_compare_fusion, bf16[16,2048]{1,0:T(8,128)(2,1)S(1)} %collective-permute-done.11, ...), kind=kLoop, calls=%fused_computation.41 | loop fusion | flops 360448 | bytes 333972 | tf_op jit(solution)/shard_map/convert_element_type | solution.py:137
  101.6 1.2 collective-permute-done.16
  102.8 1.2 bitcast_add_fusion
  104.1 2.5 %collective-permute-start.17 = (bf16[2,64,384]{2,1,0:T(8,128)(2,1)S(1)}, bf16[2,64,384]{2,1,0:T(8,128)(2,1)S(1)}, u32[]{:S(2)}, u32[]{:S(2)}) collective-permute-start(bf16[2,64,384]{2,1,0:T(8,128)(2,1)S(1)} %fusion.20), channel_id=1, source_target_pairs={{0,32},{16,48},{32,0},{48,16},{64,96},{80,112},{96,64},{112,80},{1... | collective-permute-start | bytes 294920 | tf_op jit(solution)/shard_map/ppermute | solution.py:22
  106.6 0.5 collective-permute-done.13
  107.0 1.0 bitcast_add_fusion.1
  108.1 3.3 %collective-permute-start.14 = (bf16[2,64,384]{2,1,0:T(8,128)(2,1)S(1)}, bf16[2,64,384]{2,1,0:T(8,128)(2,1)S(1)}, u32[]{:S(2)}, u32[]{:S(2)}) collective-permute-start(bf16[2,64,384]{2,1,0:T(8,128)(2,1)S(1)} %fusion.19), channel_id=1, source_target_pairs={{0,32},{16,48},{32,0},{48,16},{64,96},{80,112},{96,64},{112,80},{1... | collective-permute-start | bytes 294920 | tf_op jit(solution)/shard_map/ppermute | solution.py:22
  111.4 1.3 %collective-permute-done.17 = bf16[2,64,384]{2,1,0:T(8,128)(2,1)S(1)} collective-permute-done((bf16[2,64,384]{2,1,0:T(8,128)(2,1)S(1)}, bf16[2,64,384]{2,1,0:T(8,128)(2,1)S(1)}, u32[]{:S(2)}, u32[]{:S(2)}) %collective-permute-start.17) | collective-permute-done | bytes 98336 | tf_op jit(solution)/shard_map/ppermute | solution.py:22
  112.8 1.9 %collective-permute-start.18 = (bf16[64,384]{1,0:T(8,128)(2,1)S(1)}, bf16[64,384]{1,0:T(8,128)(2,1)S(1)}, u32[]{:S(2)}, u32[]{:S(2)}) collective-permute-start(bf16[64,384]{1,0:T(8,128)(2,1)S(1)} %fusion.23), channel_id=1, source_target_pairs={{0,64},{16,80},{32,96},{48,112},{64,0},{80,16},{96,32},{112,48},{1... | collective-permute-start | bytes 147464 | tf_op jit(solution)/shard_map/ppermute | solution.py:22
  114.7 2.9 %collective-permute-done.14 = bf16[2,64,384]{2,1,0:T(8,128)(2,1)S(1)} collective-permute-done((bf16[2,64,384]{2,1,0:T(8,128)(2,1)S(1)}, bf16[2,64,384]{2,1,0:T(8,128)(2,1)S(1)}, u32[]{:S(2)}, u32[]{:S(2)}) %collective-permute-start.14) | collective-permute-done | bytes 98336 | tf_op jit(solution)/shard_map/ppermute | solution.py:22
  117.7 4.3 %collective-permute-start.15 = (bf16[64,384]{1,0:T(8,128)(2,1)S(1)}, bf16[64,384]{1,0:T(8,128)(2,1)S(1)}, u32[]{:S(2)}, u32[]{:S(2)}) collective-permute-start(bf16[64,384]{1,0:T(8,128)(2,1)S(1)} %fusion.22), channel_id=1, source_target_pairs={{0,64},{16,80},{32,96},{48,112},{64,0},{80,16},{96,32},{112,48},{1... | collective-permute-start | bytes 147464 | tf_op jit(solution)/shard_map/ppermute | solution.py:22
  122.0 1.4 %collective-permute-done.18 = bf16[64,384]{1,0:T(8,128)(2,1)S(1)} collective-permute-done((bf16[64,384]{1,0:T(8,128)(2,1)S(1)}, bf16[64,384]{1,0:T(8,128)(2,1)S(1)}, u32[]{:S(2)}, u32[]{:S(2)}) %collective-permute-start.18) | collective-permute-done | bytes 49184 | tf_op jit(solution)/shard_map/ppermute | solution.py:22
  123.5 0.7 bitcast_add_fusion.6
  124.1 3.9 %collective-permute-done.15 = bf16[64,384]{1,0:T(8,128)(2,1)S(1)} collective-permute-done((bf16[64,384]{1,0:T(8,128)(2,1)S(1)}, bf16[64,384]{1,0:T(8,128)(2,1)S(1)}, u32[]{:S(2)}, u32[]{:S(2)}) %collective-permute-start.15) | collective-permute-done | bytes 49184 | tf_op jit(solution)/shard_map/ppermute | solution.py:22
  128.0 0.7 bitcast_add_fusion.7
  (45 shorter events, 0.5 us)
Async XLA Ops:
  0.6 46.3 %copy-start = (bf16[2048,384]{1,0:T(8,128)(2,1)S(1)}, bf16[2048,384]{1,0:T(8,128)(2,1)}, u32[]{:S(2)}) copy-start(bf16[2048,384]{1,0:T(8,128)(2,1)} %param.10) | copy-start | bytes 4718596
  2.5 19.2 %copy-start.7 = (f32[16]{0:T(128)}, f32[16]{0:T(128)S(1)}, u32[]{:S(2)}) copy-start(f32[16]{0:T(128)S(1)} %add_rsqrt_fusion) | copy-start | bytes 196
  3.4 18.2 %collective-permute-start = (bf16[16,2048]{1,0:T(8,128)(2,1)S(1)}, bf16[16,2048]{1,0:T(8,128)(2,1)S(1)}, u32[]{:S(2)}, u32[]{:S(2)}) collective-permute-start(bf16[16,2048]{1,0:T(8,128)(2,1)S(1)} %fusion.12), channel_id=1, source_target_pairs={{0,2},{1,3},{2,0},{3,1},{4,6},{5,7},{6,4},{7,5},{8,10},{9,11},{10,... | collective-permute-start | bytes 196616 | tf_op jit(solution)/shard_map/ppermute | solution.py:22
  21.7 9.6 %collective-permute-start.1 = (bf16[2,16,2048]{2,1,0:T(8,128)(2,1)S(1)}, bf16[2,16,2048]{2,1,0:T(8,128)(2,1)S(1)}, u32[]{:S(2)}, u32[]{:S(2)}) collective-permute-start(bf16[2,16,2048]{2,1,0:T(8,128)(2,1)S(1)} %maximum_select_fusion.3), channel_id=1, source_target_pairs={{0,12},{1,13},{2,14},{3,15},{4,0},{5,1},{6,2},{7,3},{8,4},{9,5},{1... | collective-permute-start | bytes 393224 | tf_op jit(solution)/shard_map/ppermute | solution.py:22
  26.3 7.2 %collective-permute-start.2 = (bf16[2,16,2048]{2,1,0:T(8,128)(2,1)S(1)}, bf16[2,16,2048]{2,1,0:T(8,128)(2,1)S(1)}, u32[]{:S(2)}, u32[]{:S(2)}) collective-permute-start(bf16[2,16,2048]{2,1,0:T(8,128)(2,1)S(1)} %maximum_select_fusion.3), channel_id=1, source_target_pairs={{0,8},{1,9},{2,10},{3,11},{4,12},{5,13},{6,14},{7,15},{8,0},{9,1},... | collective-permute-start | bytes 393224 | tf_op jit(solution)/shard_map/ppermute | solution.py:22
  28.6 6.9 %collective-permute-start.3 = (bf16[2,16,2048]{2,1,0:T(8,128)(2,1)S(1)}, bf16[2,16,2048]{2,1,0:T(8,128)(2,1)S(1)}, u32[]{:S(2)}, u32[]{:S(2)}) collective-permute-start(bf16[2,16,2048]{2,1,0:T(8,128)(2,1)S(1)} %maximum_select_fusion.3), channel_id=1, source_target_pairs={{0,4},{1,5},{2,6},{3,7},{4,8},{5,9},{6,10},{7,11},{8,12},{9,13},{1... | collective-permute-start | bytes 393224 | tf_op jit(solution)/shard_map/ppermute | solution.py:22
  36.5 8.6 %collective-permute-start.4 = (bf16[4,2,16,2048]{3,2,1,0:T(8,128)(2,1)}, bf16[4,2,16,2048]{3,2,1,0:T(8,128)(2,1)S(1)}, u32[]{:S(2)}, u32[]{:S(2)}) collective-permute-start(bf16[4,2,16,2048]{3,2,1,0:T(8,128)(2,1)} %constant_dynamic-slice_fusion.8), channel_id=1, source_target_pairs={{0,1},{1,0},{2,3},{3,2},{4,5},{5,4},{6,7},{7,6},{8,9},{9,8},{10,11... | collective-permute-start | bytes 1572872 | tf_op jit(solution)/shard_map/ppermute | solution.py:22
  43.6 1.5 %copy-start.1 = (bf16[2048,384]{1,0:T(8,128)(2,1)S(1)}, bf16[2048,384]{1,0:T(8,128)(2,1)}, u32[]{:S(2)}) copy-start(bf16[2048,384]{1,0:T(8,128)(2,1)} %param.9) | copy-start | bytes 4718596
  45.1 0.9 copy-start.5
  50.0 7.9 %collective-permute-start.5 = (bf16[4,2,16,2048]{3,2,1,0:T(8,128)(2,1)S(1)}, bf16[4,2,16,2048]{3,2,1,0:T(8,128)(2,1)S(1)}, u32[]{:S(2)}, u32[]{:S(2)}) collective-permute-start(bf16[4,2,16,2048]{3,2,1,0:T(8,128)(2,1)S(1)} %dynamic-slice_bitcast_fusion), channel_id=1, source_target_pairs={{0,1},{1,0},{2,3},{3,2},{4,5},{5,4},{6,7},{7,6},{8,9},{9,8},{10,11... | collective-permute-start | bytes 1572872 | tf_op jit(solution)/shard_map/ppermute | solution.py:22
  53.5 18.4 %collective-permute-start.9 = (bf16[2,512,384]{2,1,0:T(8,128)(2,1)S(1)}, bf16[2,512,384]{2,1,0:T(8,128)(2,1)S(1)}, u32[]{:S(2)}, u32[]{:S(2)}) collective-permute-start(bf16[2,512,384]{2,1,0:T(8,128)(2,1)S(1)} %pad_maximum_fusion), channel_id=1, source_target_pairs={{0,128},{1,385},{2,130},{3,387},{4,132},{5,389},{6,134},{7,391},{8... | collective-permute-start | bytes 2359304 | tf_op jit(solution)/shard_map/ppermute | solution.py:22
  58.2 32.7 %collective-permute-start.12 = (bf16[2,512,384]{2,1,0:T(8,128)(2,1)S(1)}, bf16[2,512,384]{2,1,0:T(8,128)(2,1)S(1)}, u32[]{:S(2)}, u32[]{:S(2)}) collective-permute-start(bf16[2,512,384]{2,1,0:T(8,128)(2,1)S(1)} %maximum_select_fusion.1), channel_id=1, source_target_pairs={{0,384},{1,129},{2,386},{3,131},{4,388},{5,133},{6,390},{7,135},{8... | collective-permute-start | bytes 2359304 | tf_op jit(solution)/shard_map/ppermute | solution.py:22
  60.2 17.2 %collective-permute-start.6 = (bf16[2,16,2048]{2,1,0:T(8,128)(2,1)S(1)}, bf16[2,16,2048]{2,1,0:T(8,128)(2,1)S(1)}, u32[]{:S(2)}, u32[]{:S(2)}) collective-permute-start(bf16[2,16,2048]{2,1,0:T(8,128)(2,1)S(1)} %get-tuple-element.20), channel_id=1, source_target_pairs={{0,4},{1,5},{2,6},{3,7},{4,8},{5,9},{6,10},{7,11},{8,12},{9,13},{1... | collective-permute-start | bytes 393224 | tf_op jit(solution)/shard_map/ppermute | solution.py:22
  62.1 15.3 %collective-permute-start.7 = (bf16[2,16,2048]{2,1,0:T(8,128)(2,1)S(1)}, bf16[2,16,2048]{2,1,0:T(8,128)(2,1)S(1)}, u32[]{:S(2)}, u32[]{:S(2)}) collective-permute-start(bf16[2,16,2048]{2,1,0:T(8,128)(2,1)S(1)} %get-tuple-element.22), channel_id=1, source_target_pairs={{0,8},{1,9},{2,10},{3,11},{4,12},{5,13},{6,14},{7,15},{8,0},{9,1},... | collective-permute-start | bytes 393224 | tf_op jit(solution)/shard_map/ppermute | solution.py:22
  65.4 12.0 %collective-permute-start.8 = (bf16[2,16,2048]{2,1,0:T(8,128)(2,1)S(1)}, bf16[2,16,2048]{2,1,0:T(8,128)(2,1)S(1)}, u32[]{:S(2)}, u32[]{:S(2)}) collective-permute-start(bf16[2,16,2048]{2,1,0:T(8,128)(2,1)S(1)} %get-tuple-element.21), channel_id=1, source_target_pairs={{0,12},{1,13},{2,14},{3,15},{4,0},{5,1},{6,2},{7,3},{8,4},{9,5},{1... | collective-permute-start | bytes 393224 | tf_op jit(solution)/shard_map/ppermute | solution.py:22
  72.0 19.0 %collective-permute-start.10 = (bf16[2,512,384]{2,1,0:T(8,128)(2,1)S(1)}, bf16[2,512,384]{2,1,0:T(8,128)(2,1)S(1)}, u32[]{:S(2)}, u32[]{:S(2)}) collective-permute-start(bf16[2,512,384]{2,1,0:T(8,128)(2,1)S(1)} %add_convert_fusion), channel_id=1, source_target_pairs={{0,128},{1,385},{2,130},{3,387},{4,132},{5,389},{6,134},{7,391},{8... | collective-permute-start | bytes 2359304 | tf_op jit(solution)/shard_map/ppermute | solution.py:22
  78.1 21.2 %collective-permute-start.11 = (bf16[16,2048]{1,0:T(8,128)(2,1)}, bf16[16,2048]{1,0:T(8,128)(2,1)S(1)}, u32[]{:S(2)}, u32[]{:S(2)}) collective-permute-start(bf16[16,2048]{1,0:T(8,128)(2,1)} %fusion.21), channel_id=1, source_target_pairs={{0,2},{1,3},{2,0},{3,1},{4,6},{5,7},{6,4},{7,5},{8,10},{9,11},{10,... | collective-permute-start | bytes 196616 | tf_op jit(solution)/shard_map/ppermute | solution.py:22
  91.0 3.6 %copy-start.3 = (bf16[1,512,384]{2,1,0:T(8,128)(2,1)}, bf16[1,512,384]{2,1,0:T(8,128)(2,1)S(1)}, u32[]{:S(2)}) copy-start(bf16[1,512,384]{2,1,0:T(8,128)(2,1)S(1)} %get-tuple-element.14) | copy-start | bytes 1179652
  91.0 8.3 %copy-start.2 = (bf16[16,2048]{1,0:T(8,128)(2,1)S(1)}, bf16[16,2048]{1,0:T(8,128)(2,1)}, u32[]{:S(2)}) copy-start(bf16[16,2048]{1,0:T(8,128)(2,1)} %param.6) | copy-start | bytes 196612
  91.0 8.3 %copy-start.6 = (bf16[2048]{0:T(1024)(128)(2,1)S(1)}, bf16[2048]{0:T(1024)(128)(2,1)}, u32[]{:S(2)}) copy-start(bf16[2048]{0:T(1024)(128)(2,1)} %param.8) | copy-start | bytes 12292
  91.1 6.9 %copy-start.4 = (bf16[1,512,384]{2,1,0:T(8,128)(2,1)}, bf16[1,512,384]{2,1,0:T(8,128)(2,1)S(1)}, u32[]{:S(2)}) copy-start(bf16[1,512,384]{2,1,0:T(8,128)(2,1)S(1)} %get-tuple-element.16) | copy-start | bytes 1179652
  92.0 10.9 %collective-permute-start.16 = (bf16[2,2,64,384]{3,2,1,0:T(8,128)(2,1)}, bf16[2,2,64,384]{3,2,1,0:T(8,128)(2,1)}, u32[]{:S(2)}, u32[]{:S(2)}) collective-permute-start(bf16[2,2,64,384]{3,2,1,0:T(8,128)(2,1)} %fusion.9), channel_id=1, source_target_pairs={{0,16},{16,0},{32,48},{48,32},{64,80},{80,64},{96,112},{112,96},{1... | collective-permute-start | bytes 589832 | tf_op jit(solution)/shard_map/ppermute | solution.py:22
  94.6 12.4 %collective-permute-start.13 = (bf16[2,2,64,384]{3,2,1,0:T(8,128)(2,1)}, bf16[2,2,64,384]{3,2,1,0:T(8,128)(2,1)}, u32[]{:S(2)}, u32[]{:S(2)}) collective-permute-start(bf16[2,2,64,384]{3,2,1,0:T(8,128)(2,1)} %fusion.8), channel_id=1, source_target_pairs={{0,16},{16,0},{32,48},{48,32},{64,80},{80,64},{96,112},{112,96},{1... | collective-permute-start | bytes 589832 | tf_op jit(solution)/shard_map/ppermute | solution.py:22
  104.1 8.6 %collective-permute-start.17 = (bf16[2,64,384]{2,1,0:T(8,128)(2,1)S(1)}, bf16[2,64,384]{2,1,0:T(8,128)(2,1)S(1)}, u32[]{:S(2)}, u32[]{:S(2)}) collective-permute-start(bf16[2,64,384]{2,1,0:T(8,128)(2,1)S(1)} %fusion.20), channel_id=1, source_target_pairs={{0,32},{16,48},{32,0},{48,16},{64,96},{80,112},{96,64},{112,80},{1... | collective-permute-start | bytes 294920 | tf_op jit(solution)/shard_map/ppermute | solution.py:22
  108.1 9.5 %collective-permute-start.14 = (bf16[2,64,384]{2,1,0:T(8,128)(2,1)S(1)}, bf16[2,64,384]{2,1,0:T(8,128)(2,1)S(1)}, u32[]{:S(2)}, u32[]{:S(2)}) collective-permute-start(bf16[2,64,384]{2,1,0:T(8,128)(2,1)S(1)} %fusion.19), channel_id=1, source_target_pairs={{0,32},{16,48},{32,0},{48,16},{64,96},{80,112},{96,64},{112,80},{1... | collective-permute-start | bytes 294920 | tf_op jit(solution)/shard_map/ppermute | solution.py:22
  112.8 10.7 %collective-permute-start.18 = (bf16[64,384]{1,0:T(8,128)(2,1)S(1)}, bf16[64,384]{1,0:T(8,128)(2,1)S(1)}, u32[]{:S(2)}, u32[]{:S(2)}) collective-permute-start(bf16[64,384]{1,0:T(8,128)(2,1)S(1)} %fusion.23), channel_id=1, source_target_pairs={{0,64},{16,80},{32,96},{48,112},{64,0},{80,16},{96,32},{112,48},{1... | collective-permute-start | bytes 147464 | tf_op jit(solution)/shard_map/ppermute | solution.py:22
  117.7 10.3 %collective-permute-start.15 = (bf16[64,384]{1,0:T(8,128)(2,1)S(1)}, bf16[64,384]{1,0:T(8,128)(2,1)S(1)}, u32[]{:S(2)}, u32[]{:S(2)}) collective-permute-start(bf16[64,384]{1,0:T(8,128)(2,1)S(1)} %fusion.22), channel_id=1, source_target_pairs={{0,64},{16,80},{32,96},{48,112},{64,0},{80,16},{96,32},{112,48},{1... | collective-permute-start | bytes 147464 | tf_op jit(solution)/shard_map/ppermute | solution.py:22
